TPU v7x, 32 devices: a whole 2x2x4 slice. The times are simulated.
32 devices in a mesh: seq: 8 (over z, y), fsdp: 4 (over x, core).
Axes of the slice: x: 2, y: 2, z: 4, core: 2. Of those that a mesh axis runs over, the one named last changes fastest.
Arguments:
- tokens: bfloat16 [4, 2048, 1024], P('fsdp', 'seq'), may hold values from -6 to 6
- cotangent: bfloat16 [4, 2048, 1024], P('fsdp', 'seq'), may hold values from -6 to 6
- lengths: int32 [4, 3], P('fsdp'), may hold values from 300 to 1024, as said below
- block_perm: int32 [4, 16], P('fsdp'), may hold values from 0 to 15, as said below
- attn_gain: bfloat16 [2, 1024], P(None, 'fsdp'), may hold values from 0.5 to 1.5
- qkv_weight: bfloat16 [2, 1024, 3072], P(None, 'fsdp'), may hold values from -0.1875 to 0.1875
- proj_weight: bfloat16 [2, 1024, 1024], P(None, 'fsdp'), may hold values from -1.5 to 1.5
- mlp_gain: bfloat16 [2, 1024], P(None, 'fsdp'), may hold values from 0.5 to 1.5
- wide_weight: bfloat16 [2, 1024, 5248], P(None, 'fsdp'), may hold values from -0.1875 to 0.1875
- narrow_weight: bfloat16 [2, 1024, 2624], P(None, 'fsdp'), may hold values from -0.125 to 0.125
Outputs:
- block_out: bfloat16 [4, 2048, 1024], P('fsdp', 'seq')
- token_grad: bfloat16 [4, 2048, 1024], P('fsdp', 'seq')
- attn_gain_grad: float32 [2, 1024], P(None, ('seq', 'fsdp'))
- qkv_grad: float32 [2, 1024, 3072], P(None, ('seq', 'fsdp'))
- proj_grad: float32 [2, 1024, 1024], P(None, ('seq', 'fsdp'))
- mlp_gain_grad: float32 [2, 1024], P(None, ('seq', 'fsdp'))
- wide_grad: float32 [2, 1024, 5248], P(None, ('seq', 'fsdp'))
- narrow_grad: float32 [2, 1024, 2624], P(None, ('seq', 'fsdp'))
Inputs may be any that keep to these rules, and one draw needn't show every extreme that they name: Sequence s of a batch takes ceil(lengths / 128) blocks, and the blocks of a batch add up to 16; every sequence but the last ends inside the 2 blocks of one index of seq, never at their end. `block_perm`: each row is a permutation. The 2 blocks that one index of seq holds in the given order go together to one index of seq; that map of indices is a composition, for bit = 0, 1, 2 and so on in turn, of swaps of some pairs of indices that differ in that bit only.
All inputs are finite; a program needn't handle non-finite values.
Results may differ from a plain program's by a relative error of at most 0.028.
Values may be sent and summed in bfloat16 or wider, within the bound.
No kernel may reach another device: no remote copies, remote signals or barrier semaphores. Data moves between devices by JAX's collectives and lax.ppermute only.
A program may use at most 448 MiB of HBM per device.

v0:
```python
import math

import jax
import jax.numpy as jnp
from jax import lax
from jax.sharding import PartitionSpec as P

HEADS = 16
HEAD_DIM = 64
FF = 2624
WINDOW = 128
BLOCK = 128
BLK_DEV = 2
LAYERS = 2


NEG = -1e30
EPS = 1e-05
THETA = 10000.0


def padded(shard, sides, width):
    for axis, dim in sides:
        devices, length = (lax.axis_size(axis), shard.shape[dim])
        up = [(i, (i + 1) % devices) for i in range(devices - 1)]
        down = [(j, i) for i, j in up]
        last = lax.slice_in_dim(shard, length - width, length, axis=dim)
        leading = lax.slice_in_dim(shard, 0, width, axis=dim)
        before = lax.ppermute(last, axis, up)
        after = lax.ppermute(leading, axis, down)
        shard = jnp.concatenate([before, shard, after], axis=dim)
    return shard


def partner(block, axis, bit):
    count = lax.axis_size(axis)
    route = []
    for low in range(count):
        high = low | 1 << bit
        if high != low and high < count:
            route += [(low, high), (high, low)]
    return lax.ppermute(block, axis, route)


def normalize(values, gain):
    average = jnp.mean(values, axis=-1, keepdims=True)
    centred = values - average
    spread = jnp.mean(centred * centred, axis=-1, keepdims=True)
    return centred * lax.rsqrt(spread + EPS) * gain


def rope_tables(position):
    inverse = jnp.power(THETA, -jnp.arange(0, HEAD_DIM, 2, dtype=jnp.float32) / HEAD_DIM)
    angles = position[:, None] * inverse[None, :]
    angles = jnp.concatenate([angles, angles], axis=-1)
    return (jnp.cos(angles)[:, None, :], jnp.sin(angles)[:, None, :])


def rotate(values, cosine, sine_tab):
    half = values.shape[-1] // 2
    turned = jnp.concatenate([-values[..., half:], values[..., :half]], axis=-1)
    return values * cosine + turned * sine_tab


def unrotate(grads, cosine, sine_tab):
    half = grads.shape[-1] // 2
    scaled = grads * sine_tab
    return grads * cosine + jnp.concatenate([scaled[..., half:], -scaled[..., :half]], axis=-1)


def layout(positions, lengths, total):
    count = lengths.shape[0]
    blocks = (lengths + BLOCK - 1) // BLOCK
    first = (jnp.cumsum(blocks) - blocks) * BLOCK
    owner = jnp.sum((positions[:, None] >= first[None, :]).astype(jnp.int32), axis=1) - 1
    table = owner[:, None] == jnp.arange(count, dtype=jnp.int32)[None, :]
    start = jnp.sum(jnp.where(table, first[None, :], 0), axis=1)
    span = jnp.sum(jnp.where(table, lengths[None, :], 0), axis=1)
    local = positions - start
    inside = (positions >= 0) & (positions < total)
    valid = inside & (local < span)
    segment = jnp.where(inside, jnp.where(valid, owner, owner + count), -1)
    return (segment, local, valid)


def gelu_pair(hidden):
    return jax.nn.gelu(hidden[:, :FF], approximate=False) * hidden[:, FF:]


def split_keys(extended):
    features = HEADS * HEAD_DIM
    key_rows = extended[:, :features].reshape(-1, HEADS, HEAD_DIM)
    value_rows = extended[:, features:].reshape(-1, HEADS, HEAD_DIM)
    return (key_rows, value_rows)


def attend_forward(queries, extended, allowed):
    scale = 1.0 / math.sqrt(HEAD_DIM)
    key_rows, value_rows = split_keys(extended)
    raw_scores = jnp.einsum("qhd,khd->hqk", queries, key_rows, preferred_element_type=jnp.float32)
    scores = jnp.where(allowed[None], raw_scores * scale, NEG)
    top = jnp.max(scores, axis=-1, keepdims=True)
    expo = jnp.exp(scores - top)
    summed = jnp.sum(expo, axis=-1, keepdims=True)
    probs = (expo / summed).astype(jnp.bfloat16)
    attended = jnp.einsum("hqk,khd->qhd", probs, value_rows, preferred_element_type=jnp.float32)
    return (attended, top + jnp.log(summed))


def attend_backward(queries, extended, log_total, attended_grad, allowed):
    scale = 1.0 / math.sqrt(HEAD_DIM)
    key_rows, value_rows = split_keys(extended)
    raw_scores = jnp.einsum("qhd,khd->hqk", queries, key_rows, preferred_element_type=jnp.float32)
    scores = jnp.where(allowed[None], raw_scores * scale, NEG)
    probs = jnp.exp(scores - log_total)
    probs_b = probs.astype(jnp.bfloat16)
    prob_grad = jnp.einsum(
        "qhd,khd->hqk", attended_grad, value_rows, preferred_element_type=jnp.float32
    )
    row_dot = jnp.sum(prob_grad * probs, axis=-1, keepdims=True)
    score_grad = (probs * (prob_grad - row_dot) * scale).astype(jnp.bfloat16)
    query_grad = jnp.einsum(
        "hqk,khd->qhd", score_grad, key_rows, preferred_element_type=jnp.float32
    )
    key_grad = jnp.einsum("hqk,qhd->khd", score_grad, queries, preferred_element_type=jnp.float32)
    value_grad = jnp.einsum(
        "hqk,qhd->khd", probs_b, attended_grad, preferred_element_type=jnp.float32
    )
    rows = extended.shape[0]
    return (
        query_grad,
        jnp.concatenate([key_grad.reshape(rows, -1), value_grad.reshape(rows, -1)], axis=1),
    )


def forward_layer(residual, weights, allowed, cosine, sine_tab):
    gain_a, w_qkv, w_proj, gain_m, w_wide, w_narrow = weights
    features = residual.shape[1]
    normed = normalize(residual, gain_a.astype(jnp.float32)).astype(jnp.bfloat16)
    projected = jnp.dot(normed, w_qkv, preferred_element_type=jnp.float32)
    queries = rotate(projected[:, :features].reshape(-1, HEADS, HEAD_DIM), cosine, sine_tab).astype(
        jnp.bfloat16
    )
    key_rows = (
        rotate(projected[:, features : 2 * features].reshape(-1, HEADS, HEAD_DIM), cosine, sine_tab)
        .astype(jnp.bfloat16)
        .reshape(-1, features)
    )
    value_rows = projected[:, 2 * features :].astype(jnp.bfloat16)
    extended = padded(jnp.concatenate([key_rows, value_rows], axis=1), (("seq", 0),), WINDOW // 2)
    attended, log_total = attend_forward(queries, extended, allowed)
    mixed_b = attended.reshape(-1, features).astype(jnp.bfloat16)
    middle = residual + jnp.dot(mixed_b, w_proj, preferred_element_type=jnp.float32)
    second = normalize(middle, gain_m.astype(jnp.float32)).astype(jnp.bfloat16)
    hidden = jnp.dot(second, w_wide, preferred_element_type=jnp.float32)
    gated_b = gelu_pair(hidden).astype(jnp.bfloat16)
    result = middle + jnp.einsum("tf,df->td", gated_b, w_narrow, preferred_element_type=jnp.float32)
    return (
        result,
        (residual, normed, queries, extended, log_total, mixed_b, middle, second, hidden, gated_b),
    )


def backward_layer(upstream, weights, kept, allowed, cosine, sine_tab):
    gain_a, w_qkv, w_proj, gain_m, w_wide, w_narrow = weights
    residual, normed, queries, extended, log_total, mixed_b, middle, second, hidden, gated_b = kept
    features = residual.shape[1]
    halo_rows = WINDOW // 2
    upstream_b = upstream.astype(jnp.bfloat16)
    narrow_term = jnp.einsum("td,tf->df", upstream_b, gated_b, preferred_element_type=jnp.float32)
    gated_grad = jnp.einsum("td,df->tf", upstream_b, w_narrow, preferred_element_type=jnp.float32)
    _, pull_gate = jax.vjp(gelu_pair, hidden)
    hidden_grad = pull_gate(gated_grad)[0].astype(jnp.bfloat16)
    wide_term = jnp.einsum("tc,tf->cf", second, hidden_grad, preferred_element_type=jnp.float32)
    second_grad = jnp.einsum("tf,cf->tc", hidden_grad, w_wide, preferred_element_type=jnp.float32)
    _, pull_second = jax.vjp(normalize, middle, gain_m.astype(jnp.float32))
    middle_part, mlp_term = pull_second(second_grad)
    middle_grad = upstream + middle_part
    middle_b = middle_grad.astype(jnp.bfloat16)
    proj_term = jnp.einsum("tc,td->cd", mixed_b, middle_b, preferred_element_type=jnp.float32)
    attended_grad = (
        jnp.einsum("td,cd->tc", middle_b, w_proj, preferred_element_type=jnp.float32)
        .astype(jnp.bfloat16)
        .reshape(-1, HEADS, HEAD_DIM)
    )
    query_grad, extended_grad = attend_backward(
        queries, extended, log_total, attended_grad, allowed
    )
    rim_rows = jnp.concatenate([extended_grad[:halo_rows], extended_grad[-halo_rows:]], axis=0)
    arrived = padded(rim_rows.astype(jnp.bfloat16), (("seq", 0),), halo_rows).astype(rim_rows.dtype)
    own_rows = extended_grad[halo_rows:-halo_rows]
    own_rows = jnp.concatenate(
        [
            own_rows[:halo_rows] + arrived[:halo_rows],
            own_rows[halo_rows:-halo_rows],
            own_rows[-halo_rows:] + arrived[-halo_rows:],
        ],
        axis=0,
    )
    query_back = unrotate(query_grad, cosine, sine_tab).reshape(-1, features)
    key_back = unrotate(
        own_rows[:, :features].reshape(-1, HEADS, HEAD_DIM), cosine, sine_tab
    ).reshape(-1, features)
    joint_grad = jnp.concatenate([query_back, key_back, own_rows[:, features:]], axis=1).astype(
        jnp.bfloat16
    )
    qkv_term = jnp.einsum("tc,tf->cf", normed, joint_grad, preferred_element_type=jnp.float32)
    normed_grad = jnp.einsum("tf,cf->tc", joint_grad, w_qkv, preferred_element_type=jnp.float32)
    _, pull_first = jax.vjp(normalize, residual, gain_a.astype(jnp.float32))
    residual_part, attn_term = pull_first(normed_grad)
    return (
        middle_grad + residual_part,
        (attn_term, qkv_term, proj_term, mlp_term, wide_term, narrow_term),
    )


def body(
    tokens,
    cotangent,
    lengths,
    block_perm,
    attn_gain,
    qkv_weight,
    proj_weight,
    mlp_gain,
    wide_weight,
    narrow_weight,
):
    seq_index = lax.axis_index("seq")
    seq_count = lax.axis_size("seq")
    levels = seq_count.bit_length() - 1
    tok_dev = tokens.shape[1]
    features = tokens.shape[2]
    block_rows = tok_dev // BLK_DEV
    halo_rows = WINDOW // 2
    order_map = block_perm[0]
    target = order_map[0::BLK_DEV] // BLK_DEV
    source = jnp.arange(seq_count, dtype=jnp.int32)

    def holder(bit_level):
        low_mask = (1 << bit_level) - 1
        place = jnp.bitwise_or(
            jnp.bitwise_and(target, low_mask), jnp.bitwise_and(source, ~low_mask)
        )
        return jnp.sum(jnp.where(place == seq_index, source, 0))

    moving = (tokens[0], cotangent[0])
    for bit_level in range(levels):
        payload = holder(bit_level)
        goal_index = jnp.sum(jnp.where(source == payload, target, 0))
        flipped = (
            jnp.bitwise_and(jnp.right_shift(jnp.bitwise_xor(seq_index, goal_index), bit_level), 1)
            == 1
        )
        arrived = partner((moving[0], moving[1]), "seq", bit_level)
        moving = (
            jnp.where(flipped, arrived[0], moving[0]),
            jnp.where(flipped, arrived[1], moving[1]),
        )
    home_index = holder(levels)
    slot_of = lax.dynamic_slice_in_dim(order_map, home_index * BLK_DEV, BLK_DEV) % BLK_DEV
    slot_range = jnp.arange(BLK_DEV, dtype=jnp.int32)
    placing = jnp.sum(
        jnp.where(slot_of[None, :] == slot_range[:, None], slot_range[None, :], 0), axis=1
    )
    packed_tok = jnp.take(
        moving[0].reshape(BLK_DEV, block_rows, features), placing, axis=0
    ).reshape(tok_dev, features)
    packed_cot = jnp.take(
        moving[1].reshape(BLK_DEV, block_rows, features), placing, axis=0
    ).reshape(tok_dev, features)
    total = seq_count * tok_dev
    own_place = seq_index * tok_dev + jnp.arange(tok_dev, dtype=jnp.int32)
    key_place = (
        seq_index * tok_dev - halo_rows + jnp.arange(tok_dev + 2 * halo_rows, dtype=jnp.int32)
    )
    seg_query, local_query, valid_query = layout(own_place, lengths[0], total)
    seg_key, _, _ = layout(key_place, lengths[0], total)
    offset = (
        jnp.arange(tok_dev, dtype=jnp.int32)[:, None]
        + halo_rows
        - jnp.arange(tok_dev + 2 * halo_rows, dtype=jnp.int32)[None, :]
    )
    allowed = (jnp.abs(offset) <= halo_rows) & (seg_query[:, None] == seg_key[None, :])
    cosine, sine_tab = rope_tables(local_query.astype(jnp.float32))
    residual = packed_tok.astype(jnp.float32)
    kept_all = []
    weights_all = []
    for layer_index in range(LAYERS):
        weights = (
            lax.all_gather(attn_gain[layer_index], "fsdp", axis=0, tiled=True),
            lax.all_gather(qkv_weight[layer_index], "fsdp", axis=0, tiled=True),
            lax.all_gather(proj_weight[layer_index], "fsdp", axis=0, tiled=True),
            lax.all_gather(mlp_gain[layer_index], "fsdp", axis=0, tiled=True),
            lax.all_gather(wide_weight[layer_index], "fsdp", axis=0, tiled=True),
            lax.all_gather(narrow_weight[layer_index], "fsdp", axis=0, tiled=True),
        )
        residual, kept = forward_layer(residual, weights, allowed, cosine, sine_tab)
        weights_all.append(weights)
        kept_all.append(kept)
    block_out = residual.astype(jnp.bfloat16)
    upstream = packed_cot.astype(jnp.float32) * valid_query[:, None].astype(jnp.float32)
    layer_terms = [None] * LAYERS
    for layer_index in reversed(range(LAYERS)):
        weights = (
            lax.all_gather(attn_gain[layer_index], "fsdp", axis=0, tiled=True),
            lax.all_gather(qkv_weight[layer_index], "fsdp", axis=0, tiled=True),
            lax.all_gather(proj_weight[layer_index], "fsdp", axis=0, tiled=True),
            lax.all_gather(mlp_gain[layer_index], "fsdp", axis=0, tiled=True),
            lax.all_gather(wide_weight[layer_index], "fsdp", axis=0, tiled=True),
            lax.all_gather(narrow_weight[layer_index], "fsdp", axis=0, tiled=True),
        )
        upstream, grad_terms = backward_layer(
            upstream, weights, kept_all[layer_index], allowed, cosine, sine_tab
        )
        layer_terms[layer_index] = (
            lax.psum_scatter(grad_terms[0], ("seq", "fsdp"), scatter_dimension=0, tiled=True),
            lax.psum_scatter(grad_terms[1], ("seq", "fsdp"), scatter_dimension=0, tiled=True),
            lax.psum_scatter(grad_terms[2], ("seq", "fsdp"), scatter_dimension=0, tiled=True),
            lax.psum_scatter(grad_terms[3], ("seq", "fsdp"), scatter_dimension=0, tiled=True),
            lax.psum_scatter(grad_terms[4], ("seq", "fsdp"), scatter_dimension=0, tiled=True),
            lax.psum_scatter(grad_terms[5], ("seq", "fsdp"), scatter_dimension=0, tiled=True),
        )
    stacked = [
        jnp.stack([layer_terms[layer_index][part_index] for layer_index in range(LAYERS)])
        for part_index in range(6)
    ]
    out_blocks = block_out.reshape(BLK_DEV, block_rows, features)
    grad_blocks = upstream.astype(jnp.bfloat16).reshape(BLK_DEV, block_rows, features)
    returning = (
        jnp.take(out_blocks, slot_of, axis=0).reshape(tok_dev, features),
        jnp.take(grad_blocks, slot_of, axis=0).reshape(tok_dev, features),
    )
    for bit_level in reversed(range(levels)):
        payload = holder(bit_level + 1)
        flipped = (
            jnp.bitwise_and(jnp.right_shift(jnp.bitwise_xor(seq_index, payload), bit_level), 1) == 1
        )
        arrived = partner((returning[0], returning[1]), "seq", bit_level)
        returning = (
            jnp.where(flipped, arrived[0], returning[0]),
            jnp.where(flipped, arrived[1], returning[1]),
        )
    return (
        returning[0][None],
        returning[1][None],
        stacked[0],
        stacked[1],
        stacked[2],
        stacked[3],
        stacked[4],
        stacked[5],
    )


def solution(mesh):
    in_specs = (
        P("fsdp", "seq", None),
        P("fsdp", "seq", None),
        P("fsdp", None),
        P("fsdp", None),
        P(None, "fsdp"),
        P(None, "fsdp", None),
        P(None, "fsdp", None),
        P(None, "fsdp"),
        P(None, "fsdp", None),
        P(None, "fsdp", None),
    )
    out_specs = (
        P("fsdp", "seq", None),
        P("fsdp", "seq", None),
        P(None, ("seq", "fsdp")),
        P(None, ("seq", "fsdp"), None),
        P(None, ("seq", "fsdp"), None),
        P(None, ("seq", "fsdp")),
        P(None, ("seq", "fsdp"), None),
        P(None, ("seq", "fsdp"), None),
    )
    return jax.shard_map(body, mesh=mesh, in_specs=in_specs, out_specs=out_specs, check_vma=False)
```

profile of v0, /device:TPU:0, one launch (start us, length us, event | category | flops | bytes accessed | tf_op | source)
XLA Modules:
  0.0 1843.6 jit_solution(14981748636283044540)
XLA Ops:
  54.7 18.1 collective-permute-done.1
  145.2 13.3 all-gather.25.cloned.1.call-done
  174.1 27.7 %all-gather.27.cloned.1.call-done = bf16[1,1024,2624]{1,2,0:T(8,128)(2,1)} async-done(((bf16[1,256,2624]{1,2,0:T(8,128)(2,1)}), bf16[1,1024,2624]{1,2,0:T(8,128)(2,1)}) %all-gather.27.cloned.1.call-update) | async-done | bytes 5373968 | tf_op jit(solution)/shard_map/all_gather | solution.py:296
  206.7 42.9 %all-gather.29.cloned.1.call-done = bf16[1,1024,3072]{2,1,0:T(8,128)(2,1)} async-done(((bf16[1,256,3072]{2,1,0:T(8,128)(2,1)}), bf16[1,1024,3072]{2,1,0:T(8,128)(2,1)}) %all-gather.29.cloned.1.call-update) | async-done | bytes 6291472 | tf_op jit(solution)/shard_map/all_gather | solution.py:292
  300.6 46.8 %all-gather.33.cloned.1.call-done = bf16[1,1024,5248]{2,1,0:T(8,128)(2,1)} async-done(((bf16[1,256,5248]{2,1,0:T(8,128)(2,1)}), bf16[1,1024,5248]{2,1,0:T(8,128)(2,1)}) %all-gather.33.cloned.1.call-update) | async-done | bytes 10747920 | tf_op jit(solution)/shard_map/all_gather | solution.py:295
  356.5 35.0 %all-gather.35.cloned.1.call-done = bf16[1,1024,2624]{1,2,0:T(8,128)(2,1)} async-done(((bf16[1,256,2624]{1,2,0:T(8,128)(2,1)}), bf16[1,1024,2624]{1,2,0:T(8,128)(2,1)}) %all-gather.35.cloned.1.call-update) | async-done | bytes 5373968 | tf_op jit(solution)/shard_map/all_gather | solution.py:296
  431.7 32.9 %fusion.37 = f32[16,64,384]{2,1,0:T(8,128)} fusion(bf16[256,16,64]{0,2,1:T(8,128)(2,1)S(1)} %copy-done.52, f32[16,256,384]{2,1,0:T(8,128)} %fusion.227, f32[16,256,384]{2,1,0:T(8,128)} %copy-done.1, f32[16,256]{1,0:T(8,128)S(1)} %log_add_fusion.1), kind=kOutput, calls=%fused_computation.66 | convolution fusion | flops 212341120 | bytes 14696448 | tf_op jit(solution)/shard_map/hqk,qhd->khd/dot_general | solution.py:125
  471.6 25.4 %collective-permute-done.13 = bf16[64,2048]{0,1:T(8,128)(2,1)S(1)} collective-permute-done((bf16[64,2048]{0,1:T(8,128)(2,1)S(1)}, bf16[64,2048]{0,1:T(8,128)(2,1)S(1)}, u32[]{:S(2)}, u32[]{:S(2)}) %collective-permute-start.13) | collective-permute-done | bytes 262176 | tf_op jit(solution)/shard_map/ppermute | solution.py:29
  501.1 29.7 %broadcast_multiply_fusion.3 = (f32[256,16,64]{0,2,1:T(8,128)}, f32[256,16,64]{0,2,1:T(8,128)}, f32[256,16,64]{0,2,1:T(8,128)}) fusion(f32[256,64]{0,1:T(8,128)S(1)} %get-tuple-element.99, f32[256,16,64]{0,2,1:T(8,128)} %bitcast.280, bf16[384,16,64]{0,2,1:T(8,128)(2,1)} %bitcast.267, f32[16,256,384]{2,1,0:T(8,128)} %fusion.227, ...), kind=kOutput, calls=%fused_computation.234 | convolution fusion | flops 212865408 | bytes 17645568 | tf_op jit(solution)/shard_map/hqk,khd->qhd/dot_general | solution.py:122
  548.2 12.5 multiply_reduce_fusion.3
  596.2 31.8 %fusion.43 = f32[16,64,384]{2,1,0:T(8,128)S(1)} fusion(bf16[256,16,64]{0,2,1:T(8,128)(2,1)} %fusion.132, f32[16,256,384]{2,1,0:T(8,128)} %fusion.228, f32[16,256,384]{2,1,0:T(8,128)} %copy-done, f32[16,256]{1,0:T(8,128)S(1)} %log_add_fusion), kind=kOutput, calls=%fused_computation.68 | convolution fusion | flops 212341120 | bytes 14696448 | tf_op jit(solution)/shard_map/hqk,qhd->khd/dot_general | solution.py:125
  637.9 24.8 %collective-permute-done.15 = bf16[64,2048]{0,1:T(8,128)(2,1)S(1)} collective-permute-done((bf16[64,2048]{0,1:T(8,128)(2,1)S(1)}, bf16[64,2048]{0,1:T(8,128)(2,1)S(1)}, u32[]{:S(2)}, u32[]{:S(2)}) %collective-permute-start.15) | collective-permute-done | bytes 262176 | tf_op jit(solution)/shard_map/ppermute | solution.py:29
  666.8 29.8 %broadcast_multiply_fusion.1 = (f32[256,16,64]{0,2,1:T(8,128)}, f32[256,16,64]{0,2,1:T(8,128)}, f32[256,16,64]{0,2,1:T(8,128)}) fusion(f32[256,64]{0,1:T(8,128)S(1)} %get-tuple-element.99, f32[256,16,64]{0,2,1:T(8,128)} %bitcast.279, bf16[384,16,64]{0,2,1:T(8,128)(2,1)} %bitcast.263, f32[16,256,384]{2,1,0:T(8,128)} %fusion.228, ...), kind=kOutput, calls=%fused_computation.232 | convolution fusion | flops 212865408 | bytes 17645568 | tf_op jit(solution)/shard_map/hqk,khd->qhd/dot_general | solution.py:122
  708.3 11.9 fusion.147
  720.3 13.1 fusion.148
  759.8 95.4 %all-reduce.8 = (f32[1024]{0:T(1024)S(1)}, f32[1024]{0:T(1024)S(1)}, f32[1024]{0:T(1024)S(1)}, f32[1024]{0:T(1024)S(1)}) all-reduce(f32[1024]{0:T(1024)S(1)} %get-tuple-element.13, f32[1024]{0:T(1024)S(1)} %get-tuple-element.15, f32[1024]{0:T(1024)S(1)} %get-tuple-element.11, ...), channel_id=15, replica_groups=mesh['seq'=8,'fsdp'=4] {'seq','fsdp'}, use_global_device_ids=true, to_apply=%region_40.42.clone | all-reduce | flops 4096 | bytes 32768
  857.7 18.8 %collective-permute-done.8 = bf16[256,1024]{1,0:T(8,128)(2,1)S(1)} collective-permute-done((bf16[256,1024]{1,0:T(8,128)(2,1)S(1)}, bf16[256,1024]{1,0:T(8,128)(2,1)S(1)}, u32[]{:S(2)}, u32[]{:S(2)}) %collective-permute-start.8) | collective-permute-done | bytes 524320 | tf_op jit(solution)/shard_map/ppermute | solution.py:42
  877.8 16.8 collective-permute-done.18
  896.9 11.1 collective-permute-done.19
  910.5 133.0 %reduce-scatter.21.cloned.1.call-done = f32[32,2624]{1,0:T(8,128)} async-done(((f32[1024,2624]{1,0:T(8,128)}), f32[32,2624]{1,0:T(8,128)}) %reduce-scatter.21.cloned.1.call-update) | async-done | bytes 335888 | tf_op jit(solution)/shard_map/reduce_scatter | solution.py:322
  1045.5 158.5 %reduce-scatter.11.cloned.1.call-done = f32[32,3072]{1,0:T(8,128)} async-done(((f32[1024,3072]{1,0:T(8,128)}), f32[32,3072]{1,0:T(8,128)}) %reduce-scatter.11.cloned.1.call-update) | async-done | bytes 393232 | tf_op jit(solution)/shard_map/reduce_scatter | solution.py:318
  1204.0 161.4 %reduce-scatter.9.cloned.1.call-done = f32[32,3072]{1,0:T(8,128)} async-done(((f32[1024,3072]{1,0:T(8,128)}), f32[32,3072]{1,0:T(8,128)}) %reduce-scatter.9.cloned.1.call-update) | async-done | bytes 393232 | tf_op jit(solution)/shard_map/reduce_scatter | solution.py:318
  1367.4 229.7 %reduce-scatter.19.cloned.1.call-done = f32[32,5248]{1,0:T(8,128)} async-done(((f32[1024,5248]{1,0:T(8,128)}), f32[32,5248]{1,0:T(8,128)}) %reduce-scatter.19.cloned.1.call-update) | async-done | bytes 671760 | tf_op jit(solution)/shard_map/reduce_scatter | solution.py:321
  1597.1 237.3 %reduce-scatter.17.cloned.1.call-done = f32[32,5248]{1,0:T(8,128)} async-done(((f32[1024,5248]{1,0:T(8,128)}), f32[32,5248]{1,0:T(8,128)}) %reduce-scatter.17.cloned.1.call-update) | async-done | bytes 671760 | tf_op jit(solution)/shard_map/reduce_scatter | solution.py:321
  (442 shorter events, 365.7 us)
Async XLA Ops:
  7.2 96.7 %all-gather.21.cloned.1.call-start = ((), (), s32[]{:S(2)}) async-start(), calls=%async_computation.16 | async-start | bytes 7864320 | tf_op jit(solution)/shard_map/all_gather | solution.py:292
  11.1 131.1 %all-gather.23.cloned.1.call-start = ((), (), s32[]{:S(2)}) async-start(), calls=%async_computation.17 | async-start | bytes 2621440 | tf_op jit(solution)/shard_map/all_gather | solution.py:293
  12.2 146.2 %all-gather.25.cloned.1.call-start = ((), (), s32[]{:S(2)}) async-start(), calls=%async_computation.18 | async-start | bytes 13434880 | tf_op jit(solution)/shard_map/all_gather | solution.py:295
  17.6 184.2 %all-gather.27.cloned.1.call-start = ((), (), s32[]{:S(2)}) async-start(), calls=%async_computation.19 | async-start | bytes 6717440 | tf_op jit(solution)/shard_map/all_gather | solution.py:296
  21.0 228.6 %all-gather.29.cloned.1.call-start = ((), (), s32[]{:S(2)}) async-start(), calls=%async_computation.20 | async-start | bytes 7864320 | tf_op jit(solution)/shard_map/all_gather | solution.py:292
  21.6 276.1 %all-gather.31.cloned.1.call-start = ((), (), s32[]{:S(2)}) async-start(), calls=%async_computation.21 | async-start | bytes 2621440 | tf_op jit(solution)/shard_map/all_gather | solution.py:293
  22.2 325.3 %all-gather.33.cloned.1.call-start = ((), (), s32[]{:S(2)}) async-start(), calls=%async_computation.22 | async-start | bytes 13434880 | tf_op jit(solution)/shard_map/all_gather | solution.py:295
  22.9 368.6 %all-gather.35.cloned.1.call-start = ((), (), s32[]{:S(2)}) async-start(), calls=%async_computation.23 | async-start | bytes 6717440 | tf_op jit(solution)/shard_map/all_gather | solution.py:296
  26.4 882.4 %reduce-scatter.15.cloned.1.call-start = ((), (), s32[]{:S(2)}) async-start(), calls=%async_computation.11 | async-start | bytes 4325376 | tf_op jit(solution)/shard_map/reduce_scatter | solution.py:319
  52.0 43.1 %collective-permute-start.12 = (bf16[256,1024]{1,0:T(8,128)(2,1)S(1)}, bf16[256,1024]{1,0:T(8,128)(2,1)}, u32[]{:S(2)}, u32[]{:S(2)}) collective-permute-start(bf16[256,1024]{1,0:T(8,128)(2,1)S(1)} %broadcast_select_fusion.6), channel_id=1, source_target_pairs={{0,16},{16,0},{4,20},{20,4},{8,24},{24,8},{12,28},{28,12},{1,17},{... | collective-permute-start | bytes 1572872 | tf_op jit(solution)/shard_map/ppermute | solution.py:42
  72.8 26.5 %collective-permute-start.2 = (bf16[256,1024]{1,0:T(8,128)(2,1)S(1)}, bf16[256,1024]{1,0:T(8,128)(2,1)}, u32[]{:S(2)}, u32[]{:S(2)}) collective-permute-start(bf16[256,1024]{1,0:T(8,128)(2,1)S(1)} %broadcast_select_fusion.7), channel_id=1, source_target_pairs={{0,16},{16,0},{4,20},{20,4},{8,24},{24,8},{12,28},{28,12},{1,17},{... | collective-permute-start | bytes 1572872 | tf_op jit(solution)/shard_map/ppermute | solution.py:42
  430.7 478.1 %reduce-scatter.13.cloned.1.call-start = ((), (), s32[]{:S(2)}) async-start(), calls=%async_computation.10 | async-start | bytes 4325376 | tf_op jit(solution)/shard_map/reduce_scatter | solution.py:319
  466.6 30.4 %collective-permute-start.13 = (bf16[64,2048]{0,1:T(8,128)(2,1)S(1)}, bf16[64,2048]{0,1:T(8,128)(2,1)S(1)}, u32[]{:S(2)}, u32[]{:S(2)}) collective-permute-start(bf16[64,2048]{0,1:T(8,128)(2,1)S(1)} %get-tuple-element.66), channel_id=1, source_target_pairs={{0,4},{4,8},{8,12},{12,16},{16,20},{20,24},{24,28},{1,5},{5,9},{9,... | collective-permute-start | bytes 786440 | tf_op jit(solution)/shard_map/ppermute | solution.py:29
  470.0 27.0 %collective-permute-start.14 = (bf16[64,2048]{0,1:T(8,128)(2,1)S(1)}, bf16[64,2048]{0,1:T(8,128)(2,1)S(1)}, u32[]{:S(2)}, u32[]{:S(2)}) collective-permute-start(bf16[64,2048]{0,1:T(8,128)(2,1)S(1)} %get-tuple-element.67), channel_id=1, source_target_pairs={{4,0},{8,4},{12,8},{16,12},{20,16},{24,20},{28,24},{5,1},{9,5},{13... | collective-permute-start | bytes 786440 | tf_op jit(solution)/shard_map/ppermute | solution.py:30
  564.6 345.9 %reduce-scatter.23.cloned.1.call-start = ((), (), s32[]{:S(2)}) async-start(), calls=%async_computation.15 | async-start | bytes 11354112 | tf_op jit(solution)/shard_map/reduce_scatter | solution.py:322
  571.9 471.6 %reduce-scatter.21.cloned.1.call-start = ((), (), s32[]{:S(2)}) async-start(), calls=%async_computation.14 | async-start | bytes 11354112 | tf_op jit(solution)/shard_map/reduce_scatter | solution.py:322
  579.5 624.5 %reduce-scatter.11.cloned.1.call-start = ((), (), s32[]{:S(2)}) async-start(), calls=%async_computation.9 | async-start | bytes 12976128 | tf_op jit(solution)/shard_map/reduce_scatter | solution.py:318
  587.4 778.0 %reduce-scatter.9.cloned.1.call-start = ((), (), s32[]{:S(2)}) async-start(), calls=%async_computation.8 | async-start | bytes 12976128 | tf_op jit(solution)/shard_map/reduce_scatter | solution.py:318
  632.1 30.6 %collective-permute-start.15 = (bf16[64,2048]{0,1:T(8,128)(2,1)S(1)}, bf16[64,2048]{0,1:T(8,128)(2,1)S(1)}, u32[]{:S(2)}, u32[]{:S(2)}) collective-permute-start(bf16[64,2048]{0,1:T(8,128)(2,1)S(1)} %get-tuple-element.64), channel_id=1, source_target_pairs={{0,4},{4,8},{8,12},{12,16},{16,20},{20,24},{24,28},{1,5},{5,9},{9,... | collective-permute-start | bytes 786440 | tf_op jit(solution)/shard_map/ppermute | solution.py:29
  707.1 890.1 %reduce-scatter.19.cloned.1.call-start = ((), (), s32[]{:S(2)}) async-start(), calls=%async_computation.13 | async-start | bytes 22167552 | tf_op jit(solution)/shard_map/reduce_scatter | solution.py:321
  720.2 1114.2 %reduce-scatter.17.cloned.1.call-start = ((), (), s32[]{:S(2)}) async-start(), calls=%async_computation.12 | async-start | bytes 22167552 | tf_op jit(solution)/shard_map/reduce_scatter | solution.py:321
  749.3 105.8 %collective-permute-start.7 = (bf16[256,1024]{1,0:T(8,128)(2,1)S(1)}, bf16[256,1024]{1,0:T(8,128)(2,1)S(1)}, u32[]{:S(2)}, u32[]{:S(2)}) collective-permute-start(bf16[256,1024]{1,0:T(8,128)(2,1)S(1)} %bitcast.271), channel_id=1, source_target_pairs={{0,16},{16,0},{4,20},{20,4},{8,24},{24,8},{12,28},{28,12},{1,17},{... | collective-permute-start | bytes 1572872 | tf_op jit(solution)/shard_map/ppermute | solution.py:42
  757.9 97.4 %collective-permute-start.17 = (bf16[256,1024]{1,0:T(8,128)(2,1)S(1)}, bf16[256,1024]{1,0:T(8,128)(2,1)S(1)}, u32[]{:S(2)}, u32[]{:S(2)}) collective-permute-start(bf16[256,1024]{1,0:T(8,128)(2,1)S(1)} %bitcast.270), channel_id=1, source_target_pairs={{0,16},{16,0},{4,20},{20,4},{8,24},{24,8},{12,28},{28,12},{1,17},{... | collective-permute-start | bytes 1572872 | tf_op jit(solution)/shard_map/ppermute | solution.py:42
  855.4 39.2 %collective-permute-start.18 = (bf16[256,1024]{1,0:T(8,128)(2,1)S(1)}, bf16[256,1024]{1,0:T(8,128)(2,1)S(1)}, u32[]{:S(2)}, u32[]{:S(2)}) collective-permute-start(bf16[256,1024]{1,0:T(8,128)(2,1)S(1)} %broadcast_select_fusion.10), channel_id=1, source_target_pairs={{0,8},{8,0},{4,12},{12,4},{16,24},{24,16},{20,28},{28,20},{1,9},{9... | collective-permute-start | bytes 1572872 | tf_op jit(solution)/shard_map/ppermute | solution.py:42
  (97 other events, 969.0 us)
Sparse Core Ops, SparseCore 0:
  11.2 49.0 all-gather.20
  62.5 22.6 all-gather.22
  86.7 71.6 all-gather.24
  159.8 41.8 all-gather.26
  203.2 46.3 all-gather.28
  251.6 22.5 all-gather.30
  275.8 71.6 all-gather.32
  349.6 41.8 all-gather.34
  430.8 141.5 reduce-scatter.14
  574.6 137.5 reduce-scatter.12
  718.1 177.3 reduce-scatter.22
  901.4 142.1 reduce-scatter.20
  1049.6 154.3 reduce-scatter.10
  1210.9 154.4 reduce-scatter.8
  1367.5 229.5 reduce-scatter.18
  1599.4 234.9 reduce-scatter.16
where the time goes:
time: 1850 us; the launch traced here: 1840 us
  waiting for transfers between devices  1240 us (67%)
  matrix products  302 us (16%)
  blocking collectives  116 us (6%)
  local copies, waits for them, and re-layouts  64.4 us (3%)
  other arithmetic  59.1 us (3%)
  starting transfers between devices  44.1 us (2%)
  between operations  20.1 us (1%)
    reduce_scatter x2, waiting for transfers between devices, body(): lax.psum_scatter(grad_terms[4], ('seq', 'fsdp'), scatter_dimension=0, til...  467 us
    reduce_scatter x2, waiting for transfers between devices, body(): lax.psum_scatter(grad_terms[1], ('seq', 'fsdp'), scatter_dimension=0, til...  320 us
    reduce_scatter x2, waiting for transfers between devices, body(): lax.psum_scatter(grad_terms[5], ('seq', 'fsdp'), scatter_dimension=0, til...  133 us
    unnamed x1, blocking collectives  95.4 us
    ppermute x12, waiting for transfers between devices, partner(): return lax.ppermute(block, axis, route)  83.3 us
    ppermute x4, waiting for transfers between devices, padded(): before = lax.ppermute(last, axis, up)  67.2 us
    dot_general x2, matrix products, attend_backward(): jnp.einsum('hqk,qhd->khd', score_grad, queries, preferred_element_type=jn...  64.8 us
    all_gather x2, waiting for transfers between devices, body(): lax.all_gather(narrow_weight[layer_index], 'fsdp', axis=0, tiled=True)  62.7 us
  transfers between devices with their start and end apart: 36, of which 21 were waited for; matrix products, arithmetic and copies ran while one was open for 20% of the time, Pallas kernels for 0%

commit v1 on v0

--- a/solution.py
+++ b/solution.py
@@ -40,6 +40,96 @@
         if high != low and high < count:
             route += [(low, high), (high, low)]
     return lax.ppermute(block, axis, route)
+
+
+AXES = ("seq", "fsdp")
+
+
+def swap(value, bit):
+    count = lax.axis_size("seq") * lax.axis_size("fsdp")
+    return lax.ppermute(value, AXES, [(i, i ^ (1 << bit)) for i in range(count)])
+
+
+def flat_index():
+    return lax.axis_index("seq") * lax.axis_size("fsdp") + lax.axis_index("fsdp")
+
+
+def gather_weight(shard):
+    rows, cols = shard.shape
+    half = rows // 2
+    quarter = lax.axis_index("fsdp")
+    side = lax.axis_index("seq") % 2
+    sent = lax.dynamic_slice_in_dim(shard, side * half, half, 0)
+    own_core = swap(shard, 0)
+    far_x = swap(sent, 1)
+    far_y = swap(far_x, 2)
+    far_x_core = swap(far_x, 0)
+    far_y_core = swap(far_y, 0)
+    whole = jnp.zeros((4 * rows, cols), shard.dtype)
+    whole = lax.dynamic_update_slice(whole, shard, (quarter * rows, 0))
+    whole = lax.dynamic_update_slice(whole, own_core, ((quarter ^ 1) * rows, 0))
+    whole = lax.dynamic_update_slice(whole, far_x, ((quarter ^ 2) * rows + side * half, 0))
+    whole = lax.dynamic_update_slice(whole, far_y, ((quarter ^ 2) * rows + (1 - side) * half, 0))
+    whole = lax.dynamic_update_slice(whole, far_x_core, ((quarter ^ 3) * rows + side * half, 0))
+    whole = lax.dynamic_update_slice(
+        whole, far_y_core, ((quarter ^ 3) * rows + (1 - side) * half, 0)
+    )
+    return whole
+
+
+def stage_bits(first_x):
+    levels = lax.axis_size("seq").bit_length() - 1
+    rest = [2 + level for level in range(1, levels)]
+    return ([1, 2] if first_x else [2, 1]) + rest
+
+
+def row_order(features, bits):
+    order = [0] + bits
+    per_device = features >> len(order)
+    rows = jnp.arange(features, dtype=jnp.int32)
+    place = rows // per_device
+    owner = flat_index()
+    for step, bit in enumerate(order):
+        taken = (place >> (len(order) - 1 - step)) & 1
+        owner = owner ^ (taken << bit)
+    return owner * per_device + rows % per_device
+
+
+def row_picker(features, bits):
+    order = row_order(features, bits)
+    grid = jnp.arange(features, dtype=jnp.int32)
+    return (grid[:, None] == order[None, :]).astype(jnp.bfloat16)
+
+
+def outer(left, right):
+    return jnp.einsum("tc,tf->cf", left, right, preferred_element_type=jnp.float32)
+
+
+def scatter_outer(left, right, picker, bits):
+    features = left.shape[1]
+    picked = jnp.dot(left, picker, preferred_element_type=jnp.float32).astype(jnp.bfloat16)
+    half = features // 2
+    left = jnp.concatenate([picked[:, :half], swap(picked[:, half:], 0)], axis=0)
+    right = jnp.concatenate([right, swap(right, 0)], axis=0)
+    part = half // 2
+    arrived = swap(outer(left[:, part:], right).astype(jnp.bfloat16), bits[0])
+    total = outer(left[:, :part], right) + arrived.astype(jnp.float32)
+    for bit in bits[1:]:
+        part = part // 2
+        rounded = total.astype(jnp.bfloat16)
+        arrived = swap(rounded[part:], bit)
+        total = total[:part] + arrived.astype(jnp.float32)
+    return total
+
+
+def scatter_vectors(vectors, bits):
+    features = vectors.shape[1]
+    part = features
+    total = jnp.take(vectors, row_order(features, bits), axis=1)
+    for bit in [0] + bits:
+        part = part // 2
+        total = total[:, :part] + swap(total[:, part:], bit)
+    return total
 
 
 def normalize(values, gain):
@@ -161,23 +251,30 @@
     )
 
 
-def backward_layer(upstream, weights, kept, allowed, cosine, sine_tab):
+def backward_layer(upstream, weights, kept, allowed, cosine, sine_tab, paths):
     gain_a, w_qkv, w_proj, gain_m, w_wide, w_narrow = weights
     residual, normed, queries, extended, log_total, mixed_b, middle, second, hidden, gated_b = kept
     features = residual.shape[1]
     halo_rows = WINDOW // 2
     upstream_b = upstream.astype(jnp.bfloat16)
-    narrow_term = jnp.einsum("td,tf->df", upstream_b, gated_b, preferred_element_type=jnp.float32)
+    path_x, path_y = paths
+    narrow_term = scatter_outer(upstream_b, gated_b, *path_x)
     gated_grad = jnp.einsum("td,df->tf", upstream_b, w_narrow, preferred_element_type=jnp.float32)
     _, pull_gate = jax.vjp(gelu_pair, hidden)
     hidden_grad = pull_gate(gated_grad)[0].astype(jnp.bfloat16)
-    wide_term = jnp.einsum("tc,tf->cf", second, hidden_grad, preferred_element_type=jnp.float32)
+    wide_term = jnp.concatenate(
+        [
+            scatter_outer(second, hidden_grad[:, :FF], *path_y),
+            scatter_outer(second, hidden_grad[:, FF:], *path_x),
+        ],
+        axis=1,
+    )
     second_grad = jnp.einsum("tf,cf->tc", hidden_grad, w_wide, preferred_element_type=jnp.float32)
     _, pull_second = jax.vjp(normalize, middle, gain_m.astype(jnp.float32))
     middle_part, mlp_term = pull_second(second_grad)
     middle_grad = upstream + middle_part
     middle_b = middle_grad.astype(jnp.bfloat16)
-    proj_term = jnp.einsum("tc,td->cd", mixed_b, middle_b, preferred_element_type=jnp.float32)
+    proj_term = scatter_outer(mixed_b, middle_b, *path_x)
     attended_grad = (
         jnp.einsum("td,cd->tc", middle_b, w_proj, preferred_element_type=jnp.float32)
         .astype(jnp.bfloat16)
@@ -204,7 +301,14 @@
     joint_grad = jnp.concatenate([query_back, key_back, own_rows[:, features:]], axis=1).astype(
         jnp.bfloat16
     )
-    qkv_term = jnp.einsum("tc,tf->cf", normed, joint_grad, preferred_element_type=jnp.float32)
+    split = 3 * features // 2
+    qkv_term = jnp.concatenate(
+        [
+            scatter_outer(normed, joint_grad[:, :split], *path_y),
+            scatter_outer(normed, joint_grad[:, split:], *path_x),
+        ],
+        axis=1,
+    )
     normed_grad = jnp.einsum("tf,cf->tc", joint_grad, w_qkv, preferred_element_type=jnp.float32)
     _, pull_first = jax.vjp(normalize, residual, gain_a.astype(jnp.float32))
     residual_part, attn_term = pull_first(normed_grad)
@@ -284,16 +388,22 @@
     allowed = (jnp.abs(offset) <= halo_rows) & (seg_query[:, None] == seg_key[None, :])
     cosine, sine_tab = rope_tables(local_query.astype(jnp.float32))
     residual = packed_tok.astype(jnp.float32)
+    gains = jnp.concatenate([attn_gain, mlp_gain], axis=0)
+    gains = lax.all_gather(gains, "fsdp", axis=1, tiled=True)
+    gains_a, gains_m = gains[:LAYERS], gains[LAYERS:]
+    paths = tuple(
+        (row_picker(features, stage_bits(first_x)), stage_bits(first_x)) for first_x in (True, False)
+    )
     kept_all = []
     weights_all = []
     for layer_index in range(LAYERS):
         weights = (
-            lax.all_gather(attn_gain[layer_index], "fsdp", axis=0, tiled=True),
-            lax.all_gather(qkv_weight[layer_index], "fsdp", axis=0, tiled=True),
-            lax.all_gather(proj_weight[layer_index], "fsdp", axis=0, tiled=True),
-            lax.all_gather(mlp_gain[layer_index], "fsdp", axis=0, tiled=True),
-            lax.all_gather(wide_weight[layer_index], "fsdp", axis=0, tiled=True),
-            lax.all_gather(narrow_weight[layer_index], "fsdp", axis=0, tiled=True),
+            gains_a[layer_index],
+            gather_weight(qkv_weight[layer_index]),
+            gather_weight(proj_weight[layer_index]),
+            gains_m[layer_index],
+            gather_weight(wide_weight[layer_index]),
+            gather_weight(narrow_weight[layer_index]),
         )
         residual, kept = forward_layer(residual, weights, allowed, cosine, sine_tab)
         weights_all.append(weights)
@@ -302,27 +412,25 @@
     upstream = packed_cot.astype(jnp.float32) * valid_query[:, None].astype(jnp.float32)
     layer_terms = [None] * LAYERS
     for layer_index in reversed(range(LAYERS)):
-        weights = (
-            lax.all_gather(attn_gain[layer_index], "fsdp", axis=0, tiled=True),
-            lax.all_gather(qkv_weight[layer_index], "fsdp", axis=0, tiled=True),
-            lax.all_gather(proj_weight[layer_index], "fsdp", axis=0, tiled=True),
-            lax.all_gather(mlp_gain[layer_index], "fsdp", axis=0, tiled=True),
-            lax.all_gather(wide_weight[layer_index], "fsdp", axis=0, tiled=True),
-            lax.all_gather(narrow_weight[layer_index], "fsdp", axis=0, tiled=True),
-        )
         upstream, grad_terms = backward_layer(
-            upstream, weights, kept_all[layer_index], allowed, cosine, sine_tab
-        )
-        layer_terms[layer_index] = (
-            lax.psum_scatter(grad_terms[0], ("seq", "fsdp"), scatter_dimension=0, tiled=True),
-            lax.psum_scatter(grad_terms[1], ("seq", "fsdp"), scatter_dimension=0, tiled=True),
-            lax.psum_scatter(grad_terms[2], ("seq", "fsdp"), scatter_dimension=0, tiled=True),
-            lax.psum_scatter(grad_terms[3], ("seq", "fsdp"), scatter_dimension=0, tiled=True),
-            lax.psum_scatter(grad_terms[4], ("seq", "fsdp"), scatter_dimension=0, tiled=True),
-            lax.psum_scatter(grad_terms[5], ("seq", "fsdp"), scatter_dimension=0, tiled=True),
-        )
+            upstream,
+            weights_all[layer_index],
+            kept_all[layer_index],
+            allowed,
+            cosine,
+            sine_tab,
+            paths,
+        )
+        layer_terms[layer_index] = grad_terms
+    vectors = jnp.stack(
+        [layer_terms[layer_index][0] for layer_index in range(LAYERS)]
+        + [layer_terms[layer_index][3] for layer_index in range(LAYERS)]
+    )
+    gain_sums = scatter_vectors(vectors, stage_bits(True))
     stacked = [
         jnp.stack([layer_terms[layer_index][part_index] for layer_index in range(LAYERS)])
+        if part_index not in (0, 3)
+        else gain_sums[(0 if part_index == 0 else LAYERS) :][:LAYERS]
         for part_index in range(6)
     ]
     out_blocks = block_out.reshape(BLK_DEV, block_rows, features)

time: 1850 us -> 1230 us (0.66)
  waiting for transfers between devices: 1240 us -> 406 us
  local copies, waits for them, and re-layouts: 64.4 us -> 265 us
  blocking collectives: 116 us -> 5.2 us
  starting transfers between devices: 44.1 us -> 127 us
  other arithmetic: 59.1 us -> 108 us
    reduce_scatter x8 -> x0, waiting for transfers between devices: 920 us -> none  [the longest x2 467 us: body(): lax.psum_scatter(grad_terms[4], ('seq', 'fsdp'), scatter_dimension=0, til...]
    ppermute x0 -> x117, waiting for transfers between devices: none -> 258 us  [swap(): return lax.ppermute(value, AXES, [(i, i ^ 1 << bit) for i in range(count)])]
    all_gather x8 -> x0, waiting for transfers between devices: 166 us -> none  [the longest x2 62.7 us: body(): lax.all_gather(narrow_weight[layer_index], 'fsdp', axis=0, tiled=True)]
    unnamed x1 -> x0, blocking collectives: 95.4 us -> none
    ppermute x0 -> x117, starting transfers between devices: none -> 86.2 us  [swap(): return lax.ppermute(value, AXES, [(i, i ^ 1 << bit) for i in range(count)])]
    dynamic_update_slice x0 -> x45, local copies, waits for them, and re-layouts: none -> 57.9 us  [the longest x8 15.1 us: gather_weight(): whole = lax.dynamic_update_slice(whole, own_core, ((quarter ^ 1) * rows, 0))]
    slice x2 -> x68, local copies, waits for them, and re-layouts: 0.01 us -> 49.3 us  [the longest x44 23.7 us: scatter_outer(): arrived = swap(rounded[part:], bit)]
    ppermute x4, waiting for transfers between devices: 67.2 us -> 21.5 us  [padded(): before = lax.ppermute(last, axis, up)]
  transfers between devices with their start and end apart: 36 -> 137, of which waited for: 21 -> 44; matrix products, arithmetic and copies ran while one was open for 20% -> 52% of each run, Pallas kernels for 0% -> 0%
where the time goes in v1:
time: 1230 us; the launch traced here: 1220 us
  waiting for transfers between devices  406 us (33%)
  matrix products  297 us (24%)
  local copies, waits for them, and re-layouts  265 us (22%)
  starting transfers between devices  127 us (10%)
  other arithmetic  108 us (9%)
    ppermute x117, waiting for transfers between devices, swap(): return lax.ppermute(value, AXES, [(i, i ^ 1 << bit) for i in range(count)])  258 us
    ppermute x12, waiting for transfers between devices, partner(): return lax.ppermute(block, axis, route)  126 us
    ppermute x117, starting transfers between devices, swap(): return lax.ppermute(value, AXES, [(i, i ^ 1 << bit) for i in range(count)])  86.2 us
    dot_general x24, matrix products, outer(): jnp.einsum('tc,tf->cf', left, right, preferred_element_type=jnp.float32)  65.7 us
    dot_general x2, matrix products, attend_backward(): jnp.einsum('hqk,qhd->khd', score_grad, queries, preferred_element_type=jn...  64.1 us
    dot_general x2, matrix products, attend_backward(): jnp.einsum('hqk,khd->qhd', score_grad, key_rows, preferred_element_type=j...  59.4 us
    unnamed x488, local copies, waits for them, and re-layouts  37.8 us
    ppermute x18, local copies, waits for them, and re-layouts, swap(): return lax.ppermute(value, AXES, [(i, i ^ 1 << bit) for i in range(count)])  34.9 us
  transfers between devices with their start and end apart: 137, of which 44 were waited for; matrix products, arithmetic and copies ran while one was open for 52% of the time, Pallas kernels for 0%

profile of v1, /device:TPU:0, one launch (start us, length us, event | category | flops | bytes accessed | tf_op | source)
XLA Modules:
  0.0 1218.1 jit_solution(7805954583342105073)
XLA Ops:
  86.3 9.5 collective-permute-done.12
  115.9 9.1 collective-permute-done.51
  128.0 12.1 collective-permute-done.43
  145.0 25.6 %collective-permute-done.21 = bf16[128,2624]{0,1:T(8,128)(2,1)S(1)} collective-permute-done((bf16[128,2624]{0,1:T(8,128)(2,1)S(1)}, bf16[128,2624]{0,1:T(8,128)(2,1)S(1)}, u32[]{:S(2)}, u32[]{:S(2)}) %collective-permute-start.21) | collective-permute-done | bytes 671776 | tf_op jit(solution)/shard_map/ppermute | solution.py:50
  174.9 14.2 %collective-permute-done.22 = bf16[128,2624]{0,1:T(8,128)(2,1)S(1)} collective-permute-done((bf16[128,2624]{0,1:T(8,128)(2,1)S(1)}, bf16[128,2624]{0,1:T(8,128)(2,1)S(1)}, u32[]{:S(2)}, u32[]{:S(2)}) %collective-permute-start.22) | collective-permute-done | bytes 671776 | tf_op jit(solution)/shard_map/ppermute | solution.py:50
  194.9 20.0 %collective-permute-done.2 = bf16[256,1024]{1,0:T(8,128)(2,1)S(1)} collective-permute-done((bf16[256,1024]{1,0:T(8,128)(2,1)S(1)}, bf16[256,1024]{1,0:T(8,128)(2,1)S(1)}, u32[]{:S(2)}, u32[]{:S(2)}) %collective-permute-start.2) | collective-permute-done | bytes 524320 | tf_op jit(solution)/shard_map/ppermute | solution.py:42
  216.5 24.1 %collective-permute-done.52 = bf16[256,1024]{1,0:T(8,128)(2,1)} collective-permute-done((bf16[256,1024]{1,0:T(8,128)(2,1)S(1)}, bf16[256,1024]{1,0:T(8,128)(2,1)}, u32[]{:S(2)}, u32[]{:S(2)}) %collective-permute-start.52) | collective-permute-done | bytes 524320 | tf_op jit(solution)/shard_map/ppermute | solution.py:42
  289.2 8.5 collective-permute-done.16
  297.7 28.4 %collective-permute-done.38 = bf16[128,5248]{1,0:T(8,128)(2,1)} collective-permute-done((bf16[128,5248]{1,0:T(8,128)(2,1)}, bf16[128,5248]{1,0:T(8,128)(2,1)}, u32[]{:S(2)}, u32[]{:S(2)}) %collective-permute-start.38) | collective-permute-done | bytes 1343520 | tf_op jit(solution)/shard_map/ppermute | solution.py:50
  360.3 26.0 %collective-permute-done.39 = bf16[128,5248]{1,0:T(8,128)(2,1)} collective-permute-done((bf16[128,5248]{1,0:T(8,128)(2,1)}, bf16[128,5248]{1,0:T(8,128)(2,1)}, u32[]{:S(2)}, u32[]{:S(2)}) %collective-permute-start.39) | collective-permute-done | bytes 1343520 | tf_op jit(solution)/shard_map/ppermute | solution.py:50
  505.9 32.4 %fusion.25 = f32[16,64,384]{2,1,0:T(8,128)} fusion(bf16[256,16,64]{0,2,1:T(8,128)(2,1)} %fusion.132, f32[16,256,384]{2,1,0:T(8,128)} %fusion.330, f32[16,256,384]{2,1,0:T(8,128)} %copy-done.1, f32[16,256]{1,0:T(8,128)S(1)} %log_add_fusion.1), kind=kOutput, calls=%fused_computation.69 | convolution fusion | flops 212341120 | bytes 14696448 | tf_op jit(solution)/shard_map/hqk,qhd->khd/dot_general | solution.py:215
  574.1 29.9 %broadcast_multiply_fusion.3 = (f32[256,16,64]{0,2,1:T(8,128)}, f32[256,16,64]{0,2,1:T(8,128)}, f32[256,16,64]{0,2,1:T(8,128)}) fusion(f32[256,64]{0,1:T(8,128)S(1)} %get-tuple-element.183, f32[256,16,64]{0,2,1:T(8,128)} %bitcast.295, bf16[384,16,64]{0,2,1:T(8,128)(2,1)} %bitcast.284, f32[16,256,384]{2,1,0:T(8,128)} %fusion.330, ...), kind=kOutput, calls=%fused_computation.364 | convolution fusion | flops 212865408 | bytes 17645568 | tf_op jit(solution)/shard_map/hqk,khd->qhd/dot_general | solution.py:212
  615.6 7.5 fusion.140
  645.5 31.7 %fusion.31 = f32[16,64,384]{2,1,0:T(8,128)S(1)} fusion(bf16[256,16,64]{0,2,1:T(8,128)(2,1)} %fusion.130, f32[16,256,384]{2,1,0:T(8,128)} %fusion.331, f32[16,256,384]{2,1,0:T(8,128)} %copy-done, f32[16,256]{1,0:T(8,128)S(1)} %copy-done.157), kind=kOutput, calls=%fused_computation.71 | convolution fusion | flops 212341120 | bytes 14696448 | tf_op jit(solution)/shard_map/hqk,qhd->khd/dot_general | solution.py:215
  687.8 19.1 %collective-permute-done.55 = bf16[64,2048]{0,1:T(8,128)(2,1)S(1)} collective-permute-done((bf16[64,2048]{0,1:T(8,128)(2,1)S(1)}, bf16[64,2048]{0,1:T(8,128)(2,1)S(1)}, u32[]{:S(2)}, u32[]{:S(2)}) %collective-permute-start.55) | collective-permute-done | bytes 262176 | tf_op jit(solution)/shard_map/ppermute | solution.py:29
  710.3 29.5 %broadcast_multiply_fusion.1 = (f32[256,16,64]{0,2,1:T(8,128)}, f32[256,16,64]{0,2,1:T(8,128)}, f32[256,16,64]{0,2,1:T(8,128)}) fusion(f32[256,64]{0,1:T(8,128)S(1)} %copy-done.86, f32[256,16,64]{0,2,1:T(8,128)} %bitcast.294, bf16[384,16,64]{0,2,1:T(8,128)(2,1)} %bitcast.280, f32[16,256,384]{2,1,0:T(8,128)} %fusion.331, f32[16,256,384]{2,1,0:T(8,128)} %copy-done, ...), kind=kOutput, calls=%fused_computation.362 | convolution fusion | flops 212865408 | bytes 17645568 | tf_op jit(solution)/shard_map/hqk,khd->qhd/dot_general | solution.py:212
  805.8 22.8 %collective-permute-done.57 = bf16[256,1024]{1,0:T(8,128)(2,1)S(1)} collective-permute-done((bf16[256,1024]{1,0:T(8,128)(2,1)S(1)}, bf16[256,1024]{1,0:T(8,128)(2,1)S(1)}, u32[]{:S(2)}, u32[]{:S(2)}) %collective-permute-start.57) | collective-permute-done | bytes 524320 | tf_op jit(solution)/shard_map/ppermute | solution.py:42
  829.1 9.9 collective-permute-done.47
  896.7 8.5 collective-permute-done.48
  935.4 18.6 %collective-permute-done.59 = bf16[256,1024]{1,0:T(8,128)(2,1)S(1)} collective-permute-done((bf16[256,1024]{1,0:T(8,128)(2,1)S(1)}, bf16[256,1024]{1,0:T(8,128)(2,1)S(1)}, u32[]{:S(2)}, u32[]{:S(2)}) %collective-permute-start.59) | collective-permute-done | bytes 524320 | tf_op jit(solution)/shard_map/ppermute | solution.py:42
  975.6 34.9 %collective-permute-done.80 = bf16[128,1536]{1,0:T(8,128)(2,1)S(1)} collective-permute-done((bf16[128,1536]{1,0:T(8,128)(2,1)S(1)}, bf16[128,1536]{1,0:T(8,128)(2,1)S(1)}, u32[]{:S(2)}, u32[]{:S(2)}) %collective-permute-start.80) | collective-permute-done | bytes 393248 | tf_op jit(solution)/shard_map/ppermute | solution.py:50
  1031.6 13.0 %collective-permute-done.68 = bf16[128,1536]{1,0:T(8,128)(2,1)S(1)} collective-permute-done((bf16[128,1536]{1,0:T(8,128)(2,1)S(1)}, bf16[128,1536]{1,0:T(8,128)(2,1)S(1)}, u32[]{:S(2)}, u32[]{:S(2)}) %collective-permute-start.68) | collective-permute-done | bytes 393248 | tf_op jit(solution)/shard_map/ppermute | solution.py:50
  1045.1 11.2 collective-permute-done.74
  1186.6 9.6 collective-permute-done.118
  (1179 shorter events, 752.7 us)
Async XLA Ops:
  0.7 81.0 %collective-permute-start = (bf16[256,1024]{1,0:T(8,128)(2,1)}, bf16[256,1024]{1,0:T(8,128)(2,1)}, u32[]{:S(2)}, u32[]{:S(2)}) collective-permute-start(bf16[256,1024]{1,0:T(8,128)(2,1)} %bitcast.300), channel_id=1, source_target_pairs={{0,4},{4,0},{8,12},{12,8},{16,20},{20,16},{24,28},{28,24},{1,5},{5... | collective-permute-start | bytes 1572872 | tf_op jit(solution)/shard_map/ppermute | solution.py:42
  8.0 73.5 %collective-permute-start.33 = (bf16[128,1024]{1,0:T(8,128)(2,1)}, bf16[128,1024]{1,0:T(8,128)(2,1)S(1)}, u32[]{:S(2)}, u32[]{:S(2)}) collective-permute-start(bf16[128,1024]{1,0:T(8,128)(2,1)} %dynamic-slice_bitcast_fusion.6), channel_id=1, source_target_pairs={{0,2},{1,3},{2,0},{3,1},{4,6},{5,7},{6,4},{7,5},{8,10},{9,11},{10,... | collective-permute-start | bytes 786440 | tf_op jit(solution)/shard_map/ppermute | solution.py:50
  9.5 69.8 %collective-permute-start.32 = (bf16[256,1024]{1,0:T(8,128)(2,1)}, bf16[256,1024]{1,0:T(8,128)(2,1)}, u32[]{:S(2)}, u32[]{:S(2)}) collective-permute-start(bf16[256,1024]{1,0:T(8,128)(2,1)} %get-tuple-element.136), channel_id=1, source_target_pairs={{0,1},{1,0},{2,3},{3,2},{4,5},{5,4},{6,7},{7,6},{8,9},{9,8},{10,11... | collective-permute-start | bytes 1572872 | tf_op jit(solution)/shard_map/ppermute | solution.py:50
  11.2 73.3 %collective-permute-start.11 = (bf16[128,1024]{1,0:T(8,128)(2,1)}, bf16[128,1024]{1,0:T(8,128)(2,1)}, u32[]{:S(2)}, u32[]{:S(2)}) collective-permute-start(bf16[128,1024]{1,0:T(8,128)(2,1)} %dynamic-slice_bitcast_fusion.7), channel_id=1, source_target_pairs={{0,2},{1,3},{2,0},{3,1},{4,6},{5,7},{6,4},{7,5},{8,10},{9,11},{10,... | collective-permute-start | bytes 786440 | tf_op jit(solution)/shard_map/ppermute | solution.py:50
  11.7 72.9 %collective-permute-start.50 = (bf16[256,1024]{1,0:T(8,128)(2,1)}, bf16[256,1024]{1,0:T(8,128)(2,1)}, u32[]{:S(2)}, u32[]{:S(2)}) collective-permute-start(bf16[256,1024]{1,0:T(8,128)(2,1)} %bitcast.301), channel_id=1, source_target_pairs={{0,4},{4,0},{8,12},{12,8},{16,20},{20,16},{24,28},{28,24},{1,5},{5... | collective-permute-start | bytes 1572872 | tf_op jit(solution)/shard_map/ppermute | solution.py:42
  105.4 87.3 %collective-permute-start.4 = (bf16[128,3072]{1,0:T(8,128)(2,1)S(1)}, bf16[128,3072]{1,0:T(8,128)(2,1)}, u32[]{:S(2)}, u32[]{:S(2)}) collective-permute-start(bf16[128,3072]{1,0:T(8,128)(2,1)S(1)} %copy-done.113), channel_id=1, source_target_pairs={{0,2},{1,3},{2,0},{3,1},{4,6},{5,7},{6,4},{7,5},{8,10},{9,11},{10,... | collective-permute-start | bytes 2359304 | tf_op jit(solution)/shard_map/ppermute | solution.py:50
  125.0 125.9 %collective-permute-start.3 = (bf16[256,3072]{1,0:T(8,128)(2,1)}, bf16[256,3072]{1,0:T(8,128)(2,1)}, u32[]{:S(2)}, u32[]{:S(2)}) collective-permute-start(bf16[256,3072]{1,0:T(8,128)(2,1)} %get-tuple-element.105), channel_id=1, source_target_pairs={{0,1},{1,0},{2,3},{3,2},{4,5},{5,4},{6,7},{7,6},{8,9},{9,8},{10,11... | collective-permute-start | bytes 4718600 | tf_op jit(solution)/shard_map/ppermute | solution.py:50
  125.0 91.3 %collective-permute-start.26 = (bf16[128,3072]{1,0:T(8,128)(2,1)}, bf16[128,3072]{1,0:T(8,128)(2,1)}, u32[]{:S(2)}, u32[]{:S(2)}) collective-permute-start(bf16[128,3072]{1,0:T(8,128)(2,1)} %dynamic-slice_bitcast_fusion.2), channel_id=1, source_target_pairs={{0,2},{1,3},{2,0},{3,1},{4,6},{5,7},{6,4},{7,5},{8,10},{9,11},{10,... | collective-permute-start | bytes 2359304 | tf_op jit(solution)/shard_map/ppermute | solution.py:50
  192.7 60.0 %collective-permute-start.25 = (bf16[256,3072]{1,0:T(8,128)(2,1)}, bf16[256,3072]{1,0:T(8,128)(2,1)}, u32[]{:S(2)}, u32[]{:S(2)}) collective-permute-start(bf16[256,3072]{1,0:T(8,128)(2,1)} %get-tuple-element.106), channel_id=1, source_target_pairs={{0,1},{1,0},{2,3},{3,2},{4,5},{5,4},{6,7},{7,6},{8,9},{9,8},{10,11... | collective-permute-start | bytes 4718600 | tf_op jit(solution)/shard_map/ppermute | solution.py:50
  192.7 69.3 %collective-permute-start.5 = (bf16[128,3072]{1,0:T(8,128)(2,1)}, bf16[128,3072]{1,0:T(8,128)(2,1)}, u32[]{:S(2)}, u32[]{:S(2)}) collective-permute-start(bf16[128,3072]{1,0:T(8,128)(2,1)} %collective-permute-done.4), channel_id=1, source_target_pairs={{0,4},{1,5},{2,6},{3,7},{4,0},{5,1},{6,2},{7,3},{8,12},{9,13},{10,... | collective-permute-start | bytes 2359304 | tf_op jit(solution)/shard_map/ppermute | solution.py:50
  267.5 80.3 %collective-permute-start.15 = (bf16[256,5248]{1,0:T(8,128)(2,1)}, bf16[256,5248]{1,0:T(8,128)(2,1)}, u32[]{:S(2)}, u32[]{:S(2)}) collective-permute-start(bf16[256,5248]{1,0:T(8,128)(2,1)} %get-tuple-element.95), channel_id=1, source_target_pairs={{0,1},{1,0},{2,3},{3,2},{4,5},{5,4},{6,7},{7,6},{8,9},{9,8},{10,11... | collective-permute-start | bytes 8060936 | tf_op jit(solution)/shard_map/ppermute | solution.py:50
  267.7 58.3 %collective-permute-start.38 = (bf16[128,5248]{1,0:T(8,128)(2,1)}, bf16[128,5248]{1,0:T(8,128)(2,1)}, u32[]{:S(2)}, u32[]{:S(2)}) collective-permute-start(bf16[128,5248]{1,0:T(8,128)(2,1)} %dynamic-slice_bitcast_fusion), channel_id=1, source_target_pairs={{0,2},{1,3},{2,0},{3,1},{4,6},{5,7},{6,4},{7,5},{8,10},{9,11},{10,... | collective-permute-start | bytes 4030472 | tf_op jit(solution)/shard_map/ppermute | solution.py:50
  327.2 61.5 %collective-permute-start.18 = (bf16[128,5248]{1,0:T(8,128)(2,1)}, bf16[128,5248]{1,0:T(8,128)(2,1)}, u32[]{:S(2)}, u32[]{:S(2)}) collective-permute-start(bf16[128,5248]{1,0:T(8,128)(2,1)} %collective-permute-done.16), channel_id=1, source_target_pairs={{0,1},{1,0},{2,3},{3,2},{4,5},{5,4},{6,7},{7,6},{8,9},{9,8},{10,11... | collective-permute-start | bytes 4030472 | tf_op jit(solution)/shard_map/ppermute | solution.py:50
  327.2 59.0 %collective-permute-start.39 = (bf16[128,5248]{1,0:T(8,128)(2,1)}, bf16[128,5248]{1,0:T(8,128)(2,1)}, u32[]{:S(2)}, u32[]{:S(2)}) collective-permute-start(bf16[128,5248]{1,0:T(8,128)(2,1)} %collective-permute-done.38), channel_id=1, source_target_pairs={{0,4},{1,5},{2,6},{3,7},{4,0},{5,1},{6,2},{7,3},{8,12},{9,13},{10,... | collective-permute-start | bytes 4030472 | tf_op jit(solution)/shard_map/ppermute | solution.py:50
  350.1 432.8 %collective-permute-start.65 = (bf16[256,512]{1,0:T(8,128)(2,1)}, bf16[256,512]{1,0:T(8,128)(2,1)}, u32[]{:S(2)}, u32[]{:S(2)}) collective-permute-start(bf16[256,512]{1,0:T(8,128)(2,1)} %get-tuple-element.167), channel_id=1, source_target_pairs={{0,1},{1,0},{2,3},{3,2},{4,5},{5,4},{6,7},{7,6},{8,9},{9,8},{10,11... | collective-permute-start | bytes 786440 | tf_op jit(solution)/shard_map/ppermute | solution.py:50
  358.8 424.7 %collective-permute-start.71 = (bf16[256,512]{1,0:T(8,128)(2,1)}, bf16[256,512]{1,0:T(8,128)(2,1)}, u32[]{:S(2)}, u32[]{:S(2)}) collective-permute-start(bf16[256,512]{1,0:T(8,128)(2,1)} %get-tuple-element.171), channel_id=1, source_target_pairs={{0,1},{1,0},{2,3},{3,2},{4,5},{5,4},{6,7},{7,6},{8,9},{9,8},{10,11... | collective-permute-start | bytes 786440 | tf_op jit(solution)/shard_map/ppermute | solution.py:50
  494.8 272.1 %collective-permute-start.96 = (bf16[256,1024]{1,0:T(8,128)(2,1)}, bf16[256,1024]{1,0:T(8,128)(2,1)}, u32[]{:S(2)}, u32[]{:S(2)}) collective-permute-start(bf16[256,1024]{1,0:T(8,128)(2,1)} %fusion.141), channel_id=1, source_target_pairs={{0,1},{1,0},{2,3},{3,2},{4,5},{5,4},{6,7},{7,6},{8,9},{9,8},{10,11... | collective-permute-start | bytes 1572872 | tf_op jit(solution)/shard_map/ppermute | solution.py:50
  706.9 59.4 %collective-permute-start.95 = (bf16[256,512]{1,0:T(8,128)(2,1)}, bf16[256,512]{1,0:T(8,128)(2,1)}, u32[]{:S(2)}, u32[]{:S(2)}) collective-permute-start(bf16[256,512]{1,0:T(8,128)(2,1)} %get-tuple-element.165), channel_id=1, source_target_pairs={{0,1},{1,0},{2,3},{3,2},{4,5},{5,4},{6,7},{7,6},{8,9},{9,8},{10,11... | collective-permute-start | bytes 786440 | tf_op jit(solution)/shard_map/ppermute | solution.py:50
  786.9 56.2 %collective-permute-start.126 = (bf16[256,2624]{0,1:T(8,128)(2,1)}, bf16[256,2624]{0,1:T(8,128)(2,1)}, u32[]{:S(2)}, u32[]{:S(2)}) collective-permute-start(bf16[256,2624]{0,1:T(8,128)(2,1)} %copy.307), channel_id=1, source_target_pairs={{0,1},{1,0},{2,3},{3,2},{4,5},{5,4},{6,7},{7,6},{8,9},{9,8},{10,11... | collective-permute-start | bytes 4030472 | tf_op jit(solution)/shard_map/ppermute | solution.py:50
  916.1 109.0 %collective-permute-start.127 = (bf16[256,2624]{0,1:T(8,128)(2,1)}, bf16[256,2624]{0,1:T(8,128)(2,1)}, u32[]{:S(2)}, u32[]{:S(2)}) collective-permute-start(bf16[256,2624]{0,1:T(8,128)(2,1)} %convolution_convert_fusion.1), channel_id=1, source_target_pairs={{0,2},{1,3},{2,0},{3,1},{4,6},{5,7},{6,4},{7,5},{8,10},{9,11},{10,... | collective-permute-start | bytes 4030472 | tf_op jit(solution)/shard_map/ppermute | solution.py:50
  954.0 117.8 %collective-permute-start.133 = (bf16[256,2624]{0,1:T(8,128)(2,1)S(1)}, bf16[256,2624]{0,1:T(8,128)(2,1)S(1)}, u32[]{:S(2)}, u32[]{:S(2)}) collective-permute-start(bf16[256,2624]{0,1:T(8,128)(2,1)S(1)} %copy-done.204), channel_id=1, source_target_pairs={{0,2},{1,3},{2,0},{3,1},{4,6},{5,7},{6,4},{7,5},{8,10},{9,11},{10,... | collective-permute-start | bytes 4030472 | tf_op jit(solution)/shard_map/ppermute | solution.py:50
  962.5 118.0 %collective-permute-start.115 = (bf16[256,2624]{0,1:T(8,128)(2,1)S(1)}, bf16[256,2624]{0,1:T(8,128)(2,1)}, u32[]{:S(2)}, u32[]{:S(2)}) collective-permute-start(bf16[256,2624]{0,1:T(8,128)(2,1)S(1)} %copy-done.203), channel_id=1, source_target_pairs={{0,4},{1,5},{2,6},{3,7},{4,0},{5,1},{6,2},{7,3},{8,12},{9,13},{10,... | collective-permute-start | bytes 4030472 | tf_op jit(solution)/shard_map/ppermute | solution.py:50
  973.3 109.8 %collective-permute-start.121 = (bf16[256,2624]{0,1:T(8,128)(2,1)}, bf16[256,2624]{0,1:T(8,128)(2,1)}, u32[]{:S(2)}, u32[]{:S(2)}) collective-permute-start(bf16[256,2624]{0,1:T(8,128)(2,1)} %convolution_convert_fusion.2), channel_id=1, source_target_pairs={{0,2},{1,3},{2,0},{3,1},{4,6},{5,7},{6,4},{7,5},{8,10},{9,11},{10,... | collective-permute-start | bytes 4030472 | tf_op jit(solution)/shard_map/ppermute | solution.py:50
  1024.0 86.5 %collective-permute-start.103 = (bf16[256,2624]{0,1:T(8,128)(2,1)}, bf16[256,2624]{0,1:T(8,128)(2,1)}, u32[]{:S(2)}, u32[]{:S(2)}) collective-permute-start(bf16[256,2624]{0,1:T(8,128)(2,1)} %convolution_convert_fusion.5), channel_id=1, source_target_pairs={{0,4},{1,5},{2,6},{3,7},{4,0},{5,1},{6,2},{7,3},{8,12},{9,13},{10,... | collective-permute-start | bytes 4030472 | tf_op jit(solution)/shard_map/ppermute | solution.py:50
  (356 other events, 5200.0 us)

commit v2 on v0

v2 whole, which is shorter than its diff:
```python
import functools
import math

import jax
import jax.numpy as jnp
from jax import lax
from jax.experimental import pallas as pl
from jax.experimental.pallas import tpu as pltpu
from jax.sharding import PartitionSpec as P

HEADS = 16
HEAD_DIM = 64
FF = 2624
WINDOW = 128
BLOCK = 128
BLK_DEV = 2
LAYERS = 2

NEG = -1e30
EPS = 1e-05
THETA = 10000.0

AXES = ("seq", "fsdp")
LANES = 128
HALO = WINDOW // 2
CHUNKS = 3
FF_PAD = -(-FF // (LANES * CHUNKS)) * LANES * CHUNKS
FF_CHUNK = FF_PAD // CHUNKS
F32 = jnp.float32
BF16 = jnp.bfloat16
VMEM_LIMIT = 48 * 1024 * 1024
NT = (((1,), (1,)), ((), ()))
TN = (((0,), (0,)), ((), ()))


class Links:
    DEPTH = 2

    def __init__(self):
        self.queues = {}

    def tie(self, value, key):
        queue = self.queues.setdefault(key, [])
        if len(queue) >= self.DEPTH:
            value, _ = lax.optimization_barrier((value, queue[-self.DEPTH]))
        return value

    def swap(self, value, bit):
        count = lax.axis_size("seq") * lax.axis_size("fsdp")
        value = self.tie(value, bit)
        result = lax.ppermute(value, AXES, [(i, i ^ (1 << bit)) for i in range(count)])
        self.queues.setdefault(bit, []).append(result)
        return result


def shift(value, up):
    count = lax.axis_size("seq")
    route = [(i, i + 1) for i in range(count - 1)]
    if not up:
        route = [(b, a) for a, b in route]
    return lax.ppermute(value, "seq", route)


def flat_index():
    return lax.axis_index("seq") * lax.axis_size("fsdp") + lax.axis_index("fsdp")


def gather_pieces(links, shard):
    half = shard.shape[0] // 2
    side = lax.axis_index("seq") % 2
    sent = lax.dynamic_slice_in_dim(shard, side * half, half, 0)
    own_core = links.swap(shard, 0)
    far_x = links.swap(sent, 1)
    far_y = links.swap(far_x, 2)
    far_x_core = links.swap(far_x, 0)
    far_y_core = links.swap(far_y, 0)
    return (shard, own_core, far_x, far_y, far_x_core, far_y_core)


def piece_order():
    quarter = lax.axis_index("fsdp")
    side = lax.axis_index("seq") % 2
    one = 1 - side
    order = [quarter * 2, quarter * 2 + 1, (quarter ^ 1) * 2, (quarter ^ 1) * 2 + 1]
    order += [(quarter ^ 2) * 2 + side, (quarter ^ 2) * 2 + one]
    order += [(quarter ^ 3) * 2 + side, (quarter ^ 3) * 2 + one]
    return jnp.stack(order).astype(jnp.int32)


def stage_bits(first_x):
    levels = lax.axis_size("seq").bit_length() - 1
    rest = [2 + level for level in range(1, levels)]
    return ([1, 2] if first_x else [2, 1]) + rest


def row_order(features, bits):
    order = [0] + bits
    per_device = features >> len(order)
    rows = jnp.arange(features, dtype=jnp.int32)
    place = rows // per_device
    owner = flat_index()
    for step, bit in enumerate(order):
        taken = (place >> (len(order) - 1 - step)) & 1
        owner = owner ^ (taken << bit)
    return owner * per_device + rows % per_device


def row_picker(features, bits):
    order = row_order(features, bits)
    grid = jnp.arange(features, dtype=jnp.int32)
    return (order[:, None] == grid[None, :]).astype(BF16)


def pick(links, picker, left):
    half = picker.shape[0] // 2
    rows = lax.dot_general(picker, left, NT, preferred_element_type=F32).astype(BF16)
    return (rows[:half], links.swap(rows[half:], 0))


def scatter_vectors(vectors, bits):
    links = Links()
    features = vectors.shape[1]
    part = features
    total = jnp.take(vectors, row_order(features, bits), axis=1)
    for bit in [0] + bits:
        part = part // 2
        total = total[:, :part] + links.swap(total[:, part:], bit)
    return total


def call(kernel, outs, scratch=(), smem=1, grid=None, in_specs=None, out_specs=None, flops=0):
    params = dict(
        compiler_params=pltpu.CompilerParams(vmem_limit_bytes=VMEM_LIMIT),
        out_shape=outs,
        scratch_shapes=list(scratch),
        cost_estimate=pl.CostEstimate(flops=flops, bytes_accessed=1 << 20, transcendentals=0),
    )
    if grid is not None:
        params["grid"] = grid

    def run(*args):
        specs = in_specs
        if specs is None:
            specs = [pl.BlockSpec(memory_space=pltpu.SMEM)] * smem
            specs += [pl.BlockSpec(memory_space=pltpu.VMEM)] * (len(args) - smem)
        results = out_specs
        if results is None:
            results = jax.tree.map(lambda _: pl.BlockSpec(memory_space=pltpu.VMEM), outs)
        return pl.pallas_call(kernel, in_specs=specs, out_specs=results, **params)(*args)

    return run


def struct(shape, dtype):
    return jax.ShapeDtypeStruct(shape, dtype)


def to_pieces(offs, source, target):
    for k in range(source.shape[1] // LANES):
        start = pl.multiple_of(offs[k] * LANES, LANES)
        target[:, k * LANES : (k + 1) * LANES] = source[:, pl.ds(start, LANES)]


def from_pieces(offs, source, target):
    for k in range(source.shape[1] // LANES):
        start = pl.multiple_of(offs[k] * LANES, LANES)
        target[:, pl.ds(start, LANES)] = source[:, k * LANES : (k + 1) * LANES]


def joined(pieces, columns=slice(None)):
    return jnp.concatenate([piece[:, columns] for piece in pieces], axis=0)


def statistics(values):
    average = jnp.mean(values, axis=-1, keepdims=True)
    centred = values - average
    spread = jnp.mean(centred * centred, axis=-1, keepdims=True)
    rho = lax.rsqrt(spread + EPS)
    return centred, rho


def norm_pull(values, gain, grad):
    centred, rho = statistics(values)
    unit = centred * rho
    scaled = grad * gain
    mean_a = jnp.mean(scaled, axis=-1, keepdims=True)
    mean_b = jnp.mean(scaled * unit, axis=-1, keepdims=True)
    return rho * (scaled - mean_a - unit * mean_b), jnp.sum(grad * unit, axis=0, keepdims=True)


def turn_chunk(values, cosine, sine, sign):
    lane = lax.broadcasted_iota(jnp.int32, values.shape, 1)
    ahead = pltpu.roll(values, LANES - HEAD_DIM // 2, 1)
    behind = pltpu.roll(values, HEAD_DIM // 2, 1)
    turned = jnp.where(lane % HEAD_DIM < HEAD_DIM // 2, ahead, behind)
    if sign > 0:
        return values * cosine + turned * sine
    return values * cosine - turned * sine


def qkv_kernel(offs, x, gain, cosine, sine, p0, p1, p2, p3, p4, p5, out, normed, placed):
    step = pl.program_id(0)

    @pl.when(step == 0)
    def _():
        centred, rho = statistics(x[...])
        normed[...] = (centred * rho * gain[...]).astype(BF16)
        to_pieces(offs, normed, placed)

    product = jnp.dot(
        placed[...], joined((p0, p1, p2, p3, p4, p5)), preferred_element_type=F32
    )

    @pl.when(step < 2)
    def _():
        for k in range(product.shape[1] // LANES):
            part = slice(k * LANES, (k + 1) * LANES)
            out[:, part] = turn_chunk(product[:, part], cosine[...], sine[...], 1).astype(BF16)

    @pl.when(step == 2)
    def _():
        out[...] = product.astype(BF16)


def piece_specs(rows, columns):
    half = rows // 2
    own = pl.BlockSpec((rows, columns), lambda j: (0, j))
    far = pl.BlockSpec((half, columns), lambda j: (0, j))
    return [own, own, far, far, far, far]


def whole_spec(shape):
    return pl.BlockSpec(shape, lambda j: tuple(0 for _ in shape))


def run_qkv(offs, x, gain, cosine, sine, pieces):
    tokens, features = x.shape
    return call(
        qkv_kernel,
        (struct((tokens, 3 * features), BF16), struct((tokens, features), BF16)),
        [pltpu.VMEM((tokens, features), BF16)],
        grid=(3,),
        in_specs=[pl.BlockSpec(memory_space=pltpu.SMEM)]
        + [whole_spec(v.shape) for v in (x, gain, cosine, sine)]
        + piece_specs(pieces[0].shape[0], features),
        out_specs=(
            pl.BlockSpec((tokens, features), lambda j: (0, j)),
            whole_spec((tokens, features)),
        ),
    )(offs, x, gain, cosine, sine, *pieces)


def extend(qkv, before, after, extended):
    tokens, features = qkv.shape[0], qkv.shape[1] // 3
    extended[:HALO, :] = before[...]
    extended[HALO : HALO + tokens, :] = qkv[:, features:]
    extended[HALO + tokens :, :] = after[...]


def attend_kernel(
    offs, qkv, before, after, seg_q, seg_k, x, gain,
    p0, p1, p2, p3, p4, p5, mixed, middle, second, extended, placed,
):
    tokens, features = x.shape
    extend(qkv, before, after, extended)
    scale = 1.0 / math.sqrt(HEAD_DIM)
    span = BLOCK + 2 * HALO
    row = lax.broadcasted_iota(jnp.int32, (BLOCK, span), 0)
    col = lax.broadcasted_iota(jnp.int32, (BLOCK, span), 1)
    near = (col >= row) & (col - row <= 2 * HALO)
    low = lax.broadcasted_iota(jnp.int32, (BLOCK, LANES), 1) < HEAD_DIM
    bias = []
    for block in range(tokens // BLOCK):
        base = block * BLOCK
        same = seg_q[base : base + BLOCK, :] == seg_k[:, base : base + span]
        bias.append(jnp.where(near & same, 0.0, NEG))

    def pair(index, carry):
        lanes = pl.ds(pl.multiple_of(index * LANES, LANES), LANES)
        value_lanes = pl.ds(pl.multiple_of(features + index * LANES, LANES), LANES)
        for block in range(tokens // BLOCK):
            base = block * BLOCK
            queries = qkv[base : base + BLOCK, lanes]
            keys = extended[base : base + span, lanes]
            values = extended[base : base + span, value_lanes]
            parts = []
            for keep in (low, ~low):
                chosen = jnp.where(keep, queries, jnp.zeros_like(queries))
                raw = lax.dot_general(chosen, keys, NT, preferred_element_type=F32)
                scores = raw * scale + bias[block]
                expo = jnp.exp(scores - jnp.max(scores, axis=-1, keepdims=True))
                probs = expo * (1.0 / jnp.sum(expo, axis=-1, keepdims=True))
                parts.append(jnp.dot(probs.astype(BF16), values, preferred_element_type=F32))
            mixed[base : base + BLOCK, lanes] = jnp.where(low, parts[0], parts[1]).astype(BF16)
        return carry

    lax.fori_loop(0, features // LANES, pair, 0)
    to_pieces(offs, mixed, placed)
    total = x[...] + jnp.dot(
        placed[...], joined((p0, p1, p2, p3, p4, p5)), preferred_element_type=F32
    )
    middle[...] = total
    centred, rho = statistics(total)
    second[...] = (centred * rho * gain[...]).astype(BF16)


def run_attend(offs, qkv, before, after, seg_q, seg_k, x, gain, pieces):
    tokens, features = x.shape
    return call(
        attend_kernel,
        (
            struct((tokens, features), BF16),
            struct((tokens, features), F32),
            struct((tokens, features), BF16),
        ),
        [
            pltpu.VMEM((tokens + 2 * HALO, 2 * features), BF16),
            pltpu.VMEM((tokens, features), BF16),
        ],
    )(offs, qkv, before, after, seg_q, seg_k, x, gain, *pieces)


def mlp_kernel(offs, second, carried, p0, p1, p2, p3, p4, p5, total, gated, slope, gate, placed, part):
    pieces = (p0, p1, p2, p3, p4, p5)
    to_pieces(offs, second, placed)
    source = placed[...]
    hidden = jnp.dot(source, joined(pieces, slice(0, FF_CHUNK)), preferred_element_type=F32)
    other = jnp.dot(
        source, joined(pieces, slice(FF_CHUNK, 2 * FF_CHUNK)), preferred_element_type=F32
    )
    normal = 0.5 * (1.0 + lax.erf(hidden * math.sqrt(0.5)))
    density = jnp.exp(-0.5 * hidden * hidden) * (1.0 / math.sqrt(2.0 * math.pi))
    active = hidden * normal
    product = (active * other).astype(BF16)
    gated[...] = product
    slope[...] = ((normal + hidden * density) * other).astype(BF16)
    gate[...] = active.astype(BF16)
    part[...] = lax.dot_general(
        product,
        joined(pieces, slice(2 * FF_CHUNK, 3 * FF_CHUNK)),
        NT,
        preferred_element_type=F32,
    )
    for k in range(part.shape[1] // LANES):
        lanes = pl.ds(pl.multiple_of(offs[k] * LANES, LANES), LANES)
        total[:, lanes] = carried[:, lanes] + part[:, k * LANES : (k + 1) * LANES]


def run_mlp(offs, second, carried, pieces):
    tokens, features = second.shape
    hidden = struct((tokens, FF_CHUNK), BF16)
    return call(
        mlp_kernel,
        (struct((tokens, features), F32), hidden, hidden, hidden),
        [pltpu.VMEM((tokens, features), BF16), pltpu.VMEM((tokens, features), F32)],
    )(offs, second, carried, *pieces)


def mlp_pull(offs, upstream, slope, gate, pieces, input_grad, gate_grad, placed):
    to_pieces(offs, upstream, placed)
    gated_grad = jnp.dot(
        placed[...],
        joined(pieces, slice(2 * FF_CHUNK, 3 * FF_CHUNK)),
        preferred_element_type=F32,
    )
    first = (slope[...].astype(F32) * gated_grad).astype(BF16)
    other = (gate[...].astype(F32) * gated_grad).astype(BF16)
    input_grad[...] = first
    gate_grad[...] = other
    return lax.dot_general(
        first, joined(pieces, slice(0, FF_CHUNK)), NT, preferred_element_type=F32
    ) + lax.dot_general(
        other, joined(pieces, slice(FF_CHUNK, 2 * FF_CHUNK)), NT, preferred_element_type=F32
    )


def mlp_back_kernel(
    first, offs, upstream, slope, gate, carried, p0, p1, p2, p3, p4, p5,
    total, input_grad, gate_grad, placed,
):
    part = mlp_pull(
        offs, upstream, slope, gate, (p0, p1, p2, p3, p4, p5), input_grad, gate_grad, placed
    )
    total[...] = part if first else carried[...] + part


def mlp_back_last_kernel(
    offs, upstream, slope, gate, carried, residual_grad, middle, gain, p0, p1, p2, p3, p4, p5,
    middle_grad, middle_grad_b, gain_grad, input_grad, gate_grad, placed, sums, ordered,
):
    part = mlp_pull(
        offs, upstream, slope, gate, (p0, p1, p2, p3, p4, p5), input_grad, gate_grad, placed
    )
    sums[...] = carried[...] + part
    from_pieces(offs, sums, ordered)
    pulled, gains = norm_pull(middle[...], gain[...], ordered[...])
    result = residual_grad[...] + pulled
    middle_grad[...] = result
    middle_grad_b[...] = result.astype(BF16)
    gain_grad[...] = gains


def run_mlp_back(offs, upstream, slope, gate, carried, pieces):
    tokens, features = upstream.shape
    hidden = struct((tokens, FF_CHUNK), BF16)
    first = carried is None
    if first:
        carried = jnp.zeros((8, LANES), F32)
    return call(
        functools.partial(mlp_back_kernel, first),
        (struct((tokens, features), F32), hidden, hidden),
        [pltpu.VMEM((tokens, features), BF16)],
    )(offs, upstream, slope, gate, carried, *pieces)


def run_mlp_back_last(offs, upstream, slope, gate, carried, residual_grad, middle, gain, pieces):
    tokens, features = upstream.shape
    hidden = struct((tokens, FF_CHUNK), BF16)
    return call(
        mlp_back_last_kernel,
        (
            struct((tokens, features), F32),
            struct((tokens, features), BF16),
            struct((1, features), F32),
            hidden,
            hidden,
        ),
        [
            pltpu.VMEM((tokens, features), BF16),
            pltpu.VMEM((tokens, features), F32),
            pltpu.VMEM((tokens, features), F32),
        ],
    )(offs, upstream, slope, gate, carried, residual_grad, middle, gain, *pieces)


def attend_back_kernel(
    offs, middle_grad, qkv, before, after, seg_q, seg_k, cosine, sine, p0, p1, p2, p3, p4, p5,
    query_grad, own_grad, rim_before, rim_after, extended, mixed_grad, extended_grad,
):
    tokens, features = middle_grad.shape
    extend(qkv, before, after, extended)
    placed = lax.dot_general(
        middle_grad[...], joined((p0, p1, p2, p3, p4, p5)), NT, preferred_element_type=F32
    ).astype(BF16)
    for k in range(features // LANES):
        lanes = pl.ds(pl.multiple_of(offs[k] * LANES, LANES), LANES)
        mixed_grad[:, lanes] = placed[:, k * LANES : (k + 1) * LANES]
    scale = 1.0 / math.sqrt(HEAD_DIM)
    span = BLOCK + 2 * HALO
    row = lax.broadcasted_iota(jnp.int32, (span, BLOCK), 1)
    col = lax.broadcasted_iota(jnp.int32, (span, BLOCK), 0)
    near = (col >= row) & (col - row <= 2 * HALO)
    low = lax.broadcasted_iota(jnp.int32, (BLOCK, LANES), 1) < HEAD_DIM
    bias = []
    for block in range(tokens // BLOCK):
        base = block * BLOCK
        same = seg_q[:, base : base + BLOCK] == seg_k[base : base + span, :]
        bias.append(jnp.where(near & same, 0.0, NEG))

    def pair(index, carry):
        lanes = pl.ds(pl.multiple_of(index * LANES, LANES), LANES)
        value_lanes = pl.ds(pl.multiple_of(features + index * LANES, LANES), LANES)
        key_sums = []
        value_sums = []
        for block in range(tokens // BLOCK):
            base = block * BLOCK
            here = slice(base, base + BLOCK)
            queries = qkv[here, lanes]
            grads = mixed_grad[here, lanes]
            keys = extended[base : base + span, lanes]
            values = extended[base : base + span, value_lanes]
            key_sum = None
            value_sum = None
            query_parts = []
            for keep in (low, ~low):
                chosen = jnp.where(keep, queries, jnp.zeros_like(queries))
                chosen_grad = jnp.where(keep, grads, jnp.zeros_like(grads))
                raw = lax.dot_general(keys, chosen, NT, preferred_element_type=F32)
                scores = raw * scale + bias[block]
                expo = jnp.exp(scores - jnp.max(scores, axis=0, keepdims=True))
                probs = expo * (1.0 / jnp.sum(expo, axis=0, keepdims=True))
                prob_grad = lax.dot_general(values, chosen_grad, NT, preferred_element_type=F32)
                delta = jnp.sum(prob_grad * probs, axis=0, keepdims=True)
                score_grad = (probs * (prob_grad - delta) * scale).astype(BF16)
                query_parts.append(
                    lax.dot_general(score_grad, keys, TN, preferred_element_type=F32)
                )
                to_keys = jnp.dot(score_grad, chosen, preferred_element_type=F32)
                to_values = jnp.dot(
                    probs.astype(BF16), chosen_grad, preferred_element_type=F32
                )
                key_sum = to_keys if key_sum is None else key_sum + to_keys
                value_sum = to_values if value_sum is None else value_sum + to_values
            joint = jnp.where(low, query_parts[0], query_parts[1])
            query_grad[here, lanes] = turn_chunk(
                joint, cosine[here, :], sine[here, :], -1
            ).astype(BF16)
            key_sums.append(key_sum)
            value_sums.append(value_sum)
        for sums, place in ((key_sums, lanes), (value_sums, value_lanes)):
            over = 2 * HALO
            extended_grad[:BLOCK, place] = sums[0][:BLOCK]
            extended_grad[BLOCK : BLOCK + over, place] = sums[0][BLOCK:] + sums[1][:over]
            extended_grad[BLOCK + over :, place] = sums[1][over:]
        return carry

    lax.fori_loop(0, features // LANES, pair, 0)
    rim_before[...] = extended_grad[:HALO, :].astype(BF16)
    own_grad[...] = extended_grad[HALO : HALO + tokens, :]
    rim_after[...] = extended_grad[HALO + tokens :, :].astype(BF16)


def run_attend_back(offs, middle_grad, qkv, before, after, seg_q, seg_k, cosine, sine, pieces):
    tokens, features = middle_grad.shape
    rim = struct((HALO, 2 * features), BF16)
    return call(
        attend_back_kernel,
        (struct((tokens, features), BF16), struct((tokens, 2 * features), F32), rim, rim),
        [
            pltpu.VMEM((tokens + 2 * HALO, 2 * features), BF16),
            pltpu.VMEM((tokens, features), BF16),
            pltpu.VMEM((tokens + 2 * HALO, 2 * features), F32),
        ],
    )(offs, middle_grad, qkv, before, after, seg_q, seg_k, cosine, sine, *pieces)


def qkv_back_kernel(
    offs, query_grad, own_grad, arrived_first, arrived_last, cosine, sine, x, gain, middle_grad,
    p0, p1, p2, p3, p4, p5, joint, upstream, upstream_b, gain_grad, sums, ordered,
):
    step = pl.program_id(0)
    tokens, features = x.shape

    @pl.when(step == 0)
    def _():
        joint[...] = query_grad[...]

    for part in (1, 2):

        @pl.when(step == part)
        def _():
            for k in range(features // LANES):
                here = slice(k * LANES, (k + 1) * LANES)
                there = slice((part - 1) * features + k * LANES, (part - 1) * features + (k + 1) * LANES)
                rows = [
                    own_grad[:HALO, there] + arrived_first[:, there].astype(F32),
                    own_grad[HALO : tokens - HALO, there],
                    own_grad[tokens - HALO :, there] + arrived_last[:, there].astype(F32),
                ]
                grads = jnp.concatenate(rows, axis=0)
                if part == 1:
                    grads = turn_chunk(grads, cosine[...], sine[...], -1)
                joint[:, here] = grads.astype(BF16)

    product = lax.dot_general(
        joint[...], joined((p0, p1, p2, p3, p4, p5)), NT, preferred_element_type=F32
    )

    @pl.when(step == 0)
    def _():
        sums[...] = product

    @pl.when(step > 0)
    def _():
        sums[...] += product

    @pl.when(step == 2)
    def _():
        from_pieces(offs, sums, ordered)
        pulled, gains = norm_pull(x[...], gain[...], ordered[...])
        result = middle_grad[...] + pulled
        upstream[...] = result
        upstream_b[...] = result.astype(BF16)
        gain_grad[...] = gains


def run_qkv_back(
    offs, query_grad, own_grad, arrived_first, arrived_last, cosine, sine, x, gain, middle_grad, pieces
):
    tokens, features = x.shape
    whole = (query_grad, own_grad, arrived_first, arrived_last, cosine, sine, x, gain, middle_grad)
    return call(
        qkv_back_kernel,
        (
            struct((tokens, 3 * features), BF16),
            struct((tokens, features), F32),
            struct((tokens, features), BF16),
            struct((1, features), F32),
        ),
        [pltpu.VMEM((tokens, features), F32), pltpu.VMEM((tokens, features), F32)],
        grid=(3,),
        in_specs=[pl.BlockSpec(memory_space=pltpu.SMEM)]
        + [whole_spec(v.shape) for v in whole]
        + piece_specs(pieces[0].shape[0], features),
        out_specs=(
            pl.BlockSpec((tokens, features), lambda j: (0, j)),
            whole_spec((tokens, features)),
            whole_spec((tokens, features)),
            whole_spec((1, features)),
        ),
    )(offs, *whole, *pieces)


def outer_kernel(count, *refs):
    keep, send = refs[4 * count :]
    half = keep.shape[0]
    column = 0
    for k in range(count):
        left, left_far, right, right_far = refs[4 * k : 4 * k + 4]
        width = right.shape[1]
        for rows, target in ((slice(half, 2 * half), send), (slice(0, half), keep)):
            target[:, column : column + width] = (
                jnp.dot(left[rows, :], right[...], preferred_element_type=F32)
                + jnp.dot(left_far[rows, :], right_far[...], preferred_element_type=F32)
            ).astype(BF16)
        column += width


def run_outer(terms):
    flat = []
    specs = []
    width = 0
    for (left, left_far), (right, right_far, start, columns) in terms:
        flat += [left, left_far, right, right_far]
        specs += [whole_spec(left.shape)] * 2
        specs += [
            pl.BlockSpec((right.shape[0], columns), lambda j, at=start // columns: (0, at))
        ] * 2
        width += columns
    half = terms[0][0][0].shape[0] // 2
    out = struct((half, width), BF16)
    return call(
        functools.partial(outer_kernel, len(terms)),
        (out, out),
        grid=(1,),
        in_specs=specs,
        out_specs=(whole_spec((half, width)),) * 2,
    )(*flat)


class Sum:
    def __init__(self, links, terms, bits):
        self.links = links
        self.bits = list(bits)
        self.keep, send = run_outer(terms)
        self.come = links.swap(send, self.bits.pop(0))

    def step(self, final=False):
        total = self.keep.shape[0]
        if final:
            return self.keep.astype(F32) + self.come.astype(F32)
        half = total // 2
        send = (self.keep[half:].astype(F32) + self.come[half:].astype(F32)).astype(BF16)
        self.keep = (self.keep[:half].astype(F32) + self.come[:half].astype(F32)).astype(BF16)
        self.come = self.links.swap(send, self.bits.pop(0))


class Joint:
    def __init__(self, links, sums):
        self.sums = sums
        self.links = links
        self.bits = list(sums[0].bits)
        self.keep = None

    def advance(self):
        if self.keep is None and len(self.sums[0].bits) > len(self.bits) - 1:
            for part in self.sums:
                part.step()
            self.bits = list(self.sums[0].bits)
            self.keep = False
            return None
        if self.keep is False:
            keeps = [part.keep for part in self.sums]
            comes = [part.come for part in self.sums]
        else:
            keeps, comes = [self.keep], [self.come]
        if not self.bits:
            rows = [k.astype(F32) + c.astype(F32) for k, c in zip(keeps, comes)]
            return jnp.concatenate(rows, axis=1)
        half = keeps[0].shape[0] // 2

        def added(rows):
            parts = [
                (k[rows].astype(F32) + c[rows].astype(F32)).astype(BF16)
                for k, c in zip(keeps, comes)
            ]
            return jnp.concatenate(parts, axis=1)

        send = added(slice(half, None))
        self.keep = added(slice(0, half))
        self.come = self.links.swap(send, self.bits.pop(0))
        return None


class Pipeline:
    def __init__(self):
        self.running = []

    def advance(self):
        for item in list(self.running):
            result = item[0].advance()
            if result is not None:
                item[1](result)
                self.running.remove(item)

    def add(self, joint, deliver):
        self.running.append((joint, deliver))

    def finish(self):
        while self.running:
            self.advance()


def rope_tables(position):
    inverse = jnp.power(THETA, -jnp.arange(0, HEAD_DIM, 2, dtype=F32) / HEAD_DIM)
    angles = position[:, None] * inverse[None, :]
    cosine, sine = jnp.cos(angles), jnp.sin(angles)
    return (
        jnp.concatenate([cosine, cosine, cosine, cosine], axis=-1),
        jnp.concatenate([-sine, sine, -sine, sine], axis=-1),
    )


def layout(positions, lengths, total):
    count = lengths.shape[0]
    blocks = (lengths + BLOCK - 1) // BLOCK
    first = (jnp.cumsum(blocks) - blocks) * BLOCK
    owner = jnp.sum((positions[:, None] >= first[None, :]).astype(jnp.int32), axis=1) - 1
    table = owner[:, None] == jnp.arange(count, dtype=jnp.int32)[None, :]
    start = jnp.sum(jnp.where(table, first[None, :], 0), axis=1)
    span = jnp.sum(jnp.where(table, lengths[None, :], 0), axis=1)
    local = positions - start
    inside = (positions >= 0) & (positions < total)
    valid = inside & (local < span)
    segment = jnp.where(inside, jnp.where(valid, owner, owner + count), -1)
    return (segment, local, valid)


def body(
    tokens,
    cotangent,
    lengths,
    block_perm,
    attn_gain,
    qkv_weight,
    proj_weight,
    mlp_gain,
    wide_weight,
    narrow_weight,
):
    links = Links()
    seq_index = lax.axis_index("seq")
    seq_count = lax.axis_size("seq")
    levels = seq_count.bit_length() - 1
    tok_dev = tokens.shape[1]
    features = tokens.shape[2]
    block_rows = tok_dev // BLK_DEV
    order_map = block_perm[0]
    target = order_map[0::BLK_DEV] // BLK_DEV
    source = jnp.arange(seq_count, dtype=jnp.int32)

    def holder(bit_level):
        low_mask = (1 << bit_level) - 1
        place = jnp.bitwise_or(
            jnp.bitwise_and(target, low_mask), jnp.bitwise_and(source, ~low_mask)
        )
        return jnp.sum(jnp.where(place == seq_index, source, 0))

    home_index = holder(levels)
    slot_of = lax.dynamic_slice_in_dim(order_map, home_index * BLK_DEV, BLK_DEV) % BLK_DEV
    crossed = slot_of[0] == 1

    def crossing(rows):
        turned = jnp.concatenate([rows[block_rows:], rows[:block_rows]], axis=0)
        return jnp.where(crossed, turned, rows)

    def to_packed_step(moving, bit_level):
        payload = holder(bit_level)
        goal_index = jnp.sum(jnp.where(source == payload, target, 0))
        flipped = (
            jnp.bitwise_and(jnp.right_shift(jnp.bitwise_xor(seq_index, goal_index), bit_level), 1)
            == 1
        )
        return jnp.where(flipped, links.swap(moving, 2 + bit_level), moving)

    def to_given_step(moving, bit_level):
        payload = holder(bit_level + 1)
        flipped = (
            jnp.bitwise_and(jnp.right_shift(jnp.bitwise_xor(seq_index, payload), bit_level), 1) == 1
        )
        return jnp.where(flipped, links.swap(moving, 2 + bit_level), moving)

    def to_packed(rows):
        for bit_level in range(levels):
            rows = to_packed_step(rows, bit_level)
        return crossing(rows)

    def to_given(rows):
        rows = crossing(rows)
        for bit_level in reversed(range(levels)):
            rows = to_given_step(rows, bit_level)
        return rows

    total = seq_count * tok_dev
    own_place = seq_index * tok_dev + jnp.arange(tok_dev, dtype=jnp.int32)
    key_place = seq_index * tok_dev - HALO + jnp.arange(tok_dev + 2 * HALO, dtype=jnp.int32)
    seg_query, local_query, valid_query = layout(own_place, lengths[0], total)
    seg_key, _, _ = layout(key_place, lengths[0], total)
    cosine, sine = rope_tables(local_query.astype(F32))
    seg_q_col, seg_q_row = seg_query[:, None], seg_query[None, :]
    seg_k_col, seg_k_row = seg_key[:, None], seg_key[None, :]
    offs = piece_order()
    bits_x, bits_y = stage_bits(True), stage_bits(False)
    picker_x, picker_y = row_picker(features, bits_x), row_picker(features, bits_y)

    gains = jnp.concatenate([attn_gain, mlp_gain], axis=0)
    gains = lax.all_gather(gains, "fsdp", axis=1, tiled=True).astype(F32)
    gains_a = [gains[layer : layer + 1] for layer in range(LAYERS)]
    gains_m = [gains[LAYERS + layer : LAYERS + layer + 1] for layer in range(LAYERS)]

    def mlp_shard(layer, chunk):
        parts = []
        start, stop = chunk * FF_CHUNK, min((chunk + 1) * FF_CHUNK, FF)
        for array, base in ((wide_weight, 0), (wide_weight, FF), (narrow_weight, 0)):
            part = array[layer, :, base + start : base + stop]
            parts.append(jnp.pad(part, ((0, 0), (0, FF_CHUNK - (stop - start)))))
        return jnp.concatenate(parts, axis=1)

    residual = to_packed(tokens[0]).astype(F32)
    w_qkv, w_proj, w_mlp = [], [], []
    for layer in range(LAYERS):
        w_qkv.append(gather_pieces(links, qkv_weight[layer]))
        w_proj.append(gather_pieces(links, proj_weight[layer]))
        w_mlp.append(
            [gather_pieces(links, mlp_shard(layer, chunk)) for chunk in range(CHUNKS)]
        )
    packed_cot = to_packed(cotangent[0])

    kept = []
    for layer in range(LAYERS):
        qkv, normed = run_qkv(offs, residual, gains_a[layer], cosine, sine, w_qkv[layer])
        edges = qkv[:, features:]
        before = shift(edges[tok_dev - HALO :], True)
        after = shift(edges[:HALO], False)
        mixed, middle, second = run_attend(
            offs, qkv, before, after, seg_q_col, seg_k_row, residual, gains_m[layer], w_proj[layer]
        )
        start = residual
        residual = middle
        hidden = []
        for chunk in range(CHUNKS):
            residual, gated, slope, gate = run_mlp(offs, second, residual, w_mlp[layer][chunk])
            hidden.append((gated, links.swap(gated, 0), slope, gate))
        picks = (
            pick(links, picker_x, normed),
            pick(links, picker_y, normed),
            pick(links, picker_y, mixed),
            pick(links, picker_x, second),
            pick(links, picker_y, second),
        )
        kept.append((start, qkv, before, after, middle, hidden, picks))

    block_out = to_given(residual.astype(BF16))

    upstream_b = packed_cot * valid_query[:, None].astype(BF16)
    upstream = upstream_b.astype(F32)
    grads = [None] * LAYERS
    pipeline = Pipeline()
    for layer in reversed(range(LAYERS)):
        start, qkv, before, after, middle, hidden, picks = kept[layer]
        normed_x, normed_y, mixed_y, second_x, second_y = picks
        upstream_x = pick(links, picker_x, upstream_b)
        found = {}
        carried = None
        for chunk in range(CHUNKS):
            gated, gated_far, slope, gate = hidden[chunk]
            if chunk < CHUNKS - 1:
                carried, input_grad, gate_grad = run_mlp_back(
                    offs, upstream_b, slope, gate, carried, w_mlp[layer][chunk]
                )
            else:
                middle_grad, middle_grad_b, mlp_term, input_grad, gate_grad = run_mlp_back_last(
                    offs, upstream_b, slope, gate, carried, upstream, middle, gains_m[layer],
                    w_mlp[layer][chunk],
                )
            input_far = links.swap(input_grad, 0)
            gate_far = links.swap(gate_grad, 0)
            parts = [
                Sum(
                    links,
                    [
                        (upstream_x, (gated, gated_far, 0, FF_CHUNK)),
                        (second_x, (gate_grad, gate_far, 0, FF_CHUNK)),
                    ],
                    bits_x,
                ),
                Sum(links, [(second_y, (input_grad, input_far, 0, FF_CHUNK))], bits_y),
            ]
            pipeline.advance()
            pipeline.add(
                Joint(links, parts), functools.partial(found.__setitem__, ("mlp", chunk))
            )
        middle_far = links.swap(middle_grad_b, 0)
        parts = [Sum(links, [(mixed_y, (middle_grad_b, middle_far, 0, features))], bits_y)]
        pipeline.advance()
        pipeline.add(Joint(links, parts), functools.partial(found.__setitem__, "proj"))
        query_grad, own_grad, rim_before, rim_after = run_attend_back(
            offs, middle_grad_b, qkv, before, after, seg_q_row, seg_k_col, cosine, sine, w_proj[layer]
        )
        arrived_first = shift(rim_after, True)
        arrived_last = shift(rim_before, False)
        joint_grad, upstream, upstream_b, attn_term = run_qkv_back(
            offs, query_grad, own_grad, arrived_first, arrived_last, cosine, sine, start,
            gains_a[layer], middle_grad, w_qkv[layer],
        )
        joint_far = links.swap(joint_grad, 0)
        split = 3 * features // 2
        parts = [
            Sum(links, [(normed_x, (joint_grad, joint_far, split, split))], bits_x),
            Sum(links, [(normed_y, (joint_grad, joint_far, 0, split))], bits_y),
        ]
        pipeline.advance()
        pipeline.add(Joint(links, parts), functools.partial(found.__setitem__, "qkv"))
        grads[layer] = (found, attn_term, mlp_term)
    token_grad = to_given(upstream_b)
    pipeline.finish()
    vectors = [grads[layer][1] for layer in range(LAYERS)]
    vectors += [grads[layer][2] for layer in range(LAYERS)]
    gain_sums = scatter_vectors(jnp.concatenate(vectors, axis=0), bits_x)

    def wide(found):
        parts = [found["mlp", chunk] for chunk in range(CHUNKS)]
        inputs = [part[:, 2 * FF_CHUNK :] for part in parts]
        gates = [part[:, FF_CHUNK : 2 * FF_CHUNK] for part in parts]
        return jnp.concatenate(
            [jnp.concatenate(half, axis=1)[:, :FF] for half in (inputs, gates)], axis=1
        )

    def narrow(found):
        parts = [found["mlp", chunk][:, :FF_CHUNK] for chunk in range(CHUNKS)]
        return jnp.concatenate(parts, axis=1)[:, :FF]

    def qkv_sum(found):
        split = 3 * features // 2
        return jnp.concatenate([found["qkv"][:, split:], found["qkv"][:, :split]], axis=1)

    founds = [grads[layer][0] for layer in range(LAYERS)]
    return (
        block_out[None],
        token_grad[None],
        gain_sums[:LAYERS],
        jnp.stack([qkv_sum(found) for found in founds]),
        jnp.stack([found["proj"] for found in founds]),
        gain_sums[LAYERS:],
        jnp.stack([wide(found) for found in founds]),
        jnp.stack([narrow(found) for found in founds]),
    )


def solution(mesh):
    in_specs = (
        P("fsdp", "seq", None),
        P("fsdp", "seq", None),
        P("fsdp", None),
        P("fsdp", None),
        P(None, "fsdp"),
        P(None, "fsdp", None),
        P(None, "fsdp", None),
        P(None, "fsdp"),
        P(None, "fsdp", None),
        P(None, "fsdp", None),
    )
    out_specs = (
        P("fsdp", "seq", None),
        P("fsdp", "seq", None),
        P(None, ("seq", "fsdp")),
        P(None, ("seq", "fsdp"), None),
        P(None, ("seq", "fsdp"), None),
        P(None, ("seq", "fsdp")),
        P(None, ("seq", "fsdp"), None),
        P(None, ("seq", "fsdp"), None),
    )
    return jax.shard_map(body, mesh=mesh, in_specs=in_specs, out_specs=out_specs, check_vma=False)
```

time: 1850 us -> 860 us (0.46)
  waiting for transfers between devices: 1240 us -> 334 us
  matrix products: 302 us -> 10.9 us
  Pallas kernels: 0 us -> 166 us
  starting transfers between devices: 44.1 us -> 164 us
  blocking collectives: 116 us -> 5.46 us
  local copies, waits for them, and re-layouts: 64.4 us -> 105 us
    reduce_scatter x8 -> x0, waiting for transfers between devices: 920 us -> none  [the longest x2 467 us: body(): lax.psum_scatter(grad_terms[4], ('seq', 'fsdp'), scatter_dimension=0, til...]
    dot_general x36 -> x12, matrix products: 302 us -> 10.9 us  [pick(): lax.dot_general(picker, left, NT, preferred_element_type=F32).astype(BF16)]
    ppermute x20 -> x165, waiting for transfers between devices: 151 us -> 334 us  [the longest x157 309 us: swap(): lax.ppermute(value, AXES, [(i, i ^ 1 << bit) for i in range(count)])]
    pallas_call x0 -> x38, Pallas kernels: none -> 166 us  [run(): pl.pallas_call(kernel, in_specs=specs, out_specs=results, **params)(*args)]
    all_gather x8 -> x0, waiting for transfers between devices: 166 us -> none  [the longest x2 62.7 us: body(): lax.all_gather(narrow_weight[layer_index], 'fsdp', axis=0, tiled=True)]
    ppermute x20 -> x165, starting transfers between devices: 43.4 us -> 164 us  [the longest x157 146 us: swap(): lax.ppermute(value, AXES, [(i, i ^ 1 << bit) for i in range(count)])]
    unnamed x1 -> x0, blocking collectives: 95.4 us -> none
    unnamed x170 -> x428, local copies, waits for them, and re-layouts: 22.1 us -> 49.9 us
  transfers between devices with their start and end apart: 36 -> 165, of which waited for: 21 -> 59; matrix products, arithmetic and copies ran while one was open for 20% -> 16% of each run, Pallas kernels for 0% -> 19%
where the time goes in v2:
time: 860 us; the launch traced here: 854 us
  waiting for transfers between devices  334 us (39%)
  Pallas kernels  166 us (19%)
  starting transfers between devices  164 us (19%)
  local copies, waits for them, and re-layouts  105 us (12%)
  other arithmetic  60 us (7%)
  matrix products  10.9 us (1%)
    ppermute x157, waiting for transfers between devices, swap(): lax.ppermute(value, AXES, [(i, i ^ 1 << bit) for i in range(count)])  309 us
    pallas_call x38, Pallas kernels, run(): pl.pallas_call(kernel, in_specs=specs, out_specs=results, **params)(*args)  166 us
    ppermute x157, starting transfers between devices, swap(): lax.ppermute(value, AXES, [(i, i ^ 1 << bit) for i in range(count)])  146 us
    unnamed x428, local copies, waits for them, and re-layouts  49.9 us
    ppermute x8, waiting for transfers between devices, shift(): return lax.ppermute(value, 'seq', route)  25.1 us
    ppermute x8, starting transfers between devices, shift(): return lax.ppermute(value, 'seq', route)  18.4 us
  transfers between devices with their start and end apart: 165, of which 59 were waited for; matrix products, arithmetic and copies ran while one was open for 16% of the time, Pallas kernels for 19%

profile of v2, /device:TPU:0, one launch (start us, length us, event | category | flops | bytes accessed | tf_op | source)
XLA Modules:
  0.0 854.4 jit_solution(8681299258974850395)
XLA Ops:
  53.5 18.2 %collective-permute-done.5.p3 = bf16[128,3072]{1,0:T(8,128)(2,1)S(1)} collective-permute-done((bf16[128,3072]{1,0:T(8,128)(2,1)S(1)}, bf16[128,3072]{1,0:T(8,128)(2,1)S(1)}, u32[]{:S(2)}, u32[]{:S(2)}) %collective-permute-start.5) | collective-permute-done | bytes 786464 | tf_op jit(solution)/shard_map/ppermute | solution.py:51
  101.9 14.4 %collective-permute-done.17.p3 = bf16[128,2688]{1,0:T(8,128)(2,1)S(1)} collective-permute-done((bf16[128,2688]{1,0:T(8,128)(2,1)}, bf16[128,2688]{1,0:T(8,128)(2,1)S(1)}, u32[]{:S(2)}, u32[]{:S(2)}) %collective-permute-start.17) | collective-permute-done | bytes 688160 | tf_op jit(solution)/shard_map/ppermute | solution.py:51
  123.8 11.3 %collective-permute-done.22.p3 = bf16[128,2688]{1,0:T(8,128)(2,1)S(1)} collective-permute-done((bf16[128,2688]{1,0:T(8,128)(2,1)S(1)}, bf16[128,2688]{1,0:T(8,128)(2,1)S(1)}, u32[]{:S(2)}, u32[]{:S(2)}) %collective-permute-start.22) | collective-permute-done | bytes 688160 | tf_op jit(solution)/shard_map/ppermute | solution.py:51
  141.4 8.4 collective-permute-done.1
  164.6 12.9 %collective-permute-done.2 = bf16[256,1024]{1,0:T(8,128)(2,1)} collective-permute-done((bf16[256,1024]{1,0:T(8,128)(2,1)}, bf16[256,1024]{1,0:T(8,128)(2,1)}, u32[]{:S(2)}, u32[]{:S(2)}) %collective-permute-start.2) | collective-permute-done | bytes 524320 | tf_op jit(solution)/shard_map/ppermute | solution.py:51
  195.1 8.9 %collective-permute-done.39.p3 = bf16[128,1024]{1,0:T(8,128)(2,1)S(1)} collective-permute-done((bf16[128,1024]{1,0:T(8,128)(2,1)}, bf16[128,1024]{1,0:T(8,128)(2,1)S(1)}, u32[]{:S(2)}, u32[]{:S(2)}) %collective-permute-start.39) | collective-permute-done | bytes 262176 | tf_op jit(solution)/shard_map/ppermute | solution.py:51
  206.2 11.9 %collective-permute-done.49.p3 = bf16[128,2688]{1,0:T(8,128)(2,1)} collective-permute-done((bf16[128,2688]{1,0:T(8,128)(2,1)S(1)}, bf16[128,2688]{1,0:T(8,128)(2,1)}, u32[]{:S(2)}, u32[]{:S(2)}) %collective-permute-start.49) | collective-permute-done | bytes 688160 | tf_op jit(solution)/shard_map/ppermute | solution.py:51
  230.7 9.1 %collective-permute-done.9.after = bf16[64,2048]{1,0:T(8,128)(2,1)S(1)} collective-permute-done((bf16[64,2048]{1,0:T(8,128)(2,1)S(1)}, bf16[64,2048]{1,0:T(8,128)(2,1)S(1)}, u32[]{:S(2)}, u32[]{:S(2)}) %collective-permute-start.9) | collective-permute-done | bytes 262176 | tf_op jit(solution)/shard_map/ppermute | solution.py:61
  239.9 10.4 %shard_map.162 = (bf16[256,1024]{1,0:T(8,128)(2,1)S(1)}, f32[256,1024]{1,0:T(8,128)S(1)}, bf16[256,1024]{1,0:T(8,128)(2,1)S(1)}) custom-call(s32[8]{0:T(128)S(1)} %stack.71.offs, bf16[256,3072]{1,0:T(8,128)(2,1)} %get-tuple-element.258.qkv, bf16[64,2048]{1,0:T(8,128)(2,1)S(1)} %collective-permute-done.8.before, ...), custom_call_target="tpu_custom_call" | custom-call | bytes 1048576 | tf_op jit(solution)/shard_map/pallas_call | solution.py:149
  260.4 7.3 collective-permute-done.61
  304.1 7.1 shard_map.166
  326.3 10.1 %shard_map.167 = (bf16[256,1024]{1,0:T(8,128)(2,1)S(1)}, f32[256,1024]{1,0:T(8,128)S(1)}, bf16[256,1024]{1,0:T(8,128)(2,1)S(1)}) custom-call(s32[8]{0:T(128)S(1)} %stack.71.offs, bf16[256,3072]{1,0:T(8,128)(2,1)} %get-tuple-element.288.qkv, bf16[64,2048]{1,0:T(8,128)(2,1)S(1)} %collective-permute-done.35.before, ...), custom_call_target="tpu_custom_call" | custom-call | bytes 1048576 | tf_op jit(solution)/shard_map/pallas_call | solution.py:149
  392.9 15.7 %shard_map.174 = (bf16[256,1024]{1,0:T(8,128)(2,1)S(1)}, f32[256,2048]{1,0:T(8,128)}, bf16[64,2048]{1,0:T(8,128)(2,1)S(1)}, bf16[64,2048]{1,0:T(8,128)(2,1)S(1)}) custom-call(s32[8]{0:T(128)S(1)} %stack.71.offs, bf16[256,1024]{1,0:T(8,128)(2,1)S(1)} %get-tuple-element.369.middle_grad.refs_2_, bf16[256,3072]{1,0:T(8,128)(2,1)} %get-tuple-element.288.qkv, ...), custom_call_target="tpu_custom_call" | custom-call | bytes 1048576 | tf_op jit(solution)/shard_map/pallas_call | solution.py:149
  416.5 8.3 collective-permute-done.63.arrived_first
  424.8 7.9 shard_map.175
  453.5 16.4 %shard_map.179 = (bf16[256,1024]{1,0:T(8,128)(2,1)S(1)}, f32[256,2048]{1,0:T(8,128)}, bf16[64,2048]{1,0:T(8,128)(2,1)S(1)}, bf16[64,2048]{1,0:T(8,128)(2,1)S(1)}) custom-call(s32[8]{0:T(128)S(1)} %stack.71.offs, bf16[256,1024]{1,0:T(8,128)(2,1)S(1)} %get-tuple-element.483.middle_grad.refs_2_, bf16[256,3072]{1,0:T(8,128)(2,1)} %get-tuple-element.258.qkv, ...), custom_call_target="tpu_custom_call" | custom-call | bytes 1048576 | tf_op jit(solution)/shard_map/pallas_call | solution.py:149
  485.1 8.2 shard_map.180
  519.3 11.7 %collective-permute-done.142 = f32[4,64]{0,1:T(8,128)S(1)} collective-permute-done((f32[4,64]{0,1:T(8,128)S(1)}, f32[4,64]{0,1:T(8,128)S(1)}, u32[]{:S(2)}, u32[]{:S(2)}) %collective-permute-start.142) | collective-permute-done | bytes 1056 | tf_op jit(solution)/shard_map/ppermute | solution.py:51
  573.5 14.5 %collective-permute-done.97 = bf16[128,896]{1,0:T(8,128)(2,1)S(1)} collective-permute-done((bf16[128,896]{1,0:T(8,128)(2,1)S(1)}, bf16[128,896]{1,0:T(8,128)(2,1)S(1)}, u32[]{:S(2)}, u32[]{:S(2)}) %collective-permute-start.97) | collective-permute-done | bytes 229408 | tf_op jit(solution)/shard_map/ppermute | solution.py:51
  680.8 21.8 %collective-permute-done.115 = bf16[128,1536]{1,0:T(8,128)(2,1)S(1)} collective-permute-done((bf16[128,1536]{1,0:T(8,128)(2,1)}, bf16[128,1536]{1,0:T(8,128)(2,1)S(1)}, u32[]{:S(2)}, u32[]{:S(2)}) %collective-permute-start.115) | collective-permute-done | bytes 393248 | tf_op jit(solution)/shard_map/ppermute | solution.py:51
  760.7 12.2 %collective-permute-done.145 = bf16[256,1536]{1,0:T(8,128)(2,1)} collective-permute-done((bf16[256,1536]{1,0:T(8,128)(2,1)S(1)}, bf16[256,1536]{1,0:T(8,128)(2,1)}, u32[]{:S(2)}, u32[]{:S(2)}) %collective-permute-start.145) | collective-permute-done | bytes 786464 | tf_op jit(solution)/shard_map/ppermute | solution.py:51
  776.9 7.6 collective-permute-done.123
  795.2 11.9 %collective-permute-done.159 = bf16[32,2688]{1,0:T(8,128)(2,1)S(1)} collective-permute-done((bf16[32,2688]{1,0:T(8,128)(2,1)S(1)}, bf16[32,2688]{1,0:T(8,128)(2,1)S(1)}, u32[]{:S(2)}, u32[]{:S(2)}) %collective-permute-start.159) | collective-permute-done | bytes 172064 | tf_op jit(solution)/shard_map/ppermute | solution.py:51
  820.9 12.2 %collective-permute-done.155 = bf16[64,2688]{1,0:T(8,128)(2,1)S(1)} collective-permute-done((bf16[64,2688]{1,0:T(8,128)(2,1)S(1)}, bf16[64,2688]{1,0:T(8,128)(2,1)S(1)}, u32[]{:S(2)}, u32[]{:S(2)}) %collective-permute-start.155) | collective-permute-done | bytes 344096 | tf_op jit(solution)/shard_map/ppermute | solution.py:51
  (975 shorter events, 567.8 us)
Async XLA Ops:
  0.6 72.7 %collective-permute-start = (bf16[256,1024]{1,0:T(8,128)(2,1)}, bf16[256,1024]{1,0:T(8,128)(2,1)}, u32[]{:S(2)}, u32[]{:S(2)}) collective-permute-start(bf16[256,1024]{1,0:T(8,128)(2,1)} %bitcast.117), channel_id=1, source_target_pairs={{0,4},{1,5},{2,6},{3,7},{4,0},{5,1},{6,2},{7,3},{8,12},{9,13},{10,... | collective-permute-start | bytes 1572872 | tf_op jit(solution)/shard_map/ppermute | solution.py:51
  8.1 45.4 %collective-permute-start.3 = (bf16[256,3072]{1,0:T(8,128)(2,1)}, bf16[256,3072]{1,0:T(8,128)(2,1)}, u32[]{:S(2)}, u32[]{:S(2)}) collective-permute-start(bf16[256,3072]{1,0:T(8,128)(2,1)} %get-tuple-element.564.p0), channel_id=1, source_target_pairs={{0,1},{1,0},{2,3},{3,2},{4,5},{5,4},{6,7},{7,6},{8,9},{9,8},{10,11... | collective-permute-start | bytes 4718600 | tf_op jit(solution)/shard_map/ppermute | solution.py:51
  9.0 42.9 %collective-permute-start.4 = (bf16[128,3072]{1,0:T(8,128)(2,1)}, bf16[128,3072]{1,0:T(8,128)(2,1)S(1)}, u32[]{:S(2)}, u32[]{:S(2)}) collective-permute-start(bf16[128,3072]{1,0:T(8,128)(2,1)} %dynamic-slice_bitcast_fusion.1), channel_id=1, source_target_pairs={{0,2},{1,3},{2,0},{3,1},{4,6},{5,7},{6,4},{7,5},{8,10},{9,11},{10,... | collective-permute-start | bytes 2359304 | tf_op jit(solution)/shard_map/ppermute | solution.py:51
  13.5 59.9 %collective-permute-start.11 = (bf16[128,1024]{1,0:T(8,128)(2,1)}, bf16[128,1024]{1,0:T(8,128)(2,1)}, u32[]{:S(2)}, u32[]{:S(2)}) collective-permute-start(bf16[128,1024]{1,0:T(8,128)(2,1)} %dynamic-slice_bitcast_fusion.3), channel_id=1, source_target_pairs={{0,2},{1,3},{2,0},{3,1},{4,6},{5,7},{6,4},{7,5},{8,10},{9,11},{10,... | collective-permute-start | bytes 786440 | tf_op jit(solution)/shard_map/ppermute | solution.py:51
  100.5 34.6 %collective-permute-start.20 = (bf16[256,2688]{1,0:T(8,128)(2,1)S(1)}, bf16[256,2688]{1,0:T(8,128)(2,1)}, u32[]{:S(2)}, u32[]{:S(2)}) collective-permute-start(bf16[256,2688]{1,0:T(8,128)(2,1)S(1)} %copy-done.169), channel_id=1, source_target_pairs={{0,1},{1,0},{2,3},{3,2},{4,5},{5,4},{6,7},{7,6},{8,9},{9,8},{10,11... | collective-permute-start | bytes 4128776 | tf_op jit(solution)/shard_map/ppermute | solution.py:51
  163.6 61.1 %collective-permute-start.30 = (bf16[256,3072]{1,0:T(8,128)(2,1)}, bf16[256,3072]{1,0:T(8,128)(2,1)}, u32[]{:S(2)}, u32[]{:S(2)}) collective-permute-start(bf16[256,3072]{1,0:T(8,128)(2,1)} %get-tuple-element.283.p0), channel_id=1, source_target_pairs={{0,1},{1,0},{2,3},{3,2},{4,5},{5,4},{6,7},{7,6},{8,9},{9,8},{10,11... | collective-permute-start | bytes 4718600 | tf_op jit(solution)/shard_map/ppermute | solution.py:51
  164.4 39.9 %collective-permute-start.29 = (bf16[128,2688]{1,0:T(8,128)(2,1)}, bf16[128,2688]{1,0:T(8,128)(2,1)S(1)}, u32[]{:S(2)}, u32[]{:S(2)}) collective-permute-start(bf16[128,2688]{1,0:T(8,128)(2,1)} %collective-permute-done.27.p3), channel_id=1, source_target_pairs={{0,1},{1,0},{2,3},{3,2},{4,5},{5,4},{6,7},{7,6},{8,9},{9,8},{10,11... | collective-permute-start | bytes 2064392 | tf_op jit(solution)/shard_map/ppermute | solution.py:51
  180.5 39.9 %collective-permute-start.32 = (bf16[128,3072]{1,0:T(8,128)(2,1)}, bf16[128,3072]{1,0:T(8,128)(2,1)S(1)}, u32[]{:S(2)}, u32[]{:S(2)}) collective-permute-start(bf16[128,3072]{1,0:T(8,128)(2,1)} %collective-permute-done.31.p2), channel_id=1, source_target_pairs={{0,4},{1,5},{2,6},{3,7},{4,0},{5,1},{6,2},{7,3},{8,12},{9,13},{10,... | collective-permute-start | bytes 2359304 | tf_op jit(solution)/shard_map/ppermute | solution.py:51
  229.2 46.3 %collective-permute-start.53 = (bf16[128,2688]{1,0:T(8,128)(2,1)S(1)}, bf16[128,2688]{1,0:T(8,128)(2,1)}, u32[]{:S(2)}, u32[]{:S(2)}) collective-permute-start(bf16[128,2688]{1,0:T(8,128)(2,1)S(1)} %copy-done.182), channel_id=1, source_target_pairs={{0,2},{1,3},{2,0},{3,1},{4,6},{5,7},{6,4},{7,5},{8,10},{9,11},{10,... | collective-permute-start | bytes 2064392 | tf_op jit(solution)/shard_map/ppermute | solution.py:51
  239.9 35.6 %collective-permute-start.44 = (bf16[128,2688]{1,0:T(8,128)(2,1)S(1)}, bf16[128,2688]{1,0:T(8,128)(2,1)S(1)}, u32[]{:S(2)}, u32[]{:S(2)}) collective-permute-start(bf16[128,2688]{1,0:T(8,128)(2,1)S(1)} %collective-permute-done.43.p2), channel_id=1, source_target_pairs={{0,4},{1,5},{2,6},{3,7},{4,0},{5,1},{6,2},{7,3},{8,12},{9,13},{10,... | collective-permute-start | bytes 2064392 | tf_op jit(solution)/shard_map/ppermute | solution.py:51
  258.9 36.9 %collective-permute-start.42 = (bf16[256,2688]{1,0:T(8,128)(2,1)}, bf16[256,2688]{1,0:T(8,128)(2,1)}, u32[]{:S(2)}, u32[]{:S(2)}) collective-permute-start(bf16[256,2688]{1,0:T(8,128)(2,1)} %pad_maximum_fusion.2.p0), channel_id=1, source_target_pairs={{0,1},{1,0},{2,3},{3,2},{4,5},{5,4},{6,7},{7,6},{8,9},{9,8},{10,11... | collective-permute-start | bytes 4128776 | tf_op jit(solution)/shard_map/ppermute | solution.py:51
  276.4 61.9 %collective-permute-start.54 = (bf16[128,2688]{1,0:T(8,128)(2,1)}, bf16[128,2688]{1,0:T(8,128)(2,1)}, u32[]{:S(2)}, u32[]{:S(2)}) collective-permute-start(bf16[128,2688]{1,0:T(8,128)(2,1)} %collective-permute-done.53.p2), channel_id=1, source_target_pairs={{0,4},{1,5},{2,6},{3,7},{4,0},{5,1},{6,2},{7,3},{8,12},{9,13},{10,... | collective-permute-start | bytes 2064392 | tf_op jit(solution)/shard_map/ppermute | solution.py:51
  338.3 35.4 %collective-permute-start.56 = (bf16[128,2688]{1,0:T(8,128)(2,1)}, bf16[128,2688]{1,0:T(8,128)(2,1)}, u32[]{:S(2)}, u32[]{:S(2)}) collective-permute-start(bf16[128,2688]{1,0:T(8,128)(2,1)} %collective-permute-done.54.p3), channel_id=1, source_target_pairs={{0,1},{1,0},{2,3},{3,2},{4,5},{5,4},{6,7},{7,6},{8,9},{9,8},{10,11... | collective-permute-start | bytes 2064392 | tf_op jit(solution)/shard_map/ppermute | solution.py:51
  339.6 75.0 %collective-permute-start.82 = (bf16[512,256]{1,0:T(8,128)(2,1)}, bf16[512,256]{1,0:T(8,128)(2,1)}, u32[]{:S(2)}, u32[]{:S(2)}) collective-permute-start(bf16[512,256]{1,0:T(8,128)(2,1)} %get-tuple-element.375), channel_id=1, source_target_pairs={{0,1},{1,0},{2,3},{3,2},{4,5},{5,4},{6,7},{7,6},{8,9},{9,8},{10,11... | collective-permute-start | bytes 786440 | tf_op jit(solution)/shard_map/ppermute | solution.py:51
  414.3 61.3 %collective-permute-start.67 = (bf16[256,896]{1,0:T(8,128)(2,1)}, bf16[256,896]{1,0:T(8,128)(2,1)}, u32[]{:S(2)}, u32[]{:S(2)}) collective-permute-start(bf16[256,896]{1,0:T(8,128)(2,1)} %get-tuple-element.358.refs_2_), channel_id=1, source_target_pairs={{0,1},{1,0},{2,3},{3,2},{4,5},{5,4},{6,7},{7,6},{8,9},{9,8},{10,11... | collective-permute-start | bytes 1376264 | tf_op jit(solution)/shard_map/ppermute | solution.py:51
  414.6 61.2 %collective-permute-start.83 = (bf16[512,256]{1,0:T(8,128)(2,1)}, bf16[512,256]{1,0:T(8,128)(2,1)S(1)}, u32[]{:S(2)}, u32[]{:S(2)}) collective-permute-start(bf16[512,256]{1,0:T(8,128)(2,1)} %get-tuple-element.376), channel_id=1, source_target_pairs={{0,1},{1,0},{2,3},{3,2},{4,5},{5,4},{6,7},{7,6},{8,9},{9,8},{10,11... | collective-permute-start | bytes 786440 | tf_op jit(solution)/shard_map/ppermute | solution.py:51
  477.2 38.1 %collective-permute-start.57 = (bf16[256,1024]{1,0:T(8,128)(2,1)}, bf16[256,1024]{1,0:T(8,128)(2,1)}, u32[]{:S(2)}, u32[]{:S(2)}) collective-permute-start(bf16[256,1024]{1,0:T(8,128)(2,1)} %maximum_select_fusion.1), channel_id=1, source_target_pairs={{0,16},{1,17},{2,18},{3,19},{4,20},{5,21},{6,22},{7,23},{8,24},{9,... | collective-permute-start | bytes 1572872 | tf_op jit(solution)/shard_map/ppermute | solution.py:51
  554.6 34.0 %collective-permute-start.107 = (bf16[256,1792]{1,0:T(8,128)(2,1)S(1)}, bf16[256,1792]{1,0:T(8,128)(2,1)}, u32[]{:S(2)}, u32[]{:S(2)}) collective-permute-start(bf16[256,1792]{1,0:T(8,128)(2,1)S(1)} %get-tuple-element.425), channel_id=1, source_target_pairs={{0,2},{1,3},{2,0},{3,1},{4,6},{5,7},{6,4},{7,5},{8,10},{9,11},{10,... | collective-permute-start | bytes 2752520 | tf_op jit(solution)/shard_map/ppermute | solution.py:51
  561.8 73.2 %collective-permute-start.93 = (bf16[256,3072]{1,0:T(8,128)(2,1)S(1)}, bf16[256,3072]{1,0:T(8,128)(2,1)S(1)}, u32[]{:S(2)}, u32[]{:S(2)}) collective-permute-start(bf16[256,3072]{1,0:T(8,128)(2,1)S(1)} %copy-done.3), channel_id=1, source_target_pairs={{0,1},{1,0},{2,3},{3,2},{4,5},{5,4},{6,7},{7,6},{8,9},{9,8},{10,11... | collective-permute-start | bytes 4718600 | tf_op jit(solution)/shard_map/ppermute | solution.py:51
  591.8 34.5 %collective-permute-start.108 = (bf16[256,1792]{1,0:T(8,128)(2,1)S(1)}, bf16[256,1792]{1,0:T(8,128)(2,1)S(1)}, u32[]{:S(2)}, u32[]{:S(2)}) collective-permute-start(bf16[256,1792]{1,0:T(8,128)(2,1)S(1)} %get-tuple-element.426), channel_id=1, source_target_pairs={{0,2},{1,3},{2,0},{3,1},{4,6},{5,7},{6,4},{7,5},{8,10},{9,11},{10,... | collective-permute-start | bytes 2752520 | tf_op jit(solution)/shard_map/ppermute | solution.py:51
  669.8 68.7 %collective-permute-start.144 = (bf16[256,3072]{1,0:T(8,128)(2,1)S(1)}, bf16[256,3072]{1,0:T(8,128)(2,1)S(1)}, u32[]{:S(2)}, u32[]{:S(2)}) collective-permute-start(bf16[256,3072]{1,0:T(8,128)(2,1)S(1)} %copy-done.2), channel_id=1, source_target_pairs={{0,1},{1,0},{2,3},{3,2},{4,5},{5,4},{6,7},{7,6},{8,9},{9,8},{10,11... | collective-permute-start | bytes 4718600 | tf_op jit(solution)/shard_map/ppermute | solution.py:51
  671.1 53.8 %collective-permute-start.100 = (bf16[256,1792]{1,0:T(8,128)(2,1)}, bf16[256,1792]{1,0:T(8,128)(2,1)S(1)}, u32[]{:S(2)}, u32[]{:S(2)}) collective-permute-start(bf16[256,1792]{1,0:T(8,128)(2,1)} %get-tuple-element.408), channel_id=1, source_target_pairs={{0,2},{1,3},{2,0},{3,1},{4,6},{5,7},{6,4},{7,5},{8,10},{9,11},{10,... | collective-permute-start | bytes 2752520 | tf_op jit(solution)/shard_map/ppermute | solution.py:51
  748.7 35.8 %collective-permute-start.150 = (bf16[256,1536]{1,0:T(8,128)(2,1)S(1)}, bf16[256,1536]{1,0:T(8,128)(2,1)S(1)}, u32[]{:S(2)}, u32[]{:S(2)}) collective-permute-start(bf16[256,1536]{1,0:T(8,128)(2,1)S(1)} %get-tuple-element.488), channel_id=1, source_target_pairs={{0,4},{1,5},{2,6},{3,7},{4,0},{5,1},{6,2},{7,3},{8,12},{9,13},{10,... | collective-permute-start | bytes 2359304 | tf_op jit(solution)/shard_map/ppermute | solution.py:51
  758.5 35.2 %collective-permute-start.136 = (bf16[256,1792]{1,0:T(8,128)(2,1)S(1)}, bf16[256,1792]{1,0:T(8,128)(2,1)S(1)}, u32[]{:S(2)}, u32[]{:S(2)}) collective-permute-start(bf16[256,1792]{1,0:T(8,128)(2,1)S(1)} %copy-done.165), channel_id=1, source_target_pairs={{0,2},{1,3},{2,0},{3,1},{4,6},{5,7},{6,4},{7,5},{8,10},{9,11},{10,... | collective-permute-start | bytes 2752520 | tf_op jit(solution)/shard_map/ppermute | solution.py:51
  (351 other events, 4940.9 us)

commit v3 on v2

v3 whole, which is shorter than its diff:
```python
import functools
import math

import jax
import jax.numpy as jnp
from jax import lax
from jax.experimental import pallas as pl
from jax.experimental.pallas import tpu as pltpu
from jax.sharding import PartitionSpec as P

HEADS = 16
HEAD_DIM = 64
FF = 2624
WINDOW = 128
BLOCK = 128
BLK_DEV = 2
LAYERS = 2

NEG = -1e30
EPS = 1e-05
THETA = 10000.0

AXES = ("seq", "fsdp")
LANES = 128
HALO = WINDOW // 2
SPLIT = (5, 8, 8)
FF_PAD = sum(SPLIT) * LANES
WIDTHS = tuple(blocks * LANES for blocks in SPLIT)
STARTS = tuple(sum(WIDTHS[:k]) for k in range(len(WIDTHS)))
CHUNKS = len(SPLIT)
TILES = 3
F32 = jnp.float32
BF16 = jnp.bfloat16
VMEM_LIMIT = 60 * 1024 * 1024
NT = (((1,), (1,)), ((), ()))
TN = (((0,), (0,)), ((), ()))


class Phases:
    def __init__(self):
        self.gate = ()
        self.made = []

    def next(self):
        self.gate = tuple(self.made)
        self.made = []

    def tie(self, value):
        return lax.optimization_barrier((value,) + self.gate)[0] if self.gate else value

    def keep(self, *values):
        self.made += values

    def route(self, value, axes, pairs):
        result = lax.ppermute(self.tie(value), axes, pairs)
        self.made.append(result)
        return result

    def swap(self, value, bit):
        count = lax.axis_size("seq") * lax.axis_size("fsdp")
        return self.route(value, AXES, [(i, i ^ (1 << bit)) for i in range(count)])

    def shift(self, value, up):
        pairs = [(i, i + 1) for i in range(lax.axis_size("seq") - 1)]
        if not up:
            pairs = [(b, a) for a, b in pairs]
        return self.route(value, "seq", pairs)


def flat_index():
    return lax.axis_index("seq") * lax.axis_size("fsdp") + lax.axis_index("fsdp")


class Weights:
    def __init__(self, flow, shard, sent):
        self.flow = flow
        self.shard = shard
        self.sent = sent

    def own(self):
        self.own_core = self.flow.swap(self.shard, 0)

    def over_x(self):
        self.far_x = self.flow.swap(self.sent, 1)

    def over_y(self):
        self.far_y = self.flow.swap(self.far_x, 2)

    def over_core(self):
        far = jnp.concatenate([self.far_x, self.flow.tie(self.far_y)], axis=0)
        self.pieces = (self.shard, far, self.own_core, self.flow.swap(far, 0))


def piece_order():
    quarter = lax.axis_index("fsdp")
    side = lax.axis_index("seq") % 2
    one = 1 - side
    order = []
    for core in (quarter, quarter ^ 1):
        order += [core * 2, core * 2 + 1, (core ^ 2) * 2 + side, (core ^ 2) * 2 + one]
    return jnp.stack(order).astype(jnp.int32)


def stage_bits(first_x):
    levels = lax.axis_size("seq").bit_length() - 1
    rest = [2 + level for level in range(1, levels)]
    return ([1, 2] if first_x else [2, 1]) + rest


def row_order(features, bits):
    order = [0] + bits
    per_device = features >> len(order)
    rows = jnp.arange(features, dtype=jnp.int32)
    place = rows // per_device
    owner = flat_index()
    for step, bit in enumerate(order):
        taken = (place >> (len(order) - 1 - step)) & 1
        owner = owner ^ (taken << bit)
    return owner * per_device + rows % per_device


def row_picker(features, bits):
    order = row_order(features, bits)
    grid = jnp.arange(features, dtype=jnp.int32)
    return (order[:, None] == grid[None, :]).astype(BF16)


def call(kernel, outs, scratch=(), smem=1, grid=None, in_specs=None, out_specs=None):
    params = dict(
        compiler_params=pltpu.CompilerParams(vmem_limit_bytes=VMEM_LIMIT),
        out_shape=outs,
        scratch_shapes=list(scratch),
        cost_estimate=pl.CostEstimate(
            flops=0, bytes_accessed=0, transcendentals=0
        ),
    )
    if grid is not None:
        params["grid"] = grid

    def run(*args):
        specs = in_specs
        if specs is None:
            specs = [pl.BlockSpec(memory_space=pltpu.SMEM)] * smem
            specs += [pl.BlockSpec(memory_space=pltpu.VMEM)] * (len(args) - smem)
        results = out_specs
        if results is None:
            results = jax.tree.map(lambda _: pl.BlockSpec(memory_space=pltpu.VMEM), outs)
        return pl.pallas_call(kernel, in_specs=specs, out_specs=results, **params)(*args)

    return run


def struct(shape, dtype):
    return jax.ShapeDtypeStruct(shape, dtype)


def to_pieces(offs, source, target):
    for k in range(source.shape[1] // LANES):
        start = pl.multiple_of(offs[k] * LANES, LANES)
        target[:, k * LANES : (k + 1) * LANES] = source[:, pl.ds(start, LANES)]


def from_pieces(offs, source, target):
    for k in range(source.shape[1] // LANES):
        start = pl.multiple_of(offs[k] * LANES, LANES)
        target[:, pl.ds(start, LANES)] = source[:, k * LANES : (k + 1) * LANES]


def joined(pieces, columns=slice(None)):
    return jnp.concatenate([piece[:, columns] for piece in pieces], axis=0)


def statistics(values):
    average = jnp.mean(values, axis=-1, keepdims=True)
    centred = values - average
    spread = jnp.mean(centred * centred, axis=-1, keepdims=True)
    rho = lax.rsqrt(spread + EPS)
    return centred, rho


def norm_pull(values, gain, grad):
    centred, rho = statistics(values)
    unit = centred * rho
    scaled = grad * gain
    mean_a = jnp.mean(scaled, axis=-1, keepdims=True)
    mean_b = jnp.mean(scaled * unit, axis=-1, keepdims=True)
    return rho * (scaled - mean_a - unit * mean_b), jnp.sum(grad * unit, axis=0, keepdims=True)


def turn_chunk(values, cosine, sine, sign):
    lane = lax.broadcasted_iota(jnp.int32, values.shape, 1)
    ahead = pltpu.roll(values, LANES - HEAD_DIM // 2, 1)
    behind = pltpu.roll(values, HEAD_DIM // 2, 1)
    turned = jnp.where(lane % HEAD_DIM < HEAD_DIM // 2, ahead, behind)
    if sign > 0:
        return values * cosine + turned * sine
    return values * cosine - turned * sine


def pack_one_kernel(side, first, own, sent):
    half = first.shape[1] // 2
    own[...] = first[0]
    sent[...] = first[0, pl.ds(pl.multiple_of(side[0] * half, half), half), :]


def pack_kernel(side, second, wide, narrow, *outs):
    half = wide.shape[1] // 2
    features = second.shape[2]
    outs[0][:, :features] = second[0]
    for chunk in range(CHUNKS):
        own = outs[2 * chunk]
        at = features if chunk == 0 else 0
        width = WIDTHS[chunk]
        start, stop = STARTS[chunk], min(STARTS[chunk] + width, FF)
        for array, base in ((narrow, 0), (wide, 0), (wide, FF)):
            if stop - start < width:
                own[:, at + width - LANES : at + width] = jnp.zeros((2 * half, LANES), BF16)
            own[:, at : at + stop - start] = array[0, :, base + start : base + stop]
            at += width
    for k in range(0, len(outs), 2):
        outs[k + 1][...] = outs[k][pl.ds(pl.multiple_of(side[0] * half, half), half), :]


def run_pack(side, arrays, layer):
    rows = arrays[0].shape[1]
    one = len(arrays) == 1
    features = arrays[0].shape[2]
    columns = [features + 3 * WIDTHS[0]] + [3 * width for width in WIDTHS[1:]]
    if one:
        columns = [features]
    outs = tuple(struct((height, width), BF16) for width in columns for height in (rows, rows // 2))
    flat = call(
        pack_one_kernel if one else pack_kernel,
        outs,
        grid=(1,),
        in_specs=[pl.BlockSpec(memory_space=pltpu.SMEM)]
        + [pl.BlockSpec((1,) + v.shape[1:], lambda j: (layer, 0, 0)) for v in arrays],
        out_specs=tuple(whole_spec(out.shape) for out in outs),
    )(side, *arrays)
    return [flat[k : k + 2] for k in range(0, len(flat), 2)]


def qkv_kernel(offs, x, gain, cosine, sine, p0, p1, p2, p3, out, normed, first, last, placed):
    step = pl.program_id(0)
    tokens = x.shape[0]

    @pl.when(step == 0)
    def _():
        centred, rho = statistics(x[...])
        normed[...] = (centred * rho * gain[...]).astype(BF16)
        to_pieces(offs, normed, placed)

    product = jnp.dot(
        placed[...], joined((p0, p1, p2, p3)), preferred_element_type=F32
    )

    @pl.when(step < 2)
    def _():
        for k in range(product.shape[1] // LANES):
            part = slice(k * LANES, (k + 1) * LANES)
            out[:, part] = turn_chunk(product[:, part], cosine[...], sine[...], 1).astype(BF16)

    @pl.when(step == 2)
    def _():
        out[...] = product.astype(BF16)

    first[...] = out[:HALO, :]
    last[...] = out[tokens - HALO :, :]


def piece_specs(rows, columns):
    return [pl.BlockSpec((rows, columns), lambda j: (0, j))] * 4


def proj_specs(rows, columns):
    return [pl.BlockSpec((rows, columns), lambda j: (0, 0))] * 4


def whole_spec(shape):
    return pl.BlockSpec(shape, lambda j: tuple(0 for _ in shape))


def run_qkv(offs, x, gain, cosine, sine, pieces):
    tokens, features = x.shape
    return call(
        qkv_kernel,
        (
            struct((tokens, 3 * features), BF16),
            struct((tokens, features), BF16),
            struct((HALO, 2 * features), BF16),
            struct((HALO, 2 * features), BF16),
        ),
        [pltpu.VMEM((tokens, features), BF16)],
        grid=(3,),
        in_specs=[pl.BlockSpec(memory_space=pltpu.SMEM)]
        + [whole_spec(v.shape) for v in (x, gain, cosine, sine)]
        + piece_specs(pieces[0].shape[0], features),
        out_specs=(
            pl.BlockSpec((tokens, features), lambda j: (0, j)),
            whole_spec((tokens, features)),
            pl.BlockSpec((HALO, features), lambda j: (0, jnp.maximum(j - 1, 0))),
            pl.BlockSpec((HALO, features), lambda j: (0, jnp.maximum(j - 1, 0))),
        ),
    )(offs, x, gain, cosine, sine, *pieces)


def extend(qkv, before, after, extended):
    tokens, features = qkv.shape[0], qkv.shape[1] // 3
    extended[:HALO, :] = before[...]
    extended[HALO : HALO + tokens, :] = qkv[:, features:]
    extended[HALO + tokens :, :] = after[...]


def attend_kernel(
    offs, qkv, before, after, seg_q, seg_k, x, gain,
    p0, p1, p2, p3, mixed, middle, second, extended, placed,
):
    tokens, features = x.shape
    extend(qkv, before, after, extended)
    scale = 1.0 / math.sqrt(HEAD_DIM)
    span = BLOCK + 2 * HALO
    row = lax.broadcasted_iota(jnp.int32, (BLOCK, span), 0)
    col = lax.broadcasted_iota(jnp.int32, (BLOCK, span), 1)
    near = (col >= row) & (col - row <= 2 * HALO)
    low = lax.broadcasted_iota(jnp.int32, (BLOCK, LANES), 1) < HEAD_DIM
    bias = []
    for block in range(tokens // BLOCK):
        base = block * BLOCK
        same = seg_q[base : base + BLOCK, :] == seg_k[:, base : base + span]
        bias.append(jnp.where(near & same, 0.0, NEG))

    def pair(index, carry):
        lanes = pl.ds(pl.multiple_of(index * LANES, LANES), LANES)
        value_lanes = pl.ds(pl.multiple_of(features + index * LANES, LANES), LANES)
        for block in range(tokens // BLOCK):
            base = block * BLOCK
            queries = qkv[base : base + BLOCK, lanes]
            keys = extended[base : base + span, lanes]
            values = extended[base : base + span, value_lanes]
            parts = []
            for keep in (low, ~low):
                chosen = jnp.where(keep, queries, jnp.zeros_like(queries))
                raw = lax.dot_general(chosen, keys, NT, preferred_element_type=F32)
                scores = raw * scale + bias[block]
                expo = jnp.exp(scores - jnp.max(scores, axis=-1, keepdims=True))
                probs = expo * (1.0 / jnp.sum(expo, axis=-1, keepdims=True))
                parts.append(jnp.dot(probs.astype(BF16), values, preferred_element_type=F32))
            mixed[base : base + BLOCK, lanes] = jnp.where(low, parts[0], parts[1]).astype(BF16)
        return carry

    lax.fori_loop(0, features // LANES, pair, 0)
    to_pieces(offs, mixed, placed)
    total = x[...] + jnp.dot(
        placed[...], joined((p0, p1, p2, p3)), preferred_element_type=F32
    )
    middle[...] = total
    centred, rho = statistics(total)
    second[...] = (centred * rho * gain[...]).astype(BF16)


def run_attend(offs, qkv, before, after, seg_q, seg_k, x, gain, pieces):
    tokens, features = x.shape
    return call(
        attend_kernel,
        (
            struct((tokens, features), BF16),
            struct((tokens, features), F32),
            struct((tokens, features), BF16),
        ),
        [
            pltpu.VMEM((tokens + 2 * HALO, 2 * features), BF16),
            pltpu.VMEM((tokens, features), BF16),
        ],
        grid=(1,),
        in_specs=[pl.BlockSpec(memory_space=pltpu.SMEM)]
        + [whole_spec(v.shape) for v in (qkv, before, after, seg_q, seg_k, x, gain)]
        + proj_specs(pieces[0].shape[0], features),
        out_specs=(whole_spec((tokens, features)),) * 3,
    )(offs, qkv, before, after, seg_q, seg_k, x, gain, *pieces)


def chunk_parts(pieces, base, width):
    return [
        joined(pieces, slice(base + k * width, base + (k + 1) * width)) for k in range(3)
    ]


def mlp_kernel(
    base, width, offs, second, carried, p0, p1, p2, p3, total, gated, slope, gate, placed, part
):
    output, first, other = chunk_parts((p0, p1, p2, p3), base, width)
    to_pieces(offs, second, placed)
    source = placed[...]
    hidden = jnp.dot(source, first, preferred_element_type=F32)
    factor = jnp.dot(source, other, preferred_element_type=F32)
    normal = 0.5 * (1.0 + lax.erf(hidden * math.sqrt(0.5)))
    density = jnp.exp(-0.5 * hidden * hidden) * (1.0 / math.sqrt(2.0 * math.pi))
    active = hidden * normal
    product = (active * factor).astype(BF16)
    gated[...] = product
    slope[...] = ((normal + hidden * density) * factor).astype(BF16)
    gate[...] = active.astype(BF16)
    part[...] = lax.dot_general(product, output, NT, preferred_element_type=F32)
    for k in range(part.shape[1] // LANES):
        lanes = pl.ds(pl.multiple_of(offs[k] * LANES, LANES), LANES)
        total[:, lanes] = carried[:, lanes] + part[:, k * LANES : (k + 1) * LANES]


def run_mlp(offs, second, carried, pieces, chunk):
    tokens, features = second.shape
    width = WIDTHS[chunk]
    base = pieces[0].shape[1] - 3 * width
    hidden = struct((tokens, width), BF16)
    return call(
        functools.partial(mlp_kernel, base, width),
        (struct((tokens, features), F32), hidden, hidden, hidden),
        [pltpu.VMEM((tokens, features), BF16), pltpu.VMEM((tokens, features), F32)],
    )(offs, second, carried, *pieces)


def mlp_pull(base, width, offs, upstream, gated, slope, gate, pieces, right, placed):
    output, first, other = chunk_parts(pieces, base, width)
    to_pieces(offs, upstream, placed)
    gated_grad = jnp.dot(placed[...], output, preferred_element_type=F32)
    input_grad = (slope[...].astype(F32) * gated_grad).astype(BF16)
    gate_grad = (gate[...].astype(F32) * gated_grad).astype(BF16)
    store(right, 0, gated[...])
    store(right, width, input_grad)
    store(right, 2 * width, gate_grad)
    return lax.dot_general(input_grad, first, NT, preferred_element_type=F32) + lax.dot_general(
        gate_grad, other, NT, preferred_element_type=F32
    )


def store(target, at, value):
    target[:, at : at + value.shape[1]] = value


def mlp_back_kernel(
    base, width, first, offs, upstream, gated, slope, gate, carried, p0, p1, p2, p3,
    total, right, placed,
):
    part = mlp_pull(
        base, width, offs, upstream, gated, slope, gate, (p0, p1, p2, p3), right, placed
    )
    total[...] = part if first else carried[...] + part


def mlp_back_last_kernel(
    base, width, offs, upstream, gated, slope, gate, carried, residual_grad, middle, gain,
    p0, p1, p2, p3, middle_grad, middle_grad_b, gain_grad, right, placed, sums, ordered,
):
    part = mlp_pull(
        base, width, offs, upstream, gated, slope, gate, (p0, p1, p2, p3), right, placed
    )
    sums[...] = carried[...] + part
    from_pieces(offs, sums, ordered)
    pulled, gains = norm_pull(middle[...], gain[...], ordered[...])
    result = residual_grad[...] + pulled
    middle_grad[...] = result
    middle_grad_b[...] = result.astype(BF16)
    gain_grad[...] = gains
    at = 3 * width
    store(right, at, result.astype(BF16))
    at += result.shape[1]
    rest = right.shape[1] - at
    if rest:
        store(right, at, jnp.zeros((result.shape[0], rest), BF16))


def run_mlp_back(offs, upstream, hidden, carried, pieces, chunk):
    tokens, features = upstream.shape
    width = WIDTHS[chunk]
    base = pieces[0].shape[1] - 3 * width
    right = struct((tokens, 3 * features), BF16)
    first = carried is None
    if first:
        carried = jnp.zeros((8, LANES), F32)
    return call(
        functools.partial(mlp_back_kernel, base, width, first),
        (struct((tokens, features), F32), right),
        [pltpu.VMEM((tokens, features), BF16)],
    )(offs, upstream, *hidden, carried, *pieces)


def run_mlp_back_last(offs, upstream, hidden, carried, residual_grad, middle, gain, pieces, chunk):
    tokens, features = upstream.shape
    width = WIDTHS[chunk]
    base = pieces[0].shape[1] - 3 * width
    right = struct((tokens, 3 * features), BF16)
    return call(
        functools.partial(mlp_back_last_kernel, base, width),
        (
            struct((tokens, features), F32),
            struct((tokens, features), BF16),
            struct((1, features), F32),
            right,
        ),
        [
            pltpu.VMEM((tokens, features), BF16),
            pltpu.VMEM((tokens, features), F32),
            pltpu.VMEM((tokens, features), F32),
        ],
    )(offs, upstream, *hidden, carried, residual_grad, middle, gain, *pieces)


def attend_back_kernel(
    offs, middle_grad, qkv, before, after, seg_q, seg_k, cosine, sine, p0, p1, p2, p3,
    query_grad, own_grad, rim_before, rim_after, extended, mixed_grad, extended_grad,
):
    tokens, features = middle_grad.shape
    extend(qkv, before, after, extended)
    placed = lax.dot_general(
        middle_grad[...], joined((p0, p1, p2, p3)), NT, preferred_element_type=F32
    ).astype(BF16)
    for k in range(features // LANES):
        lanes = pl.ds(pl.multiple_of(offs[k] * LANES, LANES), LANES)
        mixed_grad[:, lanes] = placed[:, k * LANES : (k + 1) * LANES]
    scale = 1.0 / math.sqrt(HEAD_DIM)
    span = BLOCK + 2 * HALO
    row = lax.broadcasted_iota(jnp.int32, (span, BLOCK), 1)
    col = lax.broadcasted_iota(jnp.int32, (span, BLOCK), 0)
    near = (col >= row) & (col - row <= 2 * HALO)
    low = lax.broadcasted_iota(jnp.int32, (BLOCK, LANES), 1) < HEAD_DIM
    bias = []
    for block in range(tokens // BLOCK):
        base = block * BLOCK
        same = seg_q[:, base : base + BLOCK] == seg_k[base : base + span, :]
        bias.append(jnp.where(near & same, 0.0, NEG))

    def pair(index, carry):
        lanes = pl.ds(pl.multiple_of(index * LANES, LANES), LANES)
        value_lanes = pl.ds(pl.multiple_of(features + index * LANES, LANES), LANES)
        key_sums = []
        value_sums = []
        for block in range(tokens // BLOCK):
            base = block * BLOCK
            here = slice(base, base + BLOCK)
            queries = qkv[here, lanes]
            grads = mixed_grad[here, lanes]
            keys = extended[base : base + span, lanes]
            values = extended[base : base + span, value_lanes]
            key_sum = None
            value_sum = None
            query_parts = []
            for keep in (low, ~low):
                chosen = jnp.where(keep, queries, jnp.zeros_like(queries))
                chosen_grad = jnp.where(keep, grads, jnp.zeros_like(grads))
                raw = lax.dot_general(keys, chosen, NT, preferred_element_type=F32)
                scores = raw * scale + bias[block]
                expo = jnp.exp(scores - jnp.max(scores, axis=0, keepdims=True))
                probs = expo * (1.0 / jnp.sum(expo, axis=0, keepdims=True))
                prob_grad = lax.dot_general(values, chosen_grad, NT, preferred_element_type=F32)
                delta = jnp.sum(prob_grad * probs, axis=0, keepdims=True)
                score_grad = (probs * (prob_grad - delta) * scale).astype(BF16)
                query_parts.append(
                    lax.dot_general(score_grad, keys, TN, preferred_element_type=F32)
                )
                to_keys = jnp.dot(score_grad, chosen, preferred_element_type=F32)
                to_values = jnp.dot(
                    probs.astype(BF16), chosen_grad, preferred_element_type=F32
                )
                key_sum = to_keys if key_sum is None else key_sum + to_keys
                value_sum = to_values if value_sum is None else value_sum + to_values
            joint = jnp.where(low, query_parts[0], query_parts[1])
            query_grad[here, lanes] = turn_chunk(
                joint, cosine[here, :], sine[here, :], -1
            ).astype(BF16)
            key_sums.append(key_sum)
            value_sums.append(value_sum)
        for sums, place in ((key_sums, lanes), (value_sums, value_lanes)):
            over = 2 * HALO
            extended_grad[:BLOCK, place] = sums[0][:BLOCK]
            extended_grad[BLOCK : BLOCK + over, place] = sums[0][BLOCK:] + sums[1][:over]
            extended_grad[BLOCK + over :, place] = sums[1][over:]
        return carry

    lax.fori_loop(0, features // LANES, pair, 0)
    rim_before[...] = extended_grad[:HALO, :].astype(BF16)
    own_grad[...] = extended_grad[HALO : HALO + tokens, :]
    rim_after[...] = extended_grad[HALO + tokens :, :].astype(BF16)


def run_attend_back(offs, middle_grad, qkv, before, after, seg_q, seg_k, cosine, sine, pieces):
    tokens, features = middle_grad.shape
    rim = struct((HALO, 2 * features), BF16)
    return call(
        attend_back_kernel,
        (struct((tokens, features), BF16), struct((tokens, 2 * features), F32), rim, rim),
        [
            pltpu.VMEM((tokens + 2 * HALO, 2 * features), BF16),
            pltpu.VMEM((tokens, features), BF16),
            pltpu.VMEM((tokens + 2 * HALO, 2 * features), F32),
        ],
        grid=(1,),
        in_specs=[pl.BlockSpec(memory_space=pltpu.SMEM)]
        + [
            whole_spec(v.shape)
            for v in (middle_grad, qkv, before, after, seg_q, seg_k, cosine, sine)
        ]
        + proj_specs(pieces[0].shape[0], features),
        out_specs=(
            whole_spec((tokens, features)),
            whole_spec((tokens, 2 * features)),
            whole_spec((HALO, 2 * features)),
            whole_spec((HALO, 2 * features)),
        ),
    )(offs, middle_grad, qkv, before, after, seg_q, seg_k, cosine, sine, *pieces)


def qkv_back_kernel(
    offs, query_grad, own_grad, arrived_first, arrived_last, cosine, sine, x, gain, middle_grad,
    p0, p1, p2, p3, right, upstream, upstream_b, gain_grad, sums, ordered,
):
    step = pl.program_id(0)
    tokens, features = x.shape
    for part in range(3):

        @pl.when(step == part)
        def _():
            if part == 0:
                joint = query_grad[...]
            else:
                chunks = []
                for k in range(features // LANES):
                    at = (part - 1) * features + k * LANES
                    there = slice(at, at + LANES)
                    rows = [
                        own_grad[:HALO, there] + arrived_first[:, there].astype(F32),
                        own_grad[HALO : tokens - HALO, there],
                        own_grad[tokens - HALO :, there] + arrived_last[:, there].astype(F32),
                    ]
                    grads = jnp.concatenate(rows, axis=0)
                    if part == 1:
                        grads = turn_chunk(grads, cosine[...], sine[...], -1)
                    chunks.append(grads.astype(BF16))
                joint = jnp.concatenate(chunks, axis=1)
            store(right, part * features, joint)
            product = lax.dot_general(
                joint, joined((p0, p1, p2, p3)), NT, preferred_element_type=F32
            )
            sums[...] = product if part == 0 else sums[...] + product

    @pl.when(step == 2)
    def _():
        from_pieces(offs, sums, ordered)
        pulled, gains = norm_pull(x[...], gain[...], ordered[...])
        result = middle_grad[...] + pulled
        upstream[...] = result
        upstream_b[...] = result.astype(BF16)
        gain_grad[...] = gains


def run_qkv_back(
    offs, query_grad, own_grad, arrived_first, arrived_last, cosine, sine, x, gain, middle_grad, pieces
):
    tokens, features = x.shape
    whole = (query_grad, own_grad, arrived_first, arrived_last, cosine, sine, x, gain, middle_grad)
    outs = (
        struct((tokens, 3 * features), BF16),
        struct((tokens, features), F32),
        struct((tokens, features), BF16),
        struct((1, features), F32),
    )
    return call(
        qkv_back_kernel,
        outs,
        [pltpu.VMEM((tokens, features), F32), pltpu.VMEM((tokens, features), F32)],
        grid=(3,),
        in_specs=[pl.BlockSpec(memory_space=pltpu.SMEM)]
        + [whole_spec(v.shape) for v in whole]
        + piece_specs(pieces[0].shape[0], features),
        out_specs=tuple(whole_spec(out.shape) for out in outs),
    )(offs, *whole, *pieces)


def pick_kernel(which, *refs):
    pickers, lefts, (mine, theirs) = refs[:2], refs[2:-2], refs[-2:]
    half = pickers[0].shape[0] // 2
    for k, (picker, left) in enumerate(which):
        rows = lax.dot_general(
            pickers[picker][...], lefts[left][...], NT, preferred_element_type=F32
        ).astype(BF16)
        mine[k * half : (k + 1) * half, :] = rows[:half]
        theirs[k * half : (k + 1) * half, :] = rows[half:]


def run_pick(pickers, lefts, which):
    rows = len(which) * pickers[0].shape[0] // 2
    out = struct((rows, lefts[0].shape[0]), BF16)
    return call(functools.partial(pick_kernel, which), (out, out), smem=0)(*pickers, *lefts)


def exchange_kernel(plan, *refs):
    segments, stages = plan
    refs = list(refs)
    take = lambda count: [refs.pop(0) for _ in range(count)]
    adding, ending, far_ending, finishing = stages
    if segments:
        rights, rights_far = take(2), take(2)
        lefts = [take(2) for _ in segments]
    kept = take(2) if adding else None
    last = take(2) if ending else None
    come = take(2) if adding or ending else None
    near_pair = take(2) if far_ending else None
    far_pair = take(2) if finishing else None
    keep = take(2) if segments else None
    stay = take(2) if adding else None
    send = take(2) if segments or adding else None
    near_out = take(2) if ending else None
    far_out = take(2) if far_ending else None
    result = take(1)[0] if finishing else None

    def added(pair, rows, columns):
        return pair[0][rows, columns].astype(F32) + pair[1][rows, columns].astype(F32)

    def body(step):
        everything = slice(None)
        top = 0
        if segments:
            half, tile = keep[0].shape
            for (path, start, stop), (left, left_far) in zip(segments, lefts):
                low, high = max(start - step * tile, 0), min(stop - step * tile, tile)
                if low >= high:
                    continue
                columns = slice(low, high)
                total = jnp.dot(
                    jnp.concatenate([left[...], left_far[...]], axis=1),
                    jnp.concatenate(
                        [rights[path][:, columns], rights_far[path][:, columns]], axis=0
                    ),
                    preferred_element_type=F32,
                ).astype(BF16)
                keep[path][:, columns] = total[:half]
                send[path][:half, columns] = total[half:]
            top = half
        came = 0
        if adding:
            rows, tile = kept[0].shape
            half = rows // 2
            for path in range(2):
                total = kept[path][...].astype(F32) + come[path][:rows, :].astype(F32)
                stay[path][...] = total[:half].astype(BF16)
                send[1 - path][top : top + half, :] = total[half:].astype(BF16)
            came = rows
        if ending:
            rows, tile = last[0].shape
            half = rows // 2
            for path in range(2):
                at = (path * TILES + step) * tile
                total = last[path][...].astype(F32) + come[1 - path][
                    came : came + rows, :
                ].astype(F32)
                near_out[0][:, at : at + tile] = total[:half].astype(BF16)
                near_out[1][:, at : at + tile] = total[half:].astype(BF16)
        if step == 0 and far_ending:
            half = near_pair[0].shape[0] // 2
            far_out[0][...] = added(near_pair, slice(0, half), everything).astype(BF16)
            far_out[1][...] = added(near_pair, slice(half, 2 * half), everything).astype(BF16)
        if step == 0 and finishing:
            result[...] = added(far_pair, everything, everything).astype(result.dtype)

    for step in range(TILES):
        pl.when(pl.program_id(0) == step)(functools.partial(body, step))


class Exchange:
    def __init__(self, flow, rows, width, bits):
        self.flow = flow
        self.rows = rows
        self.width = width
        self.near, self.far = bits[:2]
        self.dtype = F32 if len(bits) == 2 else BF16
        self.kept = self.last = self.come = self.near_pair = self.far_pair = None

    def busy(self):
        return any((self.kept, self.last, self.near_pair, self.far_pair))

    def step(self, rights=None, segments=()):
        flow, rows, width = self.flow, self.rows, self.width
        tile = width // TILES
        args, specs, outs, out_specs = [], [], [], []

        def tiled(shape):
            return pl.BlockSpec((shape[0], tile), lambda j: (0, j))

        def give(pair, spec):
            if pair:
                args.extend(pair)
                specs.extend(spec(value.shape) for value in pair)

        def want(height, columns, spec, count=2, dtype=BF16):
            outs.extend([struct((height, columns), dtype)] * count)
            out_specs.extend([spec((height, columns))] * count)

        for right in rights or ():
            args += [right, right]
            block = (right.shape[0], tile)
            specs += [pl.BlockSpec(block, lambda j: (0, j))]
            specs += [pl.BlockSpec(block, lambda j: (0, TILES + j))]
        for _, _, _, left, place in segments:
            args += left
            specs += [pl.BlockSpec((rows, left[0].shape[1]), lambda j, at=place: (at, 0))] * 2
        give(self.kept, tiled)
        give(self.last, tiled)
        give(self.come if self.kept or self.last else None, tiled)
        give(self.near_pair, whole_spec)
        give(self.far_pair, whole_spec)
        height = 0
        if segments:
            want(rows // 2, width, tiled)
            height += rows // 2
        if self.kept:
            want(rows // 4, width, tiled)
            height += rows // 4
        if height:
            want(height, width, tiled)
        if self.last:
            want(rows // 8, 2 * width, whole_spec)
        if self.near_pair:
            want(rows // 16, 2 * width, whole_spec)
        if self.far_pair:
            want(rows // 16, 2 * width, whole_spec, 1, self.dtype)
        stages = tuple(map(bool, (self.kept, self.last, self.near_pair, self.far_pair)))
        plan = (
            tuple((path, start - path * width, stop - path * width) for path, start, stop, _, _ in segments),
            stages,
        )
        args[0] = flow.tie(args[0])
        results = list(
            call(
                functools.partial(exchange_kernel, plan),
                tuple(outs),
                grid=(TILES,),
                in_specs=specs,
                out_specs=tuple(out_specs),
            )(*args)
        )

        def got(wanted):
            return [results.pop(0), results.pop(0)] if wanted else None

        keep, stay, send = got(segments), got(self.kept), got(height)
        near, far = got(self.last), got(self.near_pair)
        result = results.pop(0) if self.far_pair else None
        self.kept, self.last = keep, stay
        self.come = send and [flow.swap(value, 1 + path) for path, value in enumerate(send)]
        self.near_pair = near and [near[0], flow.swap(near[1], self.near)]
        self.far_pair = far and [far[0], flow.swap(far[1], self.far)]
        return result


class Ending:
    def __init__(self, flow, value, bits, deliver):
        self.flow = flow
        self.bits = list(bits)
        self.deliver = deliver
        self.keep = value
        self.come = None

    def step(self):
        if self.come is not None:
            self.keep = self.keep.astype(F32) + self.flow.tie(self.come).astype(F32)
        if not self.bits:
            self.deliver(self.keep)
            return False
        half = self.keep.shape[0] // 2
        send = self.keep[half:].astype(BF16)
        self.keep = self.keep[:half].astype(BF16)
        self.come = self.flow.swap(send, self.bits.pop(0))
        return True


def rope_tables(position):
    inverse = jnp.power(THETA, -jnp.arange(0, HEAD_DIM, 2, dtype=F32) / HEAD_DIM)
    angles = position[:, None] * inverse[None, :]
    cosine, sine = jnp.cos(angles), jnp.sin(angles)
    return (
        jnp.concatenate([cosine, cosine, cosine, cosine], axis=-1),
        jnp.concatenate([-sine, sine, -sine, sine], axis=-1),
    )


def layout(positions, lengths, total):
    count = lengths.shape[0]
    blocks = (lengths + BLOCK - 1) // BLOCK
    first = (jnp.cumsum(blocks) - blocks) * BLOCK
    owner = jnp.sum((positions[:, None] >= first[None, :]).astype(jnp.int32), axis=1) - 1
    table = owner[:, None] == jnp.arange(count, dtype=jnp.int32)[None, :]
    start = jnp.sum(jnp.where(table, first[None, :], 0), axis=1)
    span = jnp.sum(jnp.where(table, lengths[None, :], 0), axis=1)
    local = positions - start
    inside = (positions >= 0) & (positions < total)
    valid = inside & (local < span)
    segment = jnp.where(inside, jnp.where(valid, owner, owner + count), -1)
    return (segment, local, valid)


def body(
    tokens,
    cotangent,
    lengths,
    block_perm,
    attn_gain,
    qkv_weight,
    proj_weight,
    mlp_gain,
    wide_weight,
    narrow_weight,
):
    flow = Phases()
    seq_index = lax.axis_index("seq")
    seq_count = lax.axis_size("seq")
    levels = seq_count.bit_length() - 1
    tok_dev = tokens.shape[1]
    features = tokens.shape[2]
    block_rows = tok_dev // BLK_DEV
    order_map = block_perm[0]
    target = order_map[0::BLK_DEV] // BLK_DEV
    source = jnp.arange(seq_count, dtype=jnp.int32)

    def holder(bit_level):
        low_mask = (1 << bit_level) - 1
        place = jnp.bitwise_or(
            jnp.bitwise_and(target, low_mask), jnp.bitwise_and(source, ~low_mask)
        )
        return jnp.sum(jnp.where(place == seq_index, source, 0))

    home_index = holder(levels)
    slot_of = lax.dynamic_slice_in_dim(order_map, home_index * BLK_DEV, BLK_DEV) % BLK_DEV
    crossed = slot_of[0] == 1

    def crossing(rows):
        turned = jnp.concatenate([rows[block_rows:], rows[:block_rows]], axis=0)
        return jnp.where(crossed, turned, rows)

    def crossed_over(bit_level, given):
        payload = holder(bit_level + 1 if given else bit_level)
        if not given:
            payload = jnp.sum(jnp.where(source == payload, target, 0))
        flips = jnp.right_shift(jnp.bitwise_xor(seq_index, payload), bit_level)
        return jnp.bitwise_and(flips, 1) == 1

    class Route:
        def __init__(self, rows, given):
            self.rows = crossing(rows) if given else rows
            self.given = given
            self.levels = list(range(levels))
            if given:
                self.levels.reverse()
            self.arrived = None
            self.settled = False

        def step(self):
            if self.arrived is not None:
                self.rows = jnp.where(
                    crossed_over(self.level, self.given), flow.tie(self.arrived), self.rows
                )
                self.arrived = None
            if self.levels:
                self.level = self.levels.pop(0)
                self.arrived = flow.swap(self.rows, 2 + self.level)
                return True
            if not self.given and not self.settled:
                self.rows = crossing(self.rows)
            self.settled = True
            return False

        def finish(self):
            while self.step():
                flow.next()
            return self.rows

    total = seq_count * tok_dev
    own_place = seq_index * tok_dev + jnp.arange(tok_dev, dtype=jnp.int32)
    key_place = seq_index * tok_dev - HALO + jnp.arange(tok_dev + 2 * HALO, dtype=jnp.int32)
    seg_query, local_query, valid_query = layout(own_place, lengths[0], total)
    seg_key, _, _ = layout(key_place, lengths[0], total)
    cosine, sine = rope_tables(local_query.astype(F32))
    seg_q_col, seg_q_row = seg_query[:, None], seg_query[None, :]
    seg_k_col, seg_k_row = seg_key[:, None], seg_key[None, :]
    offs = piece_order()
    bits_x, bits_y = stage_bits(True), stage_bits(False)
    picker_x, picker_y = row_picker(features, bits_x), row_picker(features, bits_y)

    gains = jnp.concatenate([attn_gain, mlp_gain], axis=0)
    gains = lax.all_gather(gains, "fsdp", axis=1, tiled=True).astype(F32)
    gains_a = [gains[layer : layer + 1] for layer in range(LAYERS)]
    gains_m = [gains[LAYERS + layer : LAYERS + layer + 1] for layer in range(LAYERS)]

    side = (seq_index % 2).astype(jnp.int32).reshape(1)
    arrays = (proj_weight, wide_weight, narrow_weight)
    items = []
    for layer in range(LAYERS):
        packs = run_pack(side, (qkv_weight,), layer) + run_pack(side, arrays, layer)
        items += [Weights(flow, *pack) for pack in packs]
    per_layer = len(items) // LAYERS
    tok_route, cot_route = Route(tokens[0], False), Route(cotangent[0], False)

    first_use = 3
    owns = {0: (0,), 1: (1, 2), 2: (3,), 4: (4, 5), 5: (6,), 6: (7,)}
    phase = 0

    def transfers():
        if phase < len(items):
            items[phase].over_x()
        if 0 <= phase - 1 < len(items):
            items[phase - 1].over_y()
        if 0 <= phase - 2 < len(items):
            items[phase - 2].over_core()
        for place in owns.get(phase, ()):
            items[place].own()

    flow.keep(gains)
    while phase < first_use or tok_route.levels:
        transfers()
        tok_route.step()
        if phase < 2:
            cot_route.step()
        if phase == 0:
            flow.keep(*(item.shard for item in items[1:]))
        phase += 1
        flow.next()
    tok_route.step()
    residual = tok_route.rows.astype(F32)
    kept = []
    for layer in range(LAYERS):
        base = layer * per_layer
        transfers()
        qkv, normed, edge_first, edge_last = run_qkv(
            offs, flow.tie(residual), gains_a[layer], cosine, sine, items[base].pieces
        )
        flow.keep(normed)
        before = flow.shift(edge_last, True)
        after = flow.shift(edge_first, False)
        phase += 1
        flow.next()
        transfers()
        if layer and kept[-1][-1] is None:
            kept[-1][-1] = (mine, flow.swap(theirs, 0))
        start = residual
        mixed, middle, second = run_attend(
            offs, flow.tie(qkv), before, after, seg_q_col, seg_k_row, residual, gains_m[layer],
            items[base + 1].pieces,
        )
        residual = middle
        hidden = []
        for chunk in range(CHUNKS):
            if chunk:
                phase += 1
                flow.next()
                transfers()
                if chunk == 1 and layer == 0:
                    cot_route.step()
            residual, gated, slope, gate = run_mlp(
                offs, second, flow.tie(residual), items[base + 1 + chunk].pieces, chunk
            )
            flow.keep(residual, gated)
            hidden.append((gated, slope, gate))
            if chunk == 1:
                lefts = (normed, mixed, second)
                which = ((0, 0), (1, 0), (1, 1), (0, 2), (1, 2))
                mine, theirs = run_pick((picker_x, picker_y), lefts, which)
                flow.keep(theirs)
        picks = None
        if layer == LAYERS - 1:
            flow.next()
            picks = (mine, flow.swap(theirs, 0))
        kept.append([start, qkv, before, after, middle, hidden, picks])
        phase += 1
        flow.next()

    upstream_b = cot_route.finish() * valid_query[:, None].astype(BF16)
    upstream = upstream_b.astype(F32)
    out_route = Route(residual.astype(BF16), True)

    late = bits_x[2:]
    exchange = Exchange(flow, features // 2, 3 * features // 2, late)
    endings = []
    sums = {}
    count = 0
    width = 3 * features // 2

    def settle(done):
        nonlocal count
        if done is None:
            return
        deliver = functools.partial(sums.__setitem__, count)
        count += 1
        if len(late) > 2:
            endings.append(Ending(flow, done, late[2:], deliver))
        else:
            deliver(done)

    def step_endings():
        for item in list(endings):
            if not item.step():
                endings.remove(item)

    def group(right, parts):
        segments = []
        at = 0
        for columns, lefts in parts:
            for path in range(2):
                low = max(at, path * width)
                high = min(at + columns, (path + 1) * width)
                if low < high:
                    segments.append((path, low, high, lefts[path][:2], lefts[path][2]))
            at += columns
        return list(right), tuple(segments)

    terms = [None] * LAYERS
    made, ready = None, None

    def backward_phase():
        nonlocal made, ready
        flow.next()
        moving = bool(made or ready or exchange.busy())
        if ready or exchange.busy():
            settle(exchange.step(*(group(*ready) if ready else ())))
        ready = None
        if made:
            right, parts = made
            ready = ((right, flow.swap(right, 0)), parts)
        made = None
        step_endings()
        return moving

    for layer in reversed(range(LAYERS)):
        start, qkv, before, after, middle, hidden, picks = kept[layer]
        base = layer * per_layer
        normed_x, normed_y, mixed_y, second_x, second_y = (picks + (row,) for row in range(5))
        carried = None
        upstream_left = None
        for chunk in reversed(range(CHUNKS)):
            if layer < LAYERS - 1 or chunk < CHUNKS - 1:
                backward_phase()
            pieces = items[base + 1 + chunk].pieces
            if upstream_left is None:
                mine, theirs = run_pick(
                    (picker_x, picker_y), (flow.tie(upstream_b),), ((0, 0), (1, 0))
                )
                flow.keep(theirs)
                upstream_left = []
            elif not upstream_left:
                far = flow.swap(theirs, 0)
                upstream_left += [(mine, far, path) for path in range(2)]
            if layer == LAYERS - 1 and chunk < CHUNKS - 1:
                out_route.step()
            args = (offs, flow.tie(upstream_b), hidden[chunk], carried)
            columns = WIDTHS[chunk]
            parts = [
                (columns, upstream_left),
                (2 * columns, (second_x, second_y)),
            ]
            if chunk:
                carried, right = run_mlp_back(*args, pieces, chunk)
                flow.keep(carried)
            else:
                middle_grad, middle_grad_b, mlp_term, right = run_mlp_back_last(
                    *args, upstream, middle, gains_m[layer], pieces, chunk
                )
                parts.append((2 * width - 3 * columns, (None, mixed_y)))
                query_grad, own_grad, rim_before, rim_after = run_attend_back(
                    offs, middle_grad_b, qkv, before, after, seg_q_row, seg_k_col, cosine, sine, pieces
                )
                flow.keep(query_grad, own_grad)
                arrived_first = flow.shift(rim_after, True)
                arrived_last = flow.shift(rim_before, False)
            flow.keep(right)
            made = (right, parts)
        backward_phase()
        right, upstream, upstream_b, attn_term = run_qkv_back(
            offs, flow.tie(query_grad), own_grad, arrived_first, arrived_last, cosine, sine, start,
            gains_a[layer], middle_grad, items[base].pieces,
        )
        flow.keep(upstream_b, right)
        made = (right, [(2 * width, (normed_x, normed_y))])
        terms[layer] = (attn_term, mlp_term)
    grad_route = Route(upstream_b, True)
    vectors = [terms[layer][0] for layer in range(LAYERS)]
    vectors += [terms[layer][1] for layer in range(LAYERS)]
    backward_phase()
    grad_route.step()
    gain_sums = lax.dot_general(
        flow.tie(jnp.concatenate(vectors, axis=0)), picker_x.astype(F32), NT, precision=lax.Precision.HIGHEST
    )
    gain_bits = [0] + list(bits_x)
    while backward_phase() or endings or gain_bits:
        if not grad_route.step():
            out_route.step()
        for bit in gain_bits[: 1 if len(gain_bits) > 2 else 2]:
            half = gain_sums.shape[1] // 2
            gain_sums = gain_sums[:, :half] + flow.swap(gain_sums[:, half:], bit)
        gain_bits = gain_bits[1 if len(gain_bits) > 2 else 2 :]
    block_out, token_grad = out_route.finish(), grad_route.finish()

    def pieces_of(layer):
        at = per_layer * (LAYERS - 1 - layer)
        parts = {chunk: sums[at + CHUNKS - 1 - chunk] for chunk in range(CHUNKS)}
        return parts, sums[at + CHUNKS]

    def hidden_sum(parts, role):
        columns = [
            parts[chunk][:, role * WIDTHS[chunk] : (role + 1) * WIDTHS[chunk]]
            for chunk in range(CHUNKS)
        ]
        return jnp.concatenate(columns, axis=1)[:, :FF]

    wide, narrow, proj, qkv_sum = [], [], [], []
    for layer in range(LAYERS):
        parts, attend = pieces_of(layer)
        narrow.append(hidden_sum(parts, 0))
        wide.append(jnp.concatenate([hidden_sum(parts, 1), hidden_sum(parts, 2)], axis=1))
        proj.append(parts[0][:, 3 * WIDTHS[0] : 3 * WIDTHS[0] + features])
        qkv_sum.append(attend)
    return (
        block_out[None],
        token_grad[None],
        gain_sums[:LAYERS],
        jnp.stack(qkv_sum),
        jnp.stack(proj),
        gain_sums[LAYERS:],
        jnp.stack(wide),
        jnp.stack(narrow),
    )


def solution(mesh):
    in_specs = (
        P("fsdp", "seq", None),
        P("fsdp", "seq", None),
        P("fsdp", None),
        P("fsdp", None),
        P(None, "fsdp"),
        P(None, "fsdp", None),
        P(None, "fsdp", None),
        P(None, "fsdp"),
        P(None, "fsdp", None),
        P(None, "fsdp", None),
    )
    out_specs = (
        P("fsdp", "seq", None),
        P("fsdp", "seq", None),
        P(None, ("seq", "fsdp")),
        P(None, ("seq", "fsdp"), None),
        P(None, ("seq", "fsdp"), None),
        P(None, ("seq", "fsdp")),
        P(None, ("seq", "fsdp"), None),
        P(None, ("seq", "fsdp"), None),
    )
    return jax.shard_map(body, mesh=mesh, in_specs=in_specs, out_specs=out_specs, check_vma=False)
```

time: 860 us -> 804 us (0.935)
  Pallas kernels: 166 us -> 296 us
  starting transfers between devices: 164 us -> 107 us
  local copies, waits for them, and re-layouts: 105 us -> 55.1 us
  waiting for transfers between devices: 334 us -> 285 us
  other arithmetic: 60 us -> 37.5 us
    pallas_call x38 -> x40, Pallas kernels: 166 us -> 296 us  [run(): pl.pallas_call(kernel, in_specs=specs, out_specs=results, **params)(*args)]
    ppermute x165 -> x103, starting transfers between devices: 164 us -> 107 us  [route(): result = lax.ppermute(self.tie(value), axes, pairs)]
    ppermute x165 -> x103, waiting for transfers between devices: 334 us -> 285 us  [route(): result = lax.ppermute(self.tie(value), axes, pairs)]
    slice x31 -> x11, local copies, waits for them, and re-layouts: 24.8 us -> 5.51 us  [the longest x6 5.35 us: hidden_sum(): parts[chunk][:, role * WIDTHS[chunk]:(role + 1) * WIDTHS[chunk]]]
    unnamed x428 -> x235, local copies, waits for them, and re-layouts: 49.9 us -> 31 us
    convert_element_type x49 -> x5, other arithmetic: 19.5 us -> 4.7 us  [the longest x2 3.47 us: row_picker(): return (order[:, None] == grid[None, :]).astype(BF16)]
    dynamic_slice x9 -> x0, local copies, waits for them, and re-layouts: 13.4 us -> none  [gather_pieces(): sent = lax.dynamic_slice_in_dim(shard, side * half, half, 0)]
    concatenate x1 -> x8, local copies, waits for them, and re-layouts: 0.22 us -> 12.2 us  [over_core(): far = jnp.concatenate([self.far_x, self.flow.tie(self.far_y)], axis=0)]
  transfers between devices with their start and end apart: 165 -> 103, of which waited for: 59 -> 36; matrix products, arithmetic and copies ran while one was open for 16% -> 8% of each run, Pallas kernels for 19% -> 33%
where the time goes in v3:
time: 804 us; the launch traced here: 797 us
  Pallas kernels  296 us (37%)
  waiting for transfers between devices  285 us (35%)
  starting transfers between devices  107 us (13%)
  local copies, waits for them, and re-layouts  55.1 us (7%)
  other arithmetic  37.5 us (5%)
    pallas_call x40, Pallas kernels, run(): pl.pallas_call(kernel, in_specs=specs, out_specs=results, **params)(*args)  296 us
    ppermute x103, waiting for transfers between devices, route(): result = lax.ppermute(self.tie(value), axes, pairs)  285 us
    ppermute x103, starting transfers between devices, route(): result = lax.ppermute(self.tie(value), axes, pairs)  107 us
    unnamed x235, local copies, waits for them, and re-layouts  31 us
  transfers between devices with their start and end apart: 103, of which 36 were waited for; matrix products, arithmetic and copies ran while one was open for 8% of the time, Pallas kernels for 33%

profile of v3, /device:TPU:0, one launch (start us, length us, event | category | flops | bytes accessed | tf_op | source)
XLA Modules:
  0.0 796.8 jit_solution(2706795985281666960)
XLA Ops:
  42.4 9.6 %collective-permute-done.9 = bf16[256,1024]{1,0:T(8,128)(2,1)S(1)} collective-permute-done((bf16[256,1024]{1,0:T(8,128)(2,1)S(1)}, bf16[256,1024]{1,0:T(8,128)(2,1)S(1)}, u32[]{:S(2)}, u32[]{:S(2)}) %collective-permute-start.9) | collective-permute-done | bytes 524320 | tf_op jit(solution)/shard_map/ppermute | solution.py:55
  55.7 10.5 %collective-permute-done.4 = bf16[256,1024]{1,0:T(8,128)(2,1)S(1)} collective-permute-done((bf16[256,1024]{1,0:T(8,128)(2,1)S(1)}, bf16[256,1024]{1,0:T(8,128)(2,1)S(1)}, u32[]{:S(2)}, u32[]{:S(2)}) %collective-permute-start.4) | collective-permute-done | bytes 524320 | tf_op jit(solution)/shard_map/ppermute | solution.py:55
  76.4 22.6 %collective-permute-done.10 = bf16[256,1024]{1,0:T(8,128)(2,1)S(1)} collective-permute-done((bf16[256,1024]{1,0:T(8,128)(2,1)S(1)}, bf16[256,1024]{1,0:T(8,128)(2,1)S(1)}, u32[]{:S(2)}, u32[]{:S(2)}) %collective-permute-start.10) | collective-permute-done | bytes 524320 | tf_op jit(solution)/shard_map/ppermute | solution.py:55
  150.6 11.8 %shard_map.166 = (bf16[256,1024]{1,0:T(8,128)(2,1)}, f32[256,1024]{1,0:T(8,128)}, bf16[256,1024]{1,0:T(8,128)(2,1)}) custom-call(s32[8]{0:T(128)} %stack.71.offs, bf16[256,3072]{1,0:T(8,128)(2,1)} %get-tuple-element.379.qkv, bf16[64,2048]{1,0:T(8,128)(2,1)} %copy-done.40, bf16[64,2048]{1,0:T(8,128)(2,1)} %copy-done.39, s32[256,1]{1,0:T(8,128)} %select_select_fusion.seg_q, ...), custom_call_target="tpu_custom_call" | custom-call | tf_op jit(solution)/shard_map/pallas_call | solution.py:148
  212.7 9.5 %collective-permute-done.31 = bf16[128,2944]{1,0:T(8,128)(2,1)} collective-permute-done((bf16[128,2944]{1,0:T(8,128)(2,1)}, bf16[128,2944]{1,0:T(8,128)(2,1)}, u32[]{:S(2)}, u32[]{:S(2)}) %collective-permute-start.31) | collective-permute-done | bytes 753696 | tf_op jit(solution)/shard_map/ppermute | solution.py:55
  262.1 11.9 %shard_map.172 = (bf16[256,1024]{1,0:T(8,128)(2,1)}, f32[256,1024]{1,0:T(8,128)}, bf16[256,1024]{1,0:T(8,128)(2,1)}) custom-call(s32[8]{0:T(128)} %stack.71.offs, bf16[256,3072]{1,0:T(8,128)(2,1)} %get-tuple-element.426.qkv, bf16[64,2048]{1,0:T(8,128)(2,1)} %copy-done.42, bf16[64,2048]{1,0:T(8,128)(2,1)} %copy-done.41, s32[256,1]{1,0:T(8,128)} %select_select_fusion.seg_q, ...), custom_call_target="tpu_custom_call" | custom-call | tf_op jit(solution)/shard_map/pallas_call | solution.py:148
  328.3 16.8 %collective-permute-done.44 = bf16[256,1024]{1,0:T(8,128)(2,1)S(1)} collective-permute-done((bf16[256,1024]{1,0:T(8,128)(2,1)S(1)}, bf16[256,1024]{1,0:T(8,128)(2,1)S(1)}, u32[]{:S(2)}, u32[]{:S(2)}) %collective-permute-start.44) | collective-permute-done | bytes 524320 | tf_op jit(solution)/shard_map/ppermute | solution.py:55
  356.3 16.7 %shard_map.181 = (bf16[256,1024]{1,0:T(8,128)(2,1)}, f32[256,2048]{1,0:T(8,128)}, bf16[64,2048]{1,0:T(8,128)(2,1)}, bf16[64,2048]{1,0:T(8,128)(2,1)}) custom-call(s32[8]{0:T(128)} %stack.71.offs, bf16[256,1024]{1,0:T(8,128)(2,1)} %get-tuple-element.467.middle_grad, bf16[256,3072]{1,0:T(8,128)(2,1)} %get-tuple-element.426.qkv, bf16[64,2048]{1,0:T(8,128)(2,1)} %copy-done.42, ...), custom_call_target="tpu_custom_call" | custom-call | tf_op jit(solution)/shard_map/pallas_call | solution.py:148
  389.7 16.4 %collective-permute-done.51.arrived_first = bf16[64,2048]{1,0:T(8,128)(2,1)S(1)} collective-permute-done((bf16[64,2048]{1,0:T(8,128)(2,1)}, bf16[64,2048]{1,0:T(8,128)(2,1)S(1)}, u32[]{:S(2)}, u32[]{:S(2)}) %collective-permute-start.51) | collective-permute-done | bytes 262176 | tf_op jit(solution)/shard_map/ppermute | solution.py:55
  428.6 16.7 %collective-permute-done.54.refs_17_ = bf16[384,1536]{1,0:T(8,128)(2,1)} collective-permute-done((bf16[384,1536]{1,0:T(8,128)(2,1)}, bf16[384,1536]{1,0:T(8,128)(2,1)}, u32[]{:S(2)}, u32[]{:S(2)}) %collective-permute-start.54) | collective-permute-done | bytes 1179680 | tf_op jit(solution)/shard_map/ppermute | solution.py:55
  471.5 13.9 %collective-permute-done.57.refs_13_ = bf16[384,1536]{1,0:T(8,128)(2,1)S(1)} collective-permute-done((bf16[384,1536]{1,0:T(8,128)(2,1)}, bf16[384,1536]{1,0:T(8,128)(2,1)S(1)}, u32[]{:S(2)}, u32[]{:S(2)}) %collective-permute-start.57) | collective-permute-done | bytes 1179680 | tf_op jit(solution)/shard_map/ppermute | solution.py:55
  486.9 9.3 %shard_map.188 = (bf16[256,1536]{1,0:T(8,128)(2,1)}, bf16[256,1536]{1,0:T(8,128)(2,1)}, bf16[128,1536]{1,0:T(8,128)(2,1)}, bf16[128,1536]{1,0:T(8,128)(2,1)}, bf...) custom-call(bf16[256,3072]{1,0:T(8,128)(2,1)} %get-tuple-element.513, ...), custom_call_target="tpu_custom_call" | custom-call | tf_op jit(solution)/shard_map/pallas_call | solution.py:148
  499.5 10.3 %collective-permute-done.63.refs_19_ = bf16[32,3072]{1,0:T(8,128)(2,1)} collective-permute-done((bf16[32,3072]{1,0:T(8,128)(2,1)}, bf16[32,3072]{1,0:T(8,128)(2,1)}, u32[]{:S(2)}, u32[]{:S(2)}) %collective-permute-start.63) | collective-permute-done | bytes 196640 | tf_op jit(solution)/shard_map/ppermute | solution.py:55
  526.2 9.5 %shard_map.192 = (bf16[256,1536]{1,0:T(8,128)(2,1)}, bf16[256,1536]{1,0:T(8,128)(2,1)}, bf16[128,1536]{1,0:T(8,128)(2,1)}, bf16[128,1536]{1,0:T(8,128)(2,1)}, bf...) custom-call(bf16[256,3072]{1,0:T(8,128)(2,1)} %get-tuple-element.540, ...), custom_call_target="tpu_custom_call" | custom-call | tf_op jit(solution)/shard_map/pallas_call | solution.py:148
  546.5 16.8 %shard_map.191 = (bf16[256,1024]{1,0:T(8,128)(2,1)}, f32[256,2048]{1,0:T(8,128)}, bf16[64,2048]{1,0:T(8,128)(2,1)}, bf16[64,2048]{1,0:T(8,128)(2,1)}) custom-call(s32[8]{0:T(128)} %stack.71.offs, bf16[256,1024]{1,0:T(8,128)(2,1)} %get-tuple-element.538.middle_grad, bf16[256,3072]{1,0:T(8,128)(2,1)} %get-tuple-element.379.qkv, bf16[64,2048]{1,0:T(8,128)(2,1)} %copy-done.40, ...), custom_call_target="tpu_custom_call" | custom-call | tf_op jit(solution)/shard_map/pallas_call | solution.py:148
  584.1 9.7 %shard_map.194 = (bf16[256,1536]{1,0:T(8,128)(2,1)}, bf16[256,1536]{1,0:T(8,128)(2,1)}, bf16[128,1536]{1,0:T(8,128)(2,1)}, bf16[128,1536]{1,0:T(8,128)(2,1)}, bf...) custom-call(bf16[256,3072]{1,0:T(8,128)(2,1)} %get-tuple-element.567, ...), custom_call_target="tpu_custom_call" | custom-call | tf_op jit(solution)/shard_map/pallas_call | solution.py:148
  599.5 8.8 %shard_map.193 = (bf16[256,3072]{1,0:T(8,128)(2,1)}, f32[256,1024]{1,0:T(8,128)}, bf16[256,1024]{1,0:T(8,128)(2,1)}, f32[1,1024]{1,0:T(1,128)}) custom-call(s32[8]{0:T(128)} %stack.71.offs, bf16[256,1024]{1,0:T(8,128)(2,1)} %get-tuple-element.564.query_grad, f32[256,2048]{1,0:T(8,128)} %get-tuple-element.558.own_grad, bf16[64,2048]{1,0:T(8,128)(2,1)} %copy-done.78, ...), custom_call_target="tpu_custom_call" | custom-call | tf_op jit(solution)/shard_map/pallas_call | solution.py:148
  611.4 10.4 %collective-permute-done.74.refs_17_ = bf16[384,1536]{1,0:T(8,128)(2,1)S(1)} collective-permute-done((bf16[384,1536]{1,0:T(8,128)(2,1)}, bf16[384,1536]{1,0:T(8,128)(2,1)S(1)}, u32[]{:S(2)}, u32[]{:S(2)}) %collective-permute-start.74) | collective-permute-done | bytes 1179680 | tf_op jit(solution)/shard_map/ppermute | solution.py:55
  624.6 9.7 %shard_map.195 = (bf16[256,1536]{1,0:T(8,128)(2,1)}, bf16[256,1536]{1,0:T(8,128)(2,1)}, bf16[128,1536]{1,0:T(8,128)(2,1)}, bf16[128,1536]{1,0:T(8,128)(2,1)}, bf...) custom-call(bf16[256,3072]{1,0:T(8,128)(2,1)} %get-tuple-element.584, ...), custom_call_target="tpu_custom_call" | custom-call | tf_op jit(solution)/shard_map/pallas_call | solution.py:148
  641.0 20.6 %collective-permute-done.81.refs_17_ = bf16[32,3072]{1,0:T(8,128)(2,1)S(1)} collective-permute-done((bf16[32,3072]{1,0:T(8,128)(2,1)S(1)}, bf16[32,3072]{1,0:T(8,128)(2,1)S(1)}, u32[]{:S(2)}, u32[]{:S(2)}) %collective-permute-start.81) | collective-permute-done | bytes 196640 | tf_op jit(solution)/shard_map/ppermute | solution.py:55
  663.7 16.9 %collective-permute-done.80.refs_15_ = bf16[64,3072]{1,0:T(8,128)(2,1)S(1)} collective-permute-done((bf16[64,3072]{1,0:T(8,128)(2,1)S(1)}, bf16[64,3072]{1,0:T(8,128)(2,1)S(1)}, u32[]{:S(2)}, u32[]{:S(2)}) %collective-permute-start.80) | collective-permute-done | bytes 393248 | tf_op jit(solution)/shard_map/ppermute | solution.py:55
  682.8 9.6 %shard_map.196 = (bf16[256,1536]{1,0:T(8,128)(2,1)}, bf16[256,1536]{1,0:T(8,128)(2,1)}, bf16[128,1536]{1,0:T(8,128)(2,1)}, bf16[128,1536]{1,0:T(8,128)(2,1)}, bf...) custom-call(bf16[256,3072]{1,0:T(8,128)(2,1)} %get-tuple-element.601, ...), custom_call_target="tpu_custom_call" | custom-call | tf_op jit(solution)/shard_map/pallas_call | solution.py:148
  702.6 21.1 %collective-permute-done.87.refs_9_ = bf16[32,3072]{1,0:T(8,128)(2,1)S(1)} collective-permute-done((bf16[32,3072]{1,0:T(8,128)(2,1)S(1)}, bf16[32,3072]{1,0:T(8,128)(2,1)S(1)}, u32[]{:S(2)}, u32[]{:S(2)}) %collective-permute-start.87) | collective-permute-done | bytes 196640 | tf_op jit(solution)/shard_map/ppermute | solution.py:55
  739.4 8.9 %collective-permute-done.93.refs_7_ = bf16[32,3072]{1,0:T(8,128)(2,1)S(1)} collective-permute-done((bf16[32,3072]{1,0:T(8,128)(2,1)}, bf16[32,3072]{1,0:T(8,128)(2,1)S(1)}, u32[]{:S(2)}, u32[]{:S(2)}) %collective-permute-start.93) | collective-permute-done | bytes 196640 | tf_op jit(solution)/shard_map/ppermute | solution.py:55
  (551 shorter events, 471.1 us)
Async XLA Ops:
  32.4 33.8 %collective-permute-start.8 = (bf16[256,3072]{1,0:T(8,128)(2,1)}, bf16[256,3072]{1,0:T(8,128)(2,1)}, u32[]{:S(2)}, u32[]{:S(2)}) collective-permute-start(bf16[256,3072]{1,0:T(8,128)(2,1)} %get-tuple-element.355.p0), channel_id=1, source_target_pairs={{0,1},{1,0},{2,3},{3,2},{4,5},{5,4},{6,7},{7,6},{8,9},{9,8},{10,11... | collective-permute-start | bytes 4718600 | tf_op jit(solution)/shard_map/ppermute | solution.py:55
  33.8 32.4 %collective-permute-start.7 = (bf16[256,2944]{1,0:T(8,128)(2,1)}, bf16[256,2944]{1,0:T(8,128)(2,1)S(1)}, u32[]{:S(2)}, u32[]{:S(2)}) collective-permute-start(bf16[256,2944]{1,0:T(8,128)(2,1)} %get-tuple-element.354.p0), channel_id=1, source_target_pairs={{0,1},{1,0},{2,3},{3,2},{4,5},{5,4},{6,7},{7,6},{8,9},{9,8},{10,11... | collective-permute-start | bytes 4521992 | tf_op jit(solution)/shard_map/ppermute | solution.py:55
  67.3 31.8 %collective-permute-start.13 = (bf16[256,3072]{1,0:T(8,128)(2,1)}, bf16[256,3072]{1,0:T(8,128)(2,1)}, u32[]{:S(2)}, u32[]{:S(2)}) collective-permute-start(bf16[256,3072]{1,0:T(8,128)(2,1)} %constant_dynamic-update-slice_fusion.p1), channel_id=1, source_target_pairs={{0,1},{1,0},{2,3},{3,2},{4,5},{5,4},{6,7},{7,6},{8,9},{9,8},{10,11... | collective-permute-start | bytes 4718600 | tf_op jit(solution)/shard_map/ppermute | solution.py:55
  67.5 31.6 %collective-permute-start.14 = (bf16[256,3072]{1,0:T(8,128)(2,1)}, bf16[256,3072]{1,0:T(8,128)(2,1)}, u32[]{:S(2)}, u32[]{:S(2)}) collective-permute-start(bf16[256,3072]{1,0:T(8,128)(2,1)} %get-tuple-element.365.p0), channel_id=1, source_target_pairs={{0,1},{1,0},{2,3},{3,2},{4,5},{5,4},{6,7},{7,6},{8,9},{9,8},{10,11... | collective-permute-start | bytes 4718600 | tf_op jit(solution)/shard_map/ppermute | solution.py:55
  100.0 36.5 %collective-permute-start.17 = (bf16[256,2944]{1,0:T(8,128)(2,1)S(1)}, bf16[256,2944]{1,0:T(8,128)(2,1)S(1)}, u32[]{:S(2)}, u32[]{:S(2)}) collective-permute-start(bf16[256,2944]{1,0:T(8,128)(2,1)S(1)} %constant_dynamic-update-slice_fusion.2.p1), channel_id=1, source_target_pairs={{0,1},{1,0},{2,3},{3,2},{4,5},{5,4},{6,7},{7,6},{8,9},{9,8},{10,11... | collective-permute-start | bytes 4521992 | tf_op jit(solution)/shard_map/ppermute | solution.py:55
  105.8 30.7 %collective-permute-start.15 = (bf16[128,3072]{1,0:T(8,128)(2,1)}, bf16[128,3072]{1,0:T(8,128)(2,1)}, u32[]{:S(2)}, u32[]{:S(2)}) collective-permute-start(bf16[128,3072]{1,0:T(8,128)(2,1)} %get-tuple-element.370), channel_id=1, source_target_pairs={{0,2},{1,3},{2,0},{3,1},{4,6},{5,7},{6,4},{7,5},{8,10},{9,11},{10,... | collective-permute-start | bytes 2359304 | tf_op jit(solution)/shard_map/ppermute | solution.py:55
  170.2 31.0 %collective-permute-start.27 = (bf16[256,3072]{1,0:T(8,128)(2,1)S(1)}, bf16[256,3072]{1,0:T(8,128)(2,1)}, u32[]{:S(2)}, u32[]{:S(2)}) collective-permute-start(bf16[256,3072]{1,0:T(8,128)(2,1)S(1)} %constant_dynamic-update-slice_fusion.6.p1), channel_id=1, source_target_pairs={{0,1},{1,0},{2,3},{3,2},{4,5},{5,4},{6,7},{7,6},{8,9},{9,8},{10,11... | collective-permute-start | bytes 4718600 | tf_op jit(solution)/shard_map/ppermute | solution.py:55
  170.3 30.9 %collective-permute-start.28 = (bf16[256,3072]{1,0:T(8,128)(2,1)}, bf16[256,3072]{1,0:T(8,128)(2,1)}, u32[]{:S(2)}, u32[]{:S(2)}) collective-permute-start(bf16[256,3072]{1,0:T(8,128)(2,1)} %get-tuple-element.399.p0), channel_id=1, source_target_pairs={{0,1},{1,0},{2,3},{3,2},{4,5},{5,4},{6,7},{7,6},{8,9},{9,8},{10,11... | collective-permute-start | bytes 4718600 | tf_op jit(solution)/shard_map/ppermute | solution.py:55
  224.1 31.2 %collective-permute-start.36 = (bf16[256,2944]{1,0:T(8,128)(2,1)S(1)}, bf16[256,2944]{1,0:T(8,128)(2,1)S(1)}, u32[]{:S(2)}, u32[]{:S(2)}) collective-permute-start(bf16[256,2944]{1,0:T(8,128)(2,1)S(1)} %constant_dynamic-update-slice_fusion.10.p1), channel_id=1, source_target_pairs={{0,1},{1,0},{2,3},{3,2},{4,5},{5,4},{6,7},{7,6},{8,9},{9,8},{10,11... | collective-permute-start | bytes 4521992 | tf_op jit(solution)/shard_map/ppermute | solution.py:55
  224.2 31.1 %collective-permute-start.34 = (bf16[128,3072]{1,0:T(8,128)(2,1)}, bf16[128,3072]{1,0:T(8,128)(2,1)}, u32[]{:S(2)}, u32[]{:S(2)}) collective-permute-start(bf16[128,3072]{1,0:T(8,128)(2,1)} %get-tuple-element.417), channel_id=1, source_target_pairs={{0,2},{1,3},{2,0},{3,1},{4,6},{5,7},{6,4},{7,5},{8,10},{9,11},{10,... | collective-permute-start | bytes 2359304 | tf_op jit(solution)/shard_map/ppermute | solution.py:55
  346.1 60.1 %collective-permute-start.50 = (bf16[256,3072]{1,0:T(8,128)(2,1)}, bf16[256,3072]{1,0:T(8,128)(2,1)S(1)}, u32[]{:S(2)}, u32[]{:S(2)}) collective-permute-start(bf16[256,3072]{1,0:T(8,128)(2,1)} %get-tuple-element.487.refs_0_.refs_1_), channel_id=1, source_target_pairs={{0,1},{1,0},{2,3},{3,2},{4,5},{5,4},{6,7},{7,6},{8,9},{9,8},{10,11... | collective-permute-start | bytes 4718600 | tf_op jit(solution)/shard_map/ppermute | solution.py:55
  407.5 39.2 %collective-permute-start.55 = (bf16[256,3072]{1,0:T(8,128)(2,1)S(1)}, bf16[256,3072]{1,0:T(8,128)(2,1)S(1)}, u32[]{:S(2)}, u32[]{:S(2)}) collective-permute-start(bf16[256,3072]{1,0:T(8,128)(2,1)S(1)} %copy-done.13), channel_id=1, source_target_pairs={{0,1},{1,0},{2,3},{3,2},{4,5},{5,4},{6,7},{7,6},{8,9},{9,8},{10,11... | collective-permute-start | bytes 4718600 | tf_op jit(solution)/shard_map/ppermute | solution.py:55
  447.9 37.6 %collective-permute-start.59 = (bf16[256,3072]{1,0:T(8,128)(2,1)}, bf16[256,3072]{1,0:T(8,128)(2,1)S(1)}, u32[]{:S(2)}, u32[]{:S(2)}) collective-permute-start(bf16[256,3072]{1,0:T(8,128)(2,1)} %get-tuple-element.513.refs_0_.refs_1_), channel_id=1, source_target_pairs={{0,1},{1,0},{2,3},{3,2},{4,5},{5,4},{6,7},{7,6},{8,9},{9,8},{10,11... | collective-permute-start | bytes 4718600 | tf_op jit(solution)/shard_map/ppermute | solution.py:55
  486.4 38.7 %collective-permute-start.64 = (bf16[256,3072]{1,0:T(8,128)(2,1)}, bf16[256,3072]{1,0:T(8,128)(2,1)S(1)}, u32[]{:S(2)}, u32[]{:S(2)}) collective-permute-start(bf16[256,3072]{1,0:T(8,128)(2,1)} %get-tuple-element.540.refs_0_.refs_1_), channel_id=1, source_target_pairs={{0,1},{1,0},{2,3},{3,2},{4,5},{5,4},{6,7},{7,6},{8,9},{9,8},{10,11... | collective-permute-start | bytes 4718600 | tf_op jit(solution)/shard_map/ppermute | solution.py:55
  525.4 57.2 %collective-permute-start.70 = (bf16[256,3072]{1,0:T(8,128)(2,1)}, bf16[256,3072]{1,0:T(8,128)(2,1)S(1)}, u32[]{:S(2)}, u32[]{:S(2)}) collective-permute-start(bf16[256,3072]{1,0:T(8,128)(2,1)} %get-tuple-element.567.refs_0_.refs_1_), channel_id=1, source_target_pairs={{0,1},{1,0},{2,3},{3,2},{4,5},{5,4},{6,7},{7,6},{8,9},{9,8},{10,11... | collective-permute-start | bytes 4718600 | tf_op jit(solution)/shard_map/ppermute | solution.py:55
  535.7 46.9 %collective-permute-start.67 = (bf16[384,1536]{1,0:T(8,128)(2,1)}, bf16[384,1536]{1,0:T(8,128)(2,1)}, u32[]{:S(2)}, u32[]{:S(2)}) collective-permute-start(bf16[384,1536]{1,0:T(8,128)(2,1)} %get-tuple-element.552), channel_id=1, source_target_pairs={{0,4},{1,5},{2,6},{3,7},{4,0},{5,1},{6,2},{7,3},{8,12},{9,13},{10,... | collective-permute-start | bytes 3538952 | tf_op jit(solution)/shard_map/ppermute | solution.py:55
  536.9 45.7 %collective-permute-start.66 = (bf16[384,1536]{1,0:T(8,128)(2,1)}, bf16[384,1536]{1,0:T(8,128)(2,1)}, u32[]{:S(2)}, u32[]{:S(2)}) collective-permute-start(bf16[384,1536]{1,0:T(8,128)(2,1)} %get-tuple-element.550), channel_id=1, source_target_pairs={{0,2},{1,3},{2,0},{3,1},{4,6},{5,7},{6,4},{7,5},{8,10},{9,11},{10,... | collective-permute-start | bytes 3538952 | tf_op jit(solution)/shard_map/ppermute | solution.py:55
  582.7 40.7 %collective-permute-start.77 = (bf16[256,3072]{1,0:T(8,128)(2,1)S(1)}, bf16[256,3072]{1,0:T(8,128)(2,1)}, u32[]{:S(2)}, u32[]{:S(2)}) collective-permute-start(bf16[256,3072]{1,0:T(8,128)(2,1)S(1)} %copy-done.12), channel_id=1, source_target_pairs={{0,1},{1,0},{2,3},{3,2},{4,5},{5,4},{6,7},{7,6},{8,9},{9,8},{10,11... | collective-permute-start | bytes 4718600 | tf_op jit(solution)/shard_map/ppermute | solution.py:55
  623.4 57.2 %collective-permute-start.82 = (bf16[256,3072]{1,0:T(8,128)(2,1)}, bf16[256,3072]{1,0:T(8,128)(2,1)S(1)}, u32[]{:S(2)}, u32[]{:S(2)}) collective-permute-start(bf16[256,3072]{1,0:T(8,128)(2,1)} %get-tuple-element.601.refs_0_.refs_1_), channel_id=1, source_target_pairs={{0,1},{1,0},{2,3},{3,2},{4,5},{5,4},{6,7},{7,6},{8,9},{9,8},{10,11... | collective-permute-start | bytes 4718600 | tf_op jit(solution)/shard_map/ppermute | solution.py:55
  634.3 46.3 %collective-permute-start.79 = (bf16[384,1536]{1,0:T(8,128)(2,1)}, bf16[384,1536]{1,0:T(8,128)(2,1)S(1)}, u32[]{:S(2)}, u32[]{:S(2)}) collective-permute-start(bf16[384,1536]{1,0:T(8,128)(2,1)} %get-tuple-element.594), channel_id=1, source_target_pairs={{0,4},{1,5},{2,6},{3,7},{4,0},{5,1},{6,2},{7,3},{8,12},{9,13},{10,... | collective-permute-start | bytes 3538952 | tf_op jit(solution)/shard_map/ppermute | solution.py:55
  634.7 45.9 %collective-permute-start.78 = (bf16[384,1536]{1,0:T(8,128)(2,1)}, bf16[384,1536]{1,0:T(8,128)(2,1)S(1)}, u32[]{:S(2)}, u32[]{:S(2)}) collective-permute-start(bf16[384,1536]{1,0:T(8,128)(2,1)} %get-tuple-element.592), channel_id=1, source_target_pairs={{0,2},{1,3},{2,0},{3,1},{4,6},{5,7},{6,4},{7,5},{8,10},{9,11},{10,... | collective-permute-start | bytes 3538952 | tf_op jit(solution)/shard_map/ppermute | solution.py:55
  640.1 40.4 %collective-permute-start.83 = (bf16[256,1024]{1,0:T(8,128)(2,1)S(1)}, bf16[256,1024]{1,0:T(8,128)(2,1)S(1)}, u32[]{:S(2)}, u32[]{:S(2)}) collective-permute-start(bf16[256,1024]{1,0:T(8,128)(2,1)S(1)} %maximum_select_fusion.3), channel_id=1, source_target_pairs={{0,16},{1,17},{2,18},{3,19},{4,20},{5,21},{6,22},{7,23},{8,24},{9,... | collective-permute-start | bytes 1572872 | tf_op jit(solution)/shard_map/ppermute | solution.py:55
  692.4 33.5 %collective-permute-start.85 = (bf16[384,1536]{1,0:T(8,128)(2,1)}, bf16[384,1536]{1,0:T(8,128)(2,1)S(1)}, u32[]{:S(2)}, u32[]{:S(2)}) collective-permute-start(bf16[384,1536]{1,0:T(8,128)(2,1)} %get-tuple-element.612), channel_id=1, source_target_pairs={{0,4},{1,5},{2,6},{3,7},{4,0},{5,1},{6,2},{7,3},{8,12},{9,13},{10,... | collective-permute-start | bytes 3538952 | tf_op jit(solution)/shard_map/ppermute | solution.py:55
  693.7 32.3 %collective-permute-start.84 = (bf16[384,1536]{1,0:T(8,128)(2,1)}, bf16[384,1536]{1,0:T(8,128)(2,1)S(1)}, u32[]{:S(2)}, u32[]{:S(2)}) collective-permute-start(bf16[384,1536]{1,0:T(8,128)(2,1)} %get-tuple-element.610), channel_id=1, source_target_pairs={{0,2},{1,3},{2,0},{3,1},{4,6},{5,7},{6,4},{7,5},{8,10},{9,11},{10,... | collective-permute-start | bytes 3538952 | tf_op jit(solution)/shard_map/ppermute | solution.py:55
  (192 other events, 2683.6 us)

commit v4 on v3

--- a/solution.py
+++ b/solution.py
@@ -31,7 +31,7 @@
 TILES = 3
 F32 = jnp.float32
 BF16 = jnp.bfloat16
-VMEM_LIMIT = 60 * 1024 * 1024
+VMEM_LIMIT = 20 * 1024 * 1024
 NT = (((1,), (1,)), ((), ()))
 TN = (((0,), (0,)), ((), ()))
 
@@ -125,9 +125,9 @@
     return (order[:, None] == grid[None, :]).astype(BF16)
 
 
-def call(kernel, outs, scratch=(), smem=1, grid=None, in_specs=None, out_specs=None):
+def call(kernel, outs, scratch=(), smem=1, grid=None, in_specs=None, out_specs=None, limit=VMEM_LIMIT):
     params = dict(
-        compiler_params=pltpu.CompilerParams(vmem_limit_bytes=VMEM_LIMIT),
+        compiler_params=pltpu.CompilerParams(vmem_limit_bytes=limit),
         out_shape=outs,
         scratch_shapes=list(scratch),
         cost_estimate=pl.CostEstimate(
@@ -942,14 +942,13 @@
         return jnp.bitwise_and(flips, 1) == 1
 
     class Route:
-        def __init__(self, rows, given):
-            self.rows = crossing(rows) if given else rows
+        def __init__(self, rows, given, last=levels):
+            self.rows = rows
             self.given = given
-            self.levels = list(range(levels))
+            self.levels = list(range(last))
             if given:
                 self.levels.reverse()
             self.arrived = None
-            self.settled = False
 
         def step(self):
             if self.arrived is not None:
@@ -961,9 +960,6 @@
                 self.level = self.levels.pop(0)
                 self.arrived = flow.swap(self.rows, 2 + self.level)
                 return True
-            if not self.given and not self.settled:
-                self.rows = crossing(self.rows)
-            self.settled = True
             return False
 
         def finish(self):
@@ -995,10 +991,10 @@
         packs = run_pack(side, (qkv_weight,), layer) + run_pack(side, arrays, layer)
         items += [Weights(flow, *pack) for pack in packs]
     per_layer = len(items) // LAYERS
-    tok_route, cot_route = Route(tokens[0], False), Route(cotangent[0], False)
+    tok_route, cot_route = Route(tokens[0], False), Route(cotangent[0], False, levels - 1)
 
     first_use = 3
-    owns = {0: (0,), 1: (1, 2), 2: (3,), 4: (4, 5), 5: (6,), 6: (7,)}
+    owns = {0: (0, 1), 1: (2,), 2: (3,), 4: (4, 5), 5: (6,), 6: (7,)}
     phase = 0
 
     def transfers():
@@ -1022,7 +1018,8 @@
         phase += 1
         flow.next()
     tok_route.step()
-    residual = tok_route.rows.astype(F32)
+    residual = crossing(tok_route.rows).astype(F32)
+    cot_halves = []
     kept = []
     for layer in range(LAYERS):
         base = layer * per_layer
@@ -1050,8 +1047,13 @@
                 phase += 1
                 flow.next()
                 transfers()
-                if chunk == 1 and layer == 0:
-                    cot_route.step()
+                if layer == 0:
+                    if not cot_halves:
+                        cot_rows = cot_route.finish()
+                        for half in (cot_rows[:block_rows], cot_rows[block_rows:]):
+                            cot_halves.append(Route(half, False))
+                            cot_halves[-1].levels = [levels - 1]
+                    cot_halves[chunk - 1].step()
             residual, gated, slope, gate = run_mlp(
                 offs, second, flow.tie(residual), items[base + 1 + chunk].pieces, chunk
             )
@@ -1070,9 +1072,15 @@
         phase += 1
         flow.next()
 
-    upstream_b = cot_route.finish() * valid_query[:, None].astype(BF16)
+    packed_cot = crossing(jnp.concatenate([half.finish() for half in cot_halves], axis=0))
+    upstream_b = packed_cot * valid_query[:, None].astype(BF16)
     upstream = upstream_b.astype(F32)
-    out_route = Route(residual.astype(BF16), True)
+
+    def both_halves(rows):
+        rows = crossing(rows)
+        return [Route(rows[:block_rows], True), Route(rows[block_rows:], True)]
+
+    out_routes = both_halves(residual.astype(BF16))
 
     late = bits_x[2:]
     exchange = Exchange(flow, features // 2, 3 * features // 2, late)
@@ -1145,8 +1153,8 @@
             elif not upstream_left:
                 far = flow.swap(theirs, 0)
                 upstream_left += [(mine, far, path) for path in range(2)]
-            if layer == LAYERS - 1 and chunk < CHUNKS - 1:
-                out_route.step()
+            if layer == LAYERS - 1 and chunk:
+                out_routes[CHUNKS - 1 - chunk].step()
             args = (offs, flow.tie(upstream_b), hidden[chunk], carried)
             columns = WIDTHS[chunk]
             parts = [
@@ -1174,26 +1182,35 @@
             offs, flow.tie(query_grad), own_grad, arrived_first, arrived_last, cosine, sine, start,
             gains_a[layer], middle_grad, items[base].pieces,
         )
+        if layer:
+            for route in out_routes:
+                route.step()
         flow.keep(upstream_b, right)
         made = (right, [(2 * width, (normed_x, normed_y))])
         terms[layer] = (attn_term, mlp_term)
-    grad_route = Route(upstream_b, True)
+    backward_phase()
+    grad_routes = both_halves(flow.tie(upstream_b))
+    grad_routes[0].step()
     vectors = [terms[layer][0] for layer in range(LAYERS)]
     vectors += [terms[layer][1] for layer in range(LAYERS)]
-    backward_phase()
-    grad_route.step()
     gain_sums = lax.dot_general(
         flow.tie(jnp.concatenate(vectors, axis=0)), picker_x.astype(F32), NT, precision=lax.Precision.HIGHEST
     )
     gain_bits = [0] + list(bits_x)
     while backward_phase() or endings or gain_bits:
-        if not grad_route.step():
-            out_route.step()
+        for route in grad_routes:
+            route.step()
+        if not grad_routes[0].levels:
+            for route in out_routes:
+                route.step()
         for bit in gain_bits[: 1 if len(gain_bits) > 2 else 2]:
             half = gain_sums.shape[1] // 2
             gain_sums = gain_sums[:, :half] + flow.swap(gain_sums[:, half:], bit)
         gain_bits = gain_bits[1 if len(gain_bits) > 2 else 2 :]
-    block_out, token_grad = out_route.finish(), grad_route.finish()
+    block_out, token_grad = (
+        jnp.concatenate([route.finish() for route in routes], axis=0)
+        for routes in (out_routes, grad_routes)
+    )
 
     def pieces_of(layer):
         at = per_layer * (LAYERS - 1 - layer)

time: 804 us -> 688 us (0.86)
  Pallas kernels: 296 us -> 175 us
  local copies, waits for them, and re-layouts: 55.1 us -> 75.6 us
  other arithmetic: 37.5 us -> 21.2 us
    pallas_call x40, Pallas kernels: 296 us -> 175 us  [run(): pl.pallas_call(kernel, in_specs=specs, out_specs=results, **params)(*args)]
    unnamed x235 -> x391, local copies, waits for them, and re-layouts: 31 us -> 69 us
    concatenate x8, local copies, waits for them, and re-layouts: 12.2 us -> 2.38 us  [over_core(): far = jnp.concatenate([self.far_x, self.flow.tie(self.far_y)], axis=0)]
    ppermute x103 -> x110, waiting for transfers between devices: 285 us -> 281 us  [route(): result = lax.ppermute(self.tie(value), axes, pairs)]
    ppermute x103 -> x110, starting transfers between devices: 107 us -> 110 us  [route(): result = lax.ppermute(self.tie(value), axes, pairs)]
  transfers between devices with their start and end apart: 103 -> 110, of which waited for: 36 -> 43; matrix products, arithmetic and copies ran while one was open for 8% -> 5% of each run, Pallas kernels for 33% -> 24%
where the time goes in v4:
time: 688 us; the launch traced here: 680 us
  waiting for transfers between devices  281 us (41%)
  Pallas kernels  175 us (25%)
  starting transfers between devices  110 us (16%)
  local copies, waits for them, and re-layouts  75.6 us (11%)
  other arithmetic  21.2 us (3%)
  between operations  8.33 us (1%)
    ppermute x110, waiting for transfers between devices, route(): result = lax.ppermute(self.tie(value), axes, pairs)  281 us
    pallas_call x40, Pallas kernels, run(): pl.pallas_call(kernel, in_specs=specs, out_specs=results, **params)(*args)  175 us
    ppermute x110, starting transfers between devices, route(): result = lax.ppermute(self.tie(value), axes, pairs)  110 us
    unnamed x391, local copies, waits for them, and re-layouts  69 us
  transfers between devices with their start and end apart: 110, of which 43 were waited for; matrix products, arithmetic and copies ran while one was open for 5% of the time, Pallas kernels for 24%

profile of v4, /device:TPU:0, one launch (start us, length us, event | category | flops | bytes accessed | tf_op | source)
XLA Modules:
  0.0 679.7 jit_solution(14254971446507816824)
XLA Ops:
  30.7 6.4 all_gather.3
  55.3 8.1 %collective-permute-done.5 = bf16[256,1024]{1,0:T(8,128)(2,1)S(1)} collective-permute-done((bf16[256,1024]{1,0:T(8,128)(2,1)S(1)}, bf16[256,1024]{1,0:T(8,128)(2,1)S(1)}, u32[]{:S(2)}, u32[]{:S(2)}) %collective-permute-start.5) | collective-permute-done | bytes 524320 | tf_op jit(solution)/shard_map/ppermute | solution.py:55
  63.3 10.8 %collective-permute-done.9 = bf16[256,1024]{1,0:T(8,128)(2,1)S(1)} collective-permute-done((bf16[256,1024]{1,0:T(8,128)(2,1)S(1)}, bf16[256,1024]{1,0:T(8,128)(2,1)S(1)}, u32[]{:S(2)}, u32[]{:S(2)}) %collective-permute-start.9) | collective-permute-done | bytes 524320 | tf_op jit(solution)/shard_map/ppermute | solution.py:55
  84.5 22.5 %collective-permute-done.10 = bf16[256,1024]{1,0:T(8,128)(2,1)S(1)} collective-permute-done((bf16[256,1024]{1,0:T(8,128)(2,1)S(1)}, bf16[256,1024]{1,0:T(8,128)(2,1)S(1)}, u32[]{:S(2)}, u32[]{:S(2)}) %collective-permute-start.10) | collective-permute-done | bytes 524320 | tf_op jit(solution)/shard_map/ppermute | solution.py:55
  126.2 13.4 %collective-permute-done.18.before = bf16[64,2048]{1,0:T(8,128)(2,1)S(1)} collective-permute-done((bf16[64,2048]{1,0:T(8,128)(2,1)S(1)}, bf16[64,2048]{1,0:T(8,128)(2,1)S(1)}, u32[]{:S(2)}, u32[]{:S(2)}) %collective-permute-start.18) | collective-permute-done | bytes 262176 | tf_op jit(solution)/shard_map/ppermute | solution.py:55
  151.7 10.0 %shard_map.166 = (bf16[256,1024]{1,0:T(8,128)(2,1)S(1)}, f32[256,1024]{1,0:T(8,128)S(1)}, bf16[256,1024]{1,0:T(8,128)(2,1)S(1)}) custom-call(s32[8]{0:T(128)S(1)} %stack.71.offs, bf16[256,3072]{1,0:T(8,128)(2,1)S(1)} %copy-done.31, bf16[64,2048]{1,0:T(8,128)(2,1)S(1)} %copy-done.59, bf16[64,2048]{1,0:T(8,128)(2,1)S(1)} %copy-done.62, ...), custom_call_target="tpu_custom_call" | custom-call | tf_op jit(solution)/shard_map/pallas_call | solution.py:148
  185.0 8.3 %collective-permute-done.29 = bf16[128,1024]{1,0:T(8,128)(2,1)S(1)} collective-permute-done((bf16[128,1024]{1,0:T(8,128)(2,1)S(1)}, bf16[128,1024]{1,0:T(8,128)(2,1)S(1)}, u32[]{:S(2)}, u32[]{:S(2)}) %collective-permute-start.29) | collective-permute-done | bytes 262176 | tf_op jit(solution)/shard_map/ppermute | solution.py:55
  205.2 8.5 %collective-permute-done.34 = bf16[128,1024]{1,0:T(8,128)(2,1)S(1)} collective-permute-done((bf16[128,1024]{1,0:T(8,128)(2,1)S(1)}, bf16[128,1024]{1,0:T(8,128)(2,1)S(1)}, u32[]{:S(2)}, u32[]{:S(2)}) %collective-permute-start.34) | collective-permute-done | bytes 262176 | tf_op jit(solution)/shard_map/ppermute | solution.py:55
  230.3 17.7 %collective-permute-done.38.before = bf16[64,2048]{1,0:T(8,128)(2,1)S(1)} collective-permute-done((bf16[64,2048]{1,0:T(8,128)(2,1)S(1)}, bf16[64,2048]{1,0:T(8,128)(2,1)S(1)}, u32[]{:S(2)}, u32[]{:S(2)}) %collective-permute-start.38) | collective-permute-done | bytes 262176 | tf_op jit(solution)/shard_map/ppermute | solution.py:55
  251.3 9.7 %shard_map.172 = (bf16[256,1024]{1,0:T(8,128)(2,1)S(1)}, f32[256,1024]{1,0:T(8,128)S(1)}, bf16[256,1024]{1,0:T(8,128)(2,1)S(1)}) custom-call(s32[8]{0:T(128)S(1)} %stack.71.offs, bf16[256,3072]{1,0:T(8,128)(2,1)S(1)} %get-tuple-element.440.qkv, bf16[64,2048]{1,0:T(8,128)(2,1)S(1)} %collective-permute-done.38.before, ...), custom_call_target="tpu_custom_call" | custom-call | tf_op jit(solution)/shard_map/pallas_call | solution.py:148
  287.5 10.0 %collective-permute-done.45 = bf16[128,1024]{1,0:T(8,128)(2,1)S(1)} collective-permute-done((bf16[128,1024]{1,0:T(8,128)(2,1)S(1)}, bf16[128,1024]{1,0:T(8,128)(2,1)S(1)}, u32[]{:S(2)}, u32[]{:S(2)}) %collective-permute-start.45) | collective-permute-done | bytes 262176 | tf_op jit(solution)/shard_map/ppermute | solution.py:55
  302.1 9.9 %collective-permute-done.48 = bf16[128,1024]{1,0:T(8,128)(2,1)S(1)} collective-permute-done((bf16[128,1024]{1,0:T(8,128)(2,1)S(1)}, bf16[128,1024]{1,0:T(8,128)(2,1)S(1)}, u32[]{:S(2)}, u32[]{:S(2)}) %collective-permute-start.48) | collective-permute-done | bytes 262176 | tf_op jit(solution)/shard_map/ppermute | solution.py:55
  323.9 14.0 %shard_map.182 = (bf16[256,1024]{1,0:T(8,128)(2,1)S(1)}, f32[256,2048]{1,0:T(8,128)S(1)}, bf16[64,2048]{1,0:T(8,128)(2,1)S(1)}, bf16[64,2048]{1,0:T(8,128)(2,1)S(1)}) custom-call(s32[8]{0:T(128)S(1)} %stack.71.offs, bf16[256,1024]{1,0:T(8,128)(2,1)S(1)} %get-tuple-element.489.middle_grad, bf16[256,3072]{1,0:T(8,128)(2,1)S(1)} %get-tuple-element.440.qkv, ...), custom_call_target="tpu_custom_call" | custom-call | tf_op jit(solution)/shard_map/pallas_call | solution.py:148
  343.8 9.9 %collective-permute-done.52.arrived_first = bf16[64,2048]{1,0:T(8,128)(2,1)S(1)} collective-permute-done((bf16[64,2048]{1,0:T(8,128)(2,1)S(1)}, bf16[64,2048]{1,0:T(8,128)(2,1)S(1)}, u32[]{:S(2)}, u32[]{:S(2)}) %collective-permute-start.52) | collective-permute-done | bytes 262176 | tf_op jit(solution)/shard_map/ppermute | solution.py:55
  384.5 7.6 %collective-permute-done.55.refs_16_ = bf16[384,1536]{1,0:T(8,128)(2,1)} collective-permute-done((bf16[384,1536]{1,0:T(8,128)(2,1)}, bf16[384,1536]{1,0:T(8,128)(2,1)}, u32[]{:S(2)}, u32[]{:S(2)}) %collective-permute-start.55) | collective-permute-done | bytes 1179680 | tf_op jit(solution)/shard_map/ppermute | solution.py:55
  412.9 14.7 %collective-permute-done.59.refs_12_ = bf16[384,1536]{1,0:T(8,128)(2,1)S(1)} collective-permute-done((bf16[384,1536]{1,0:T(8,128)(2,1)S(1)}, bf16[384,1536]{1,0:T(8,128)(2,1)S(1)}, u32[]{:S(2)}, u32[]{:S(2)}) %collective-permute-start.59) | collective-permute-done | bytes 1179680 | tf_op jit(solution)/shard_map/ppermute | solution.py:55
  435.6 11.3 %collective-permute-done.66.refs_19_ = bf16[32,3072]{1,0:T(8,128)(2,1)S(1)} collective-permute-done((bf16[32,3072]{1,0:T(8,128)(2,1)S(1)}, bf16[32,3072]{1,0:T(8,128)(2,1)S(1)}, u32[]{:S(2)}, u32[]{:S(2)}) %collective-permute-start.66) | collective-permute-done | bytes 196640 | tf_op jit(solution)/shard_map/ppermute | solution.py:55
  451.2 6.7 collective-permute-done.65.refs_17_
  475.5 14.0 %shard_map.191 = (bf16[256,1024]{1,0:T(8,128)(2,1)S(1)}, f32[256,2048]{1,0:T(8,128)S(1)}, bf16[64,2048]{1,0:T(8,128)(2,1)S(1)}, bf16[64,2048]{1,0:T(8,128)(2,1)S(1)}) custom-call(s32[8]{0:T(128)S(1)} %stack.71.offs, bf16[256,1024]{1,0:T(8,128)(2,1)S(1)} %get-tuple-element.556.middle_grad, bf16[256,3072]{1,0:T(8,128)(2,1)S(1)} %copy-done.32, ...), custom_call_target="tpu_custom_call" | custom-call | tf_op jit(solution)/shard_map/pallas_call | solution.py:148
  501.5 9.1 %collective-permute-done.75.arrived_last = bf16[64,2048]{1,0:T(8,128)(2,1)S(1)} collective-permute-done((bf16[64,2048]{1,0:T(8,128)(2,1)S(1)}, bf16[64,2048]{1,0:T(8,128)(2,1)S(1)}, u32[]{:S(2)}, u32[]{:S(2)}) %collective-permute-start.75) | collective-permute-done | bytes 262176 | tf_op jit(solution)/shard_map/ppermute | solution.py:55
  564.2 12.4 %collective-permute-done.84.refs_17_ = bf16[32,3072]{1,0:T(8,128)(2,1)S(1)} collective-permute-done((bf16[32,3072]{1,0:T(8,128)(2,1)S(1)}, bf16[32,3072]{1,0:T(8,128)(2,1)S(1)}, u32[]{:S(2)}, u32[]{:S(2)}) %collective-permute-start.84) | collective-permute-done | bytes 196640 | tf_op jit(solution)/shard_map/ppermute | solution.py:55
  580.2 11.0 %collective-permute-done.86 = bf16[128,1024]{1,0:T(8,128)(2,1)S(1)} collective-permute-done((bf16[128,1024]{1,0:T(8,128)(2,1)S(1)}, bf16[128,1024]{1,0:T(8,128)(2,1)S(1)}, u32[]{:S(2)}, u32[]{:S(2)}) %collective-permute-start.86) | collective-permute-done | bytes 262176 | tf_op jit(solution)/shard_map/ppermute | solution.py:55
  603.2 10.6 %collective-permute-done.90.refs_9_ = bf16[32,3072]{1,0:T(8,128)(2,1)S(1)} collective-permute-done((bf16[32,3072]{1,0:T(8,128)(2,1)S(1)}, bf16[32,3072]{1,0:T(8,128)(2,1)S(1)}, u32[]{:S(2)}, u32[]{:S(2)}) %collective-permute-start.90) | collective-permute-done | bytes 196640 | tf_op jit(solution)/shard_map/ppermute | solution.py:55
  642.3 10.7 %collective-permute-done.100 = bf16[128,1024]{1,0:T(8,128)(2,1)S(1)} collective-permute-done((bf16[128,1024]{1,0:T(8,128)(2,1)S(1)}, bf16[128,1024]{1,0:T(8,128)(2,1)S(1)}, u32[]{:S(2)}, u32[]{:S(2)}) %collective-permute-start.100) | collective-permute-done | bytes 262176 | tf_op jit(solution)/shard_map/ppermute | solution.py:55
  (730 shorter events, 404.2 us)
Async XLA Ops:
  3.9 39.3 %collective-permute-start.2 = (bf16[256,3072]{1,0:T(8,128)(2,1)}, bf16[256,3072]{1,0:T(8,128)(2,1)}, u32[]{:S(2)}, u32[]{:S(2)}) collective-permute-start(bf16[256,3072]{1,0:T(8,128)(2,1)} %get-tuple-element.355.p0), channel_id=1, source_target_pairs={{0,1},{1,0},{2,3},{3,2},{4,5},{5,4},{6,7},{7,6},{8,9},{9,8},{10,11... | collective-permute-start | bytes 4718600 | tf_op jit(solution)/shard_map/ppermute | solution.py:55
  43.1 31.1 %collective-permute-start.8 = (bf16[256,3072]{1,0:T(8,128)(2,1)}, bf16[256,3072]{1,0:T(8,128)(2,1)}, u32[]{:S(2)}, u32[]{:S(2)}) collective-permute-start(bf16[256,3072]{1,0:T(8,128)(2,1)} %copy-done.33), channel_id=1, source_target_pairs={{0,1},{1,0},{2,3},{3,2},{4,5},{5,4},{6,7},{7,6},{8,9},{9,8},{10,11... | collective-permute-start | bytes 4718600 | tf_op jit(solution)/shard_map/ppermute | solution.py:55
  74.3 32.8 %collective-permute-start.13 = (bf16[256,3072]{1,0:T(8,128)(2,1)S(1)}, bf16[256,3072]{1,0:T(8,128)(2,1)}, u32[]{:S(2)}, u32[]{:S(2)}) collective-permute-start(bf16[256,3072]{1,0:T(8,128)(2,1)S(1)} %constant_dynamic-update-slice_fusion.p1), channel_id=1, source_target_pairs={{0,1},{1,0},{2,3},{3,2},{4,5},{5,4},{6,7},{7,6},{8,9},{9,8},{10,11... | collective-permute-start | bytes 4718600 | tf_op jit(solution)/shard_map/ppermute | solution.py:55
  75.2 31.8 %collective-permute-start.14 = (bf16[256,3072]{1,0:T(8,128)(2,1)}, bf16[256,3072]{1,0:T(8,128)(2,1)}, u32[]{:S(2)}, u32[]{:S(2)}) collective-permute-start(bf16[256,3072]{1,0:T(8,128)(2,1)} %get-tuple-element.378.p0), channel_id=1, source_target_pairs={{0,1},{1,0},{2,3},{3,2},{4,5},{5,4},{6,7},{7,6},{8,9},{9,8},{10,11... | collective-permute-start | bytes 4718600 | tf_op jit(solution)/shard_map/ppermute | solution.py:55
  107.2 32.5 %collective-permute-start.17 = (bf16[256,2944]{1,0:T(8,128)(2,1)S(1)}, bf16[256,2944]{1,0:T(8,128)(2,1)S(1)}, u32[]{:S(2)}, u32[]{:S(2)}) collective-permute-start(bf16[256,2944]{1,0:T(8,128)(2,1)S(1)} %constant_dynamic-update-slice_fusion.2.p1), channel_id=1, source_target_pairs={{0,1},{1,0},{2,3},{3,2},{4,5},{5,4},{6,7},{7,6},{8,9},{9,8},{10,11... | collective-permute-start | bytes 4521992 | tf_op jit(solution)/shard_map/ppermute | solution.py:55
  109.9 29.8 %collective-permute-start.15 = (bf16[128,3072]{1,0:T(8,128)(2,1)}, bf16[128,3072]{1,0:T(8,128)(2,1)S(1)}, u32[]{:S(2)}, u32[]{:S(2)}) collective-permute-start(bf16[128,3072]{1,0:T(8,128)(2,1)} %copy-done.133), channel_id=1, source_target_pairs={{0,2},{1,3},{2,0},{3,1},{4,6},{5,7},{6,4},{7,5},{8,10},{9,11},{10,... | collective-permute-start | bytes 2359304 | tf_op jit(solution)/shard_map/ppermute | solution.py:55
  140.8 29.7 %collective-permute-start.22 = (bf16[256,3072]{1,0:T(8,128)(2,1)}, bf16[256,3072]{1,0:T(8,128)(2,1)}, u32[]{:S(2)}, u32[]{:S(2)}) collective-permute-start(bf16[256,3072]{1,0:T(8,128)(2,1)} %constant_dynamic-update-slice_fusion.4.p1), channel_id=1, source_target_pairs={{0,1},{1,0},{2,3},{3,2},{4,5},{5,4},{6,7},{7,6},{8,9},{9,8},{10,11... | collective-permute-start | bytes 4718600 | tf_op jit(solution)/shard_map/ppermute | solution.py:55
  218.2 29.9 %collective-permute-start.37 = (bf16[256,2944]{1,0:T(8,128)(2,1)S(1)}, bf16[256,2944]{1,0:T(8,128)(2,1)S(1)}, u32[]{:S(2)}, u32[]{:S(2)}) collective-permute-start(bf16[256,2944]{1,0:T(8,128)(2,1)S(1)} %constant_dynamic-update-slice_fusion.10.p1), channel_id=1, source_target_pairs={{0,1},{1,0},{2,3},{3,2},{4,5},{5,4},{6,7},{7,6},{8,9},{9,8},{10,11... | collective-permute-start | bytes 4521992 | tf_op jit(solution)/shard_map/ppermute | solution.py:55
  218.2 29.8 %collective-permute-start.35 = (bf16[128,3072]{1,0:T(8,128)(2,1)S(1)}, bf16[128,3072]{1,0:T(8,128)(2,1)S(1)}, u32[]{:S(2)}, u32[]{:S(2)}) collective-permute-start(bf16[128,3072]{1,0:T(8,128)(2,1)S(1)} %copy-done.129), channel_id=1, source_target_pairs={{0,2},{1,3},{2,0},{3,1},{4,6},{5,7},{6,4},{7,5},{8,10},{9,11},{10,... | collective-permute-start | bytes 2359304 | tf_op jit(solution)/shard_map/ppermute | solution.py:55
  312.0 43.1 %collective-permute-start.51 = (bf16[256,3072]{1,0:T(8,128)(2,1)S(1)}, bf16[256,3072]{1,0:T(8,128)(2,1)S(1)}, u32[]{:S(2)}, u32[]{:S(2)}) collective-permute-start(bf16[256,3072]{1,0:T(8,128)(2,1)S(1)} %get-tuple-element.503.refs_0_.refs_1_), channel_id=1, source_target_pairs={{0,1},{1,0},{2,3},{3,2},{4,5},{5,4},{6,7},{7,6},{8,9},{9,8},{10,11... | collective-permute-start | bytes 4718600 | tf_op jit(solution)/shard_map/ppermute | solution.py:55
  314.9 40.2 %collective-permute-start.49 = (bf16[256,1536]{1,0:T(8,128)(2,1)S(1)}, bf16[256,1536]{1,0:T(8,128)(2,1)S(1)}, u32[]{:S(2)}, u32[]{:S(2)}) collective-permute-start(bf16[256,1536]{1,0:T(8,128)(2,1)S(1)} %get-tuple-element.482), channel_id=1, source_target_pairs={{0,2},{1,3},{2,0},{3,1},{4,6},{5,7},{6,4},{7,5},{8,10},{9,11},{10,... | collective-permute-start | bytes 2359304 | tf_op jit(solution)/shard_map/ppermute | solution.py:55
  316.0 39.2 %collective-permute-start.50 = (bf16[256,1536]{1,0:T(8,128)(2,1)S(1)}, bf16[256,1536]{1,0:T(8,128)(2,1)S(1)}, u32[]{:S(2)}, u32[]{:S(2)}) collective-permute-start(bf16[256,1536]{1,0:T(8,128)(2,1)S(1)} %get-tuple-element.484), channel_id=1, source_target_pairs={{0,4},{1,5},{2,6},{3,7},{4,0},{5,1},{6,2},{7,3},{8,12},{9,13},{10,... | collective-permute-start | bytes 2359304 | tf_op jit(solution)/shard_map/ppermute | solution.py:55
  355.1 38.4 %collective-permute-start.57 = (bf16[256,3072]{1,0:T(8,128)(2,1)}, bf16[256,3072]{1,0:T(8,128)(2,1)}, u32[]{:S(2)}, u32[]{:S(2)}) collective-permute-start(bf16[256,3072]{1,0:T(8,128)(2,1)} %get-tuple-element.513.refs_0_.refs_1_), channel_id=1, source_target_pairs={{0,1},{1,0},{2,3},{3,2},{4,5},{5,4},{6,7},{7,6},{8,9},{9,8},{10,11... | collective-permute-start | bytes 4718600 | tf_op jit(solution)/shard_map/ppermute | solution.py:55
  393.6 34.7 %collective-permute-start.62 = (bf16[256,3072]{1,0:T(8,128)(2,1)S(1)}, bf16[256,3072]{1,0:T(8,128)(2,1)S(1)}, u32[]{:S(2)}, u32[]{:S(2)}) collective-permute-start(bf16[256,3072]{1,0:T(8,128)(2,1)S(1)} %get-tuple-element.531.refs_0_.refs_1_), channel_id=1, source_target_pairs={{0,1},{1,0},{2,3},{3,2},{4,5},{5,4},{6,7},{7,6},{8,9},{9,8},{10,11... | collective-permute-start | bytes 4718600 | tf_op jit(solution)/shard_map/ppermute | solution.py:55
  428.3 33.6 %collective-permute-start.67 = (bf16[256,3072]{1,0:T(8,128)(2,1)S(1)}, bf16[256,3072]{1,0:T(8,128)(2,1)S(1)}, u32[]{:S(2)}, u32[]{:S(2)}) collective-permute-start(bf16[256,3072]{1,0:T(8,128)(2,1)S(1)} %get-tuple-element.558.refs_0_.refs_1_), channel_id=1, source_target_pairs={{0,1},{1,0},{2,3},{3,2},{4,5},{5,4},{6,7},{7,6},{8,9},{9,8},{10,11... | collective-permute-start | bytes 4718600 | tf_op jit(solution)/shard_map/ppermute | solution.py:55
  461.9 49.5 %collective-permute-start.73 = (bf16[256,3072]{1,0:T(8,128)(2,1)S(1)}, bf16[256,3072]{1,0:T(8,128)(2,1)S(1)}, u32[]{:S(2)}, u32[]{:S(2)}) collective-permute-start(bf16[256,3072]{1,0:T(8,128)(2,1)S(1)} %get-tuple-element.585.refs_0_.refs_1_), channel_id=1, source_target_pairs={{0,1},{1,0},{2,3},{3,2},{4,5},{5,4},{6,7},{7,6},{8,9},{9,8},{10,11... | collective-permute-start | bytes 4718600 | tf_op jit(solution)/shard_map/ppermute | solution.py:55
  466.2 45.1 %collective-permute-start.69 = (bf16[384,1536]{1,0:T(8,128)(2,1)S(1)}, bf16[384,1536]{1,0:T(8,128)(2,1)S(1)}, u32[]{:S(2)}, u32[]{:S(2)}) collective-permute-start(bf16[384,1536]{1,0:T(8,128)(2,1)S(1)} %get-tuple-element.568), channel_id=1, source_target_pairs={{0,2},{1,3},{2,0},{3,1},{4,6},{5,7},{6,4},{7,5},{8,10},{9,11},{10,... | collective-permute-start | bytes 3538952 | tf_op jit(solution)/shard_map/ppermute | solution.py:55
  467.3 44.1 %collective-permute-start.70 = (bf16[384,1536]{1,0:T(8,128)(2,1)S(1)}, bf16[384,1536]{1,0:T(8,128)(2,1)S(1)}, u32[]{:S(2)}, u32[]{:S(2)}) collective-permute-start(bf16[384,1536]{1,0:T(8,128)(2,1)S(1)} %get-tuple-element.570), channel_id=1, source_target_pairs={{0,4},{1,5},{2,6},{3,7},{4,0},{5,1},{6,2},{7,3},{8,12},{9,13},{10,... | collective-permute-start | bytes 3538952 | tf_op jit(solution)/shard_map/ppermute | solution.py:55
  511.4 42.4 %collective-permute-start.80 = (bf16[256,3072]{1,0:T(8,128)(2,1)}, bf16[256,3072]{1,0:T(8,128)(2,1)}, u32[]{:S(2)}, u32[]{:S(2)}) collective-permute-start(bf16[256,3072]{1,0:T(8,128)(2,1)} %get-tuple-element.602.refs_0_.refs_1_), channel_id=1, source_target_pairs={{0,1},{1,0},{2,3},{3,2},{4,5},{5,4},{6,7},{7,6},{8,9},{9,8},{10,11... | collective-permute-start | bytes 4718600 | tf_op jit(solution)/shard_map/ppermute | solution.py:55
  523.8 30.0 %collective-permute-start.77 = (bf16[384,1536]{1,0:T(8,128)(2,1)}, bf16[384,1536]{1,0:T(8,128)(2,1)}, u32[]{:S(2)}, u32[]{:S(2)}) collective-permute-start(bf16[384,1536]{1,0:T(8,128)(2,1)} %get-tuple-element.595), channel_id=1, source_target_pairs={{0,4},{1,5},{2,6},{3,7},{4,0},{5,1},{6,2},{7,3},{8,12},{9,13},{10,... | collective-permute-start | bytes 3538952 | tf_op jit(solution)/shard_map/ppermute | solution.py:55
  553.7 37.5 %collective-permute-start.85 = (bf16[256,3072]{1,0:T(8,128)(2,1)S(1)}, bf16[256,3072]{1,0:T(8,128)(2,1)S(1)}, u32[]{:S(2)}, u32[]{:S(2)}) collective-permute-start(bf16[256,3072]{1,0:T(8,128)(2,1)S(1)} %get-tuple-element.620.refs_0_.refs_1_), channel_id=1, source_target_pairs={{0,1},{1,0},{2,3},{3,2},{4,5},{5,4},{6,7},{7,6},{8,9},{9,8},{10,11... | collective-permute-start | bytes 4718600 | tf_op jit(solution)/shard_map/ppermute | solution.py:55
  559.6 31.6 %collective-permute-start.81 = (bf16[384,1536]{1,0:T(8,128)(2,1)S(1)}, bf16[384,1536]{1,0:T(8,128)(2,1)S(1)}, u32[]{:S(2)}, u32[]{:S(2)}) collective-permute-start(bf16[384,1536]{1,0:T(8,128)(2,1)S(1)} %get-tuple-element.610), channel_id=1, source_target_pairs={{0,2},{1,3},{2,0},{3,1},{4,6},{5,7},{6,4},{7,5},{8,10},{9,11},{10,... | collective-permute-start | bytes 3538952 | tf_op jit(solution)/shard_map/ppermute | solution.py:55
  560.7 30.5 %collective-permute-start.82 = (bf16[384,1536]{1,0:T(8,128)(2,1)S(1)}, bf16[384,1536]{1,0:T(8,128)(2,1)S(1)}, u32[]{:S(2)}, u32[]{:S(2)}) collective-permute-start(bf16[384,1536]{1,0:T(8,128)(2,1)S(1)} %get-tuple-element.612), channel_id=1, source_target_pairs={{0,4},{1,5},{2,6},{3,7},{4,0},{5,1},{6,2},{7,3},{8,12},{9,13},{10,... | collective-permute-start | bytes 3538952 | tf_op jit(solution)/shard_map/ppermute | solution.py:55
  595.8 30.2 %collective-permute-start.87 = (bf16[384,1536]{1,0:T(8,128)(2,1)S(1)}, bf16[384,1536]{1,0:T(8,128)(2,1)S(1)}, u32[]{:S(2)}, u32[]{:S(2)}) collective-permute-start(bf16[384,1536]{1,0:T(8,128)(2,1)S(1)} %get-tuple-element.628), channel_id=1, source_target_pairs={{0,2},{1,3},{2,0},{3,1},{4,6},{5,7},{6,4},{7,5},{8,10},{9,11},{10,... | collective-permute-start | bytes 3538952 | tf_op jit(solution)/shard_map/ppermute | solution.py:55
  (277 other events, 3494.7 us)

commit v5 on v4

--- a/solution.py
+++ b/solution.py
@@ -304,6 +304,11 @@
     )(offs, x, gain, cosine, sine, *pieces)
 
 
+def stacked(rows, low):
+    zero = jnp.zeros_like(rows)
+    return jnp.concatenate([jnp.where(low, rows, zero), jnp.where(low, zero, rows)], axis=0)
+
+
 def extend(qkv, before, after, extended):
     tokens, features = qkv.shape[0], qkv.shape[1] // 3
     extended[:HALO, :] = before[...]
@@ -317,7 +322,7 @@
 ):
     tokens, features = x.shape
     extend(qkv, before, after, extended)
-    scale = 1.0 / math.sqrt(HEAD_DIM)
+    scale = jnp.asarray(1.0 / math.sqrt(HEAD_DIM), BF16)
     span = BLOCK + 2 * HALO
     row = lax.broadcasted_iota(jnp.int32, (BLOCK, span), 0)
     col = lax.broadcasted_iota(jnp.int32, (BLOCK, span), 1)
@@ -327,7 +332,8 @@
     for block in range(tokens // BLOCK):
         base = block * BLOCK
         same = seg_q[base : base + BLOCK, :] == seg_k[:, base : base + span]
-        bias.append(jnp.where(near & same, 0.0, NEG))
+        one = jnp.where(near & same, 0.0, NEG)
+        bias.append(jnp.concatenate([one, one], axis=0))
 
     def pair(index, carry):
         lanes = pl.ds(pl.multiple_of(index * LANES, LANES), LANES)
@@ -337,15 +343,14 @@
             queries = qkv[base : base + BLOCK, lanes]
             keys = extended[base : base + span, lanes]
             values = extended[base : base + span, value_lanes]
-            parts = []
-            for keep in (low, ~low):
-                chosen = jnp.where(keep, queries, jnp.zeros_like(queries))
-                raw = lax.dot_general(chosen, keys, NT, preferred_element_type=F32)
-                scores = raw * scale + bias[block]
-                expo = jnp.exp(scores - jnp.max(scores, axis=-1, keepdims=True))
-                probs = expo * (1.0 / jnp.sum(expo, axis=-1, keepdims=True))
-                parts.append(jnp.dot(probs.astype(BF16), values, preferred_element_type=F32))
-            mixed[base : base + BLOCK, lanes] = jnp.where(low, parts[0], parts[1]).astype(BF16)
+            scores = (
+                lax.dot_general(stacked(queries * scale, low), keys, NT, preferred_element_type=F32)
+                + bias[block]
+            )
+            expo = jnp.exp(scores - jnp.max(scores, axis=-1, keepdims=True))
+            probs = expo * (1.0 / jnp.sum(expo, axis=-1, keepdims=True))
+            both = jnp.dot(probs.astype(BF16), values, preferred_element_type=F32)
+            mixed[base : base + BLOCK, lanes] = jnp.where(low, both[:BLOCK], both[BLOCK:]).astype(BF16)
         return carry
 
     lax.fori_loop(0, features // LANES, pair, 0)
@@ -516,7 +521,7 @@
     for k in range(features // LANES):
         lanes = pl.ds(pl.multiple_of(offs[k] * LANES, LANES), LANES)
         mixed_grad[:, lanes] = placed[:, k * LANES : (k + 1) * LANES]
-    scale = 1.0 / math.sqrt(HEAD_DIM)
+    scale = jnp.asarray(1.0 / math.sqrt(HEAD_DIM), BF16)
     span = BLOCK + 2 * HALO
     row = lax.broadcasted_iota(jnp.int32, (span, BLOCK), 1)
     col = lax.broadcasted_iota(jnp.int32, (span, BLOCK), 0)
@@ -526,7 +531,8 @@
     for block in range(tokens // BLOCK):
         base = block * BLOCK
         same = seg_q[:, base : base + BLOCK] == seg_k[base : base + span, :]
-        bias.append(jnp.where(near & same, 0.0, NEG))
+        one = jnp.where(near & same, 0.0, NEG)
+        bias.append(jnp.concatenate([one, one], axis=1))
 
     def pair(index, carry):
         lanes = pl.ds(pl.multiple_of(index * LANES, LANES), LANES)
@@ -540,29 +546,20 @@
             grads = mixed_grad[here, lanes]
             keys = extended[base : base + span, lanes]
             values = extended[base : base + span, value_lanes]
-            key_sum = None
-            value_sum = None
-            query_parts = []
-            for keep in (low, ~low):
-                chosen = jnp.where(keep, queries, jnp.zeros_like(queries))
-                chosen_grad = jnp.where(keep, grads, jnp.zeros_like(grads))
-                raw = lax.dot_general(keys, chosen, NT, preferred_element_type=F32)
-                scores = raw * scale + bias[block]
-                expo = jnp.exp(scores - jnp.max(scores, axis=0, keepdims=True))
-                probs = expo * (1.0 / jnp.sum(expo, axis=0, keepdims=True))
-                prob_grad = lax.dot_general(values, chosen_grad, NT, preferred_element_type=F32)
-                delta = jnp.sum(prob_grad * probs, axis=0, keepdims=True)
-                score_grad = (probs * (prob_grad - delta) * scale).astype(BF16)
-                query_parts.append(
-                    lax.dot_general(score_grad, keys, TN, preferred_element_type=F32)
-                )
-                to_keys = jnp.dot(score_grad, chosen, preferred_element_type=F32)
-                to_values = jnp.dot(
-                    probs.astype(BF16), chosen_grad, preferred_element_type=F32
-                )
-                key_sum = to_keys if key_sum is None else key_sum + to_keys
-                value_sum = to_values if value_sum is None else value_sum + to_values
-            joint = jnp.where(low, query_parts[0], query_parts[1])
+            chosen = stacked(queries * scale, low)
+            chosen_grad = stacked(grads, low)
+            scores = (
+                lax.dot_general(keys, chosen, NT, preferred_element_type=F32) + bias[block]
+            )
+            expo = jnp.exp(scores - jnp.max(scores, axis=0, keepdims=True))
+            probs = expo * (1.0 / jnp.sum(expo, axis=0, keepdims=True))
+            prob_grad = lax.dot_general(values, chosen_grad, NT, preferred_element_type=F32)
+            delta = jnp.sum(prob_grad * probs, axis=0, keepdims=True)
+            score_grad = (probs * (prob_grad - delta)).astype(BF16)
+            both = lax.dot_general(score_grad, keys, TN, preferred_element_type=F32)
+            key_sum = jnp.dot(score_grad, chosen, preferred_element_type=F32)
+            value_sum = jnp.dot(probs.astype(BF16), chosen_grad, preferred_element_type=F32)
+            joint = jnp.where(low, both[:BLOCK], both[BLOCK:]) * (1.0 / math.sqrt(HEAD_DIM))
             query_grad[here, lanes] = turn_chunk(
                 joint, cosine[here, :], sine[here, :], -1
             ).astype(BF16)
@@ -994,7 +991,7 @@
     tok_route, cot_route = Route(tokens[0], False), Route(cotangent[0], False, levels - 1)
 
     first_use = 3
-    owns = {0: (0, 1), 1: (2,), 2: (3,), 4: (4, 5), 5: (6,), 6: (7,)}
+    owns = {0: (0,), 1: (1, 3), 2: (2,), 4: (4,), 5: (5,), 6: (6,), 8: (7,)}
     phase = 0
 
     def transfers():
@@ -1011,9 +1008,8 @@
     while phase < first_use or tok_route.levels:
         transfers()
         tok_route.step()
-        if phase < 2:
+        if phase == 0:
             cot_route.step()
-        if phase == 0:
             flow.keep(*(item.shard for item in items[1:]))
         phase += 1
         flow.next()
@@ -1033,6 +1029,8 @@
         phase += 1
         flow.next()
         transfers()
+        if layer == 0:
+            cot_route.step()
         if layer and kept[-1][-1] is None:
             kept[-1][-1] = (mine, flow.swap(theirs, 0))
         start = residual

time: 688 us -> 666 us (0.968)
  Pallas kernels: 175 us -> 161 us
  waiting for transfers between devices: 281 us -> 272 us
    pallas_call x40, Pallas kernels: 175 us -> 161 us  [run(): pl.pallas_call(kernel, in_specs=specs, out_specs=results, **params)(*args)]
    ppermute x110, waiting for transfers between devices: 281 us -> 272 us  [route(): result = lax.ppermute(self.tie(value), axes, pairs)]
    unnamed x391 -> x373, local copies, waits for them, and re-layouts: 69 us -> 66.5 us
  transfers between devices with their start and end apart: 110 -> 110, of which waited for: 43 -> 42; matrix products, arithmetic and copies ran while one was open for 5% -> 5% of each run, Pallas kernels for 24% -> 23%
where the time goes in v5:
time: 666 us; the launch traced here: 658 us
  waiting for transfers between devices  272 us (41%)
  Pallas kernels  161 us (24%)
  starting transfers between devices  115 us (17%)
  local copies, waits for them, and re-layouts  73.9 us (11%)
  other arithmetic  20.1 us (3%)
  between operations  8.18 us (1%)
    ppermute x110, waiting for transfers between devices, route(): result = lax.ppermute(self.tie(value), axes, pairs)  272 us
    pallas_call x40, Pallas kernels, run(): pl.pallas_call(kernel, in_specs=specs, out_specs=results, **params)(*args)  161 us
    ppermute x110, starting transfers between devices, route(): result = lax.ppermute(self.tie(value), axes, pairs)  115 us
    unnamed x373, local copies, waits for them, and re-layouts  66.5 us
  transfers between devices with their start and end apart: 110, of which 42 were waited for; matrix products, arithmetic and copies ran while one was open for 5% of the time, Pallas kernels for 23%

profile of v5, /device:TPU:0, one launch (start us, length us, event | category | flops | bytes accessed | tf_op | source)
XLA Modules:
  0.0 658.1 jit_solution(14069223141791002207)
XLA Ops:
  46.8 9.9 %collective-permute-done.4 = bf16[256,1024]{1,0:T(8,128)(2,1)S(1)} collective-permute-done((bf16[256,1024]{1,0:T(8,128)(2,1)S(1)}, bf16[256,1024]{1,0:T(8,128)(2,1)S(1)}, u32[]{:S(2)}, u32[]{:S(2)}) %collective-permute-start.4) | collective-permute-done | bytes 524320 | tf_op jit(solution)/shard_map/ppermute | solution.py:55
  71.7 21.1 %collective-permute-done.9 = bf16[256,1024]{1,0:T(8,128)(2,1)S(1)} collective-permute-done((bf16[256,1024]{1,0:T(8,128)(2,1)S(1)}, bf16[256,1024]{1,0:T(8,128)(2,1)S(1)}, u32[]{:S(2)}, u32[]{:S(2)}) %collective-permute-start.9) | collective-permute-done | bytes 524320 | tf_op jit(solution)/shard_map/ppermute | solution.py:55
  110.2 14.4 %collective-permute-done.17.before = bf16[64,2048]{1,0:T(8,128)(2,1)S(1)} collective-permute-done((bf16[64,2048]{1,0:T(8,128)(2,1)S(1)}, bf16[64,2048]{1,0:T(8,128)(2,1)S(1)}, u32[]{:S(2)}, u32[]{:S(2)}) %collective-permute-start.17) | collective-permute-done | bytes 262176 | tf_op jit(solution)/shard_map/ppermute | solution.py:55
  138.7 10.2 %shard_map.166 = (bf16[256,1024]{1,0:T(8,128)(2,1)S(1)}, f32[256,1024]{1,0:T(8,128)S(1)}, bf16[256,1024]{1,0:T(8,128)(2,1)S(1)}) custom-call(s32[8]{0:T(128)S(1)} %stack.71.offs, bf16[256,3072]{1,0:T(8,128)(2,1)S(1)} %copy-done.32, bf16[64,2048]{1,0:T(8,128)(2,1)S(1)} %copy-done.58, bf16[64,2048]{1,0:T(8,128)(2,1)S(1)} %copy-done.61, ...), custom_call_target="tpu_custom_call" | custom-call | tf_op jit(solution)/shard_map/pallas_call | solution.py:148
  217.0 18.8 %collective-permute-done.37.before = bf16[64,2048]{1,0:T(8,128)(2,1)S(1)} collective-permute-done((bf16[64,2048]{1,0:T(8,128)(2,1)S(1)}, bf16[64,2048]{1,0:T(8,128)(2,1)S(1)}, u32[]{:S(2)}, u32[]{:S(2)}) %collective-permute-start.37) | collective-permute-done | bytes 262176 | tf_op jit(solution)/shard_map/ppermute | solution.py:55
  239.2 9.3 %shard_map.172 = (bf16[256,1024]{1,0:T(8,128)(2,1)S(1)}, f32[256,1024]{1,0:T(8,128)S(1)}, bf16[256,1024]{1,0:T(8,128)(2,1)S(1)}) custom-call(s32[8]{0:T(128)S(1)} %stack.71.offs, bf16[256,3072]{1,0:T(8,128)(2,1)S(1)} %get-tuple-element.441.qkv, bf16[64,2048]{1,0:T(8,128)(2,1)S(1)} %collective-permute-done.37.before, ...), custom_call_target="tpu_custom_call" | custom-call | tf_op jit(solution)/shard_map/pallas_call | solution.py:148
  250.7 6.5 collective-permute-done.39
  276.3 8.3 %collective-permute-done.45 = bf16[128,1024]{1,0:T(8,128)(2,1)S(1)} collective-permute-done((bf16[128,1024]{1,0:T(8,128)(2,1)S(1)}, bf16[128,1024]{1,0:T(8,128)(2,1)S(1)}, u32[]{:S(2)}, u32[]{:S(2)}) %collective-permute-start.45) | collective-permute-done | bytes 262176 | tf_op jit(solution)/shard_map/ppermute | solution.py:55
  287.9 11.5 %collective-permute-done.48 = bf16[128,1024]{1,0:T(8,128)(2,1)S(1)} collective-permute-done((bf16[128,1024]{1,0:T(8,128)(2,1)S(1)}, bf16[128,1024]{1,0:T(8,128)(2,1)S(1)}, u32[]{:S(2)}, u32[]{:S(2)}) %collective-permute-start.48) | collective-permute-done | bytes 262176 | tf_op jit(solution)/shard_map/ppermute | solution.py:55
  307.9 10.1 %shard_map.182 = (bf16[256,1024]{1,0:T(8,128)(2,1)S(1)}, f32[256,2048]{1,0:T(8,128)S(1)}, bf16[64,2048]{1,0:T(8,128)(2,1)S(1)}, bf16[64,2048]{1,0:T(8,128)(2,1)S(1)}) custom-call(s32[8]{0:T(128)S(1)} %stack.71.offs, bf16[256,1024]{1,0:T(8,128)(2,1)S(1)} %get-tuple-element.491.middle_grad, bf16[256,3072]{1,0:T(8,128)(2,1)S(1)} %get-tuple-element.441.qkv, ...), custom_call_target="tpu_custom_call" | custom-call | tf_op jit(solution)/shard_map/pallas_call | solution.py:148
  324.3 9.9 %collective-permute-done.52.arrived_first = bf16[64,2048]{1,0:T(8,128)(2,1)S(1)} collective-permute-done((bf16[64,2048]{1,0:T(8,128)(2,1)S(1)}, bf16[64,2048]{1,0:T(8,128)(2,1)S(1)}, u32[]{:S(2)}, u32[]{:S(2)}) %collective-permute-start.52) | collective-permute-done | bytes 262176 | tf_op jit(solution)/shard_map/ppermute | solution.py:55
  364.9 7.7 %collective-permute-done.55.refs_16_ = bf16[384,1536]{1,0:T(8,128)(2,1)} collective-permute-done((bf16[384,1536]{1,0:T(8,128)(2,1)}, bf16[384,1536]{1,0:T(8,128)(2,1)}, u32[]{:S(2)}, u32[]{:S(2)}) %collective-permute-start.55) | collective-permute-done | bytes 1179680 | tf_op jit(solution)/shard_map/ppermute | solution.py:55
  393.4 14.6 %collective-permute-done.59.refs_12_ = bf16[384,1536]{1,0:T(8,128)(2,1)S(1)} collective-permute-done((bf16[384,1536]{1,0:T(8,128)(2,1)S(1)}, bf16[384,1536]{1,0:T(8,128)(2,1)S(1)}, u32[]{:S(2)}, u32[]{:S(2)}) %collective-permute-start.59) | collective-permute-done | bytes 1179680 | tf_op jit(solution)/shard_map/ppermute | solution.py:55
  416.0 10.5 %collective-permute-done.66.refs_19_ = bf16[32,3072]{1,0:T(8,128)(2,1)S(1)} collective-permute-done((bf16[32,3072]{1,0:T(8,128)(2,1)S(1)}, bf16[32,3072]{1,0:T(8,128)(2,1)S(1)}, u32[]{:S(2)}, u32[]{:S(2)}) %collective-permute-start.66) | collective-permute-done | bytes 196640 | tf_op jit(solution)/shard_map/ppermute | solution.py:55
  455.6 10.7 %shard_map.191 = (bf16[256,1024]{1,0:T(8,128)(2,1)S(1)}, f32[256,2048]{1,0:T(8,128)S(1)}, bf16[64,2048]{1,0:T(8,128)(2,1)S(1)}, bf16[64,2048]{1,0:T(8,128)(2,1)S(1)}) custom-call(s32[8]{0:T(128)S(1)} %stack.71.offs, bf16[256,1024]{1,0:T(8,128)(2,1)S(1)} %get-tuple-element.558.middle_grad, bf16[256,3072]{1,0:T(8,128)(2,1)S(1)} %copy-done.33, ...), custom_call_target="tpu_custom_call" | custom-call | tf_op jit(solution)/shard_map/pallas_call | solution.py:148
  472.6 8.2 %collective-permute-done.74.arrived_first = bf16[64,2048]{1,0:T(8,128)(2,1)S(1)} collective-permute-done((bf16[64,2048]{1,0:T(8,128)(2,1)S(1)}, bf16[64,2048]{1,0:T(8,128)(2,1)S(1)}, u32[]{:S(2)}, u32[]{:S(2)}) %collective-permute-start.74) | collective-permute-done | bytes 262176 | tf_op jit(solution)/shard_map/ppermute | solution.py:55
  482.0 8.9 %collective-permute-done.75.arrived_last = bf16[64,2048]{1,0:T(8,128)(2,1)S(1)} collective-permute-done((bf16[64,2048]{1,0:T(8,128)(2,1)S(1)}, bf16[64,2048]{1,0:T(8,128)(2,1)S(1)}, u32[]{:S(2)}, u32[]{:S(2)}) %collective-permute-start.75) | collective-permute-done | bytes 262176 | tf_op jit(solution)/shard_map/ppermute | solution.py:55
  515.6 6.4 shard_map.193
  522.1 9.2 %collective-permute-done.76.refs_16_ = bf16[384,1536]{1,0:T(8,128)(2,1)} collective-permute-done((bf16[384,1536]{1,0:T(8,128)(2,1)}, bf16[384,1536]{1,0:T(8,128)(2,1)}, u32[]{:S(2)}, u32[]{:S(2)}) %collective-permute-start.76) | collective-permute-done | bytes 1179680 | tf_op jit(solution)/shard_map/ppermute | solution.py:55
  541.8 12.7 %collective-permute-done.84.refs_17_ = bf16[32,3072]{1,0:T(8,128)(2,1)S(1)} collective-permute-done((bf16[32,3072]{1,0:T(8,128)(2,1)S(1)}, bf16[32,3072]{1,0:T(8,128)(2,1)S(1)}, u32[]{:S(2)}, u32[]{:S(2)}) %collective-permute-start.84) | collective-permute-done | bytes 196640 | tf_op jit(solution)/shard_map/ppermute | solution.py:55
  558.1 11.3 %collective-permute-done.86 = bf16[128,1024]{1,0:T(8,128)(2,1)S(1)} collective-permute-done((bf16[128,1024]{1,0:T(8,128)(2,1)S(1)}, bf16[128,1024]{1,0:T(8,128)(2,1)S(1)}, u32[]{:S(2)}, u32[]{:S(2)}) %collective-permute-start.86) | collective-permute-done | bytes 262176 | tf_op jit(solution)/shard_map/ppermute | solution.py:55
  580.6 10.6 %collective-permute-done.90.refs_9_ = bf16[32,3072]{1,0:T(8,128)(2,1)S(1)} collective-permute-done((bf16[32,3072]{1,0:T(8,128)(2,1)S(1)}, bf16[32,3072]{1,0:T(8,128)(2,1)S(1)}, u32[]{:S(2)}, u32[]{:S(2)}) %collective-permute-start.90) | collective-permute-done | bytes 196640 | tf_op jit(solution)/shard_map/ppermute | solution.py:55
  594.6 6.9 %collective-permute-done.91 = bf16[128,1024]{1,0:T(8,128)(2,1)S(1)} collective-permute-done((bf16[128,1024]{1,0:T(8,128)(2,1)S(1)}, bf16[128,1024]{1,0:T(8,128)(2,1)S(1)}, u32[]{:S(2)}, u32[]{:S(2)}) %collective-permute-start.91) | collective-permute-done | bytes 262176 | tf_op jit(solution)/shard_map/ppermute | solution.py:55
  620.4 10.8 %collective-permute-done.100 = bf16[128,1024]{1,0:T(8,128)(2,1)S(1)} collective-permute-done((bf16[128,1024]{1,0:T(8,128)(2,1)S(1)}, bf16[128,1024]{1,0:T(8,128)(2,1)S(1)}, u32[]{:S(2)}, u32[]{:S(2)}) %collective-permute-start.100) | collective-permute-done | bytes 262176 | tf_op jit(solution)/shard_map/ppermute | solution.py:55
  (712 shorter events, 391.6 us)
Async XLA Ops:
  3.9 31.1 %collective-permute-start.2 = (bf16[256,3072]{1,0:T(8,128)(2,1)}, bf16[256,3072]{1,0:T(8,128)(2,1)}, u32[]{:S(2)}, u32[]{:S(2)}) collective-permute-start(bf16[256,3072]{1,0:T(8,128)(2,1)} %get-tuple-element.356.p0), channel_id=1, source_target_pairs={{0,1},{1,0},{2,3},{3,2},{4,5},{5,4},{6,7},{7,6},{8,9},{9,8},{10,11... | collective-permute-start | bytes 4718600 | tf_op jit(solution)/shard_map/ppermute | solution.py:55
  4.3 30.7 %collective-permute-start.1 = (bf16[128,3072]{1,0:T(8,128)(2,1)S(1)}, bf16[128,3072]{1,0:T(8,128)(2,1)}, u32[]{:S(2)}, u32[]{:S(2)}) collective-permute-start(bf16[128,3072]{1,0:T(8,128)(2,1)S(1)} %get-tuple-element.355), channel_id=1, source_target_pairs={{0,2},{1,3},{2,0},{3,1},{4,6},{5,7},{6,4},{7,5},{8,10},{9,11},{10,... | collective-permute-start | bytes 2359304 | tf_op jit(solution)/shard_map/ppermute | solution.py:55
  60.9 31.9 %collective-permute-start.12 = (bf16[256,3072]{1,0:T(8,128)(2,1)}, bf16[256,3072]{1,0:T(8,128)(2,1)}, u32[]{:S(2)}, u32[]{:S(2)}) collective-permute-start(bf16[256,3072]{1,0:T(8,128)(2,1)} %constant_dynamic-update-slice_fusion.p1), channel_id=1, source_target_pairs={{0,1},{1,0},{2,3},{3,2},{4,5},{5,4},{6,7},{7,6},{8,9},{9,8},{10,11... | collective-permute-start | bytes 4718600 | tf_op jit(solution)/shard_map/ppermute | solution.py:55
  60.9 31.9 %collective-permute-start.13 = (bf16[256,3072]{1,0:T(8,128)(2,1)}, bf16[256,3072]{1,0:T(8,128)(2,1)}, u32[]{:S(2)}, u32[]{:S(2)}) collective-permute-start(bf16[256,3072]{1,0:T(8,128)(2,1)} %get-tuple-element.378.p0), channel_id=1, source_target_pairs={{0,1},{1,0},{2,3},{3,2},{4,5},{5,4},{6,7},{7,6},{8,9},{9,8},{10,11... | collective-permute-start | bytes 4718600 | tf_op jit(solution)/shard_map/ppermute | solution.py:55
  92.9 31.8 %collective-permute-start.16 = (bf16[256,2944]{1,0:T(8,128)(2,1)S(1)}, bf16[256,2944]{1,0:T(8,128)(2,1)}, u32[]{:S(2)}, u32[]{:S(2)}) collective-permute-start(bf16[256,2944]{1,0:T(8,128)(2,1)S(1)} %constant_dynamic-update-slice_fusion.2.p1), channel_id=1, source_target_pairs={{0,1},{1,0},{2,3},{3,2},{4,5},{5,4},{6,7},{7,6},{8,9},{9,8},{10,11... | collective-permute-start | bytes 4521992 | tf_op jit(solution)/shard_map/ppermute | solution.py:55
  125.7 30.7 %collective-permute-start.21 = (bf16[256,3072]{1,0:T(8,128)(2,1)}, bf16[256,3072]{1,0:T(8,128)(2,1)}, u32[]{:S(2)}, u32[]{:S(2)}) collective-permute-start(bf16[256,3072]{1,0:T(8,128)(2,1)} %constant_dynamic-update-slice_fusion.4.p1), channel_id=1, source_target_pairs={{0,1},{1,0},{2,3},{3,2},{4,5},{5,4},{6,7},{7,6},{8,9},{9,8},{10,11... | collective-permute-start | bytes 4718600 | tf_op jit(solution)/shard_map/ppermute | solution.py:55
  125.7 30.7 %collective-permute-start.22 = (bf16[256,3072]{1,0:T(8,128)(2,1)}, bf16[256,3072]{1,0:T(8,128)(2,1)}, u32[]{:S(2)}, u32[]{:S(2)}) collective-permute-start(bf16[256,3072]{1,0:T(8,128)(2,1)} %get-tuple-element.402.p0), channel_id=1, source_target_pairs={{0,1},{1,0},{2,3},{3,2},{4,5},{5,4},{6,7},{7,6},{8,9},{9,8},{10,11... | collective-permute-start | bytes 4718600 | tf_op jit(solution)/shard_map/ppermute | solution.py:55
  204.9 31.0 %collective-permute-start.36 = (bf16[256,2944]{1,0:T(8,128)(2,1)S(1)}, bf16[256,2944]{1,0:T(8,128)(2,1)S(1)}, u32[]{:S(2)}, u32[]{:S(2)}) collective-permute-start(bf16[256,2944]{1,0:T(8,128)(2,1)S(1)} %constant_dynamic-update-slice_fusion.10.p1), channel_id=1, source_target_pairs={{0,1},{1,0},{2,3},{3,2},{4,5},{5,4},{6,7},{7,6},{8,9},{9,8},{10,11... | collective-permute-start | bytes 4521992 | tf_op jit(solution)/shard_map/ppermute | solution.py:55
  205.0 30.9 %collective-permute-start.34 = (bf16[128,3072]{1,0:T(8,128)(2,1)S(1)}, bf16[128,3072]{1,0:T(8,128)(2,1)S(1)}, u32[]{:S(2)}, u32[]{:S(2)}) collective-permute-start(bf16[128,3072]{1,0:T(8,128)(2,1)S(1)} %copy-done.128), channel_id=1, source_target_pairs={{0,2},{1,3},{2,0},{3,1},{4,6},{5,7},{6,4},{7,5},{8,10},{9,11},{10,... | collective-permute-start | bytes 2359304 | tf_op jit(solution)/shard_map/ppermute | solution.py:55
  206.0 29.9 %collective-permute-start.35 = (bf16[128,3072]{1,0:T(8,128)(2,1)S(1)}, bf16[128,3072]{1,0:T(8,128)(2,1)S(1)}, u32[]{:S(2)}, u32[]{:S(2)}) collective-permute-start(bf16[128,3072]{1,0:T(8,128)(2,1)S(1)} %collective-permute-done.29), channel_id=1, source_target_pairs={{0,4},{1,5},{2,6},{3,7},{4,0},{5,1},{6,2},{7,3},{8,12},{9,13},{10,... | collective-permute-start | bytes 2359304 | tf_op jit(solution)/shard_map/ppermute | solution.py:55
  299.4 36.2 %collective-permute-start.51 = (bf16[256,3072]{1,0:T(8,128)(2,1)S(1)}, bf16[256,3072]{1,0:T(8,128)(2,1)S(1)}, u32[]{:S(2)}, u32[]{:S(2)}) collective-permute-start(bf16[256,3072]{1,0:T(8,128)(2,1)S(1)} %get-tuple-element.505.refs_0_.refs_1_), channel_id=1, source_target_pairs={{0,1},{1,0},{2,3},{3,2},{4,5},{5,4},{6,7},{7,6},{8,9},{9,8},{10,11... | collective-permute-start | bytes 4718600 | tf_op jit(solution)/shard_map/ppermute | solution.py:55
  302.3 33.3 %collective-permute-start.49 = (bf16[256,1536]{1,0:T(8,128)(2,1)S(1)}, bf16[256,1536]{1,0:T(8,128)(2,1)S(1)}, u32[]{:S(2)}, u32[]{:S(2)}) collective-permute-start(bf16[256,1536]{1,0:T(8,128)(2,1)S(1)} %get-tuple-element.484), channel_id=1, source_target_pairs={{0,2},{1,3},{2,0},{3,1},{4,6},{5,7},{6,4},{7,5},{8,10},{9,11},{10,... | collective-permute-start | bytes 2359304 | tf_op jit(solution)/shard_map/ppermute | solution.py:55
  303.5 32.2 %collective-permute-start.50 = (bf16[256,1536]{1,0:T(8,128)(2,1)S(1)}, bf16[256,1536]{1,0:T(8,128)(2,1)S(1)}, u32[]{:S(2)}, u32[]{:S(2)}) collective-permute-start(bf16[256,1536]{1,0:T(8,128)(2,1)S(1)} %get-tuple-element.486), channel_id=1, source_target_pairs={{0,4},{1,5},{2,6},{3,7},{4,0},{5,1},{6,2},{7,3},{8,12},{9,13},{10,... | collective-permute-start | bytes 2359304 | tf_op jit(solution)/shard_map/ppermute | solution.py:55
  335.7 38.3 %collective-permute-start.57 = (bf16[256,3072]{1,0:T(8,128)(2,1)}, bf16[256,3072]{1,0:T(8,128)(2,1)}, u32[]{:S(2)}, u32[]{:S(2)}) collective-permute-start(bf16[256,3072]{1,0:T(8,128)(2,1)} %get-tuple-element.515.refs_0_.refs_1_), channel_id=1, source_target_pairs={{0,1},{1,0},{2,3},{3,2},{4,5},{5,4},{6,7},{7,6},{8,9},{9,8},{10,11... | collective-permute-start | bytes 4718600 | tf_op jit(solution)/shard_map/ppermute | solution.py:55
  374.0 34.8 %collective-permute-start.62 = (bf16[256,3072]{1,0:T(8,128)(2,1)S(1)}, bf16[256,3072]{1,0:T(8,128)(2,1)S(1)}, u32[]{:S(2)}, u32[]{:S(2)}) collective-permute-start(bf16[256,3072]{1,0:T(8,128)(2,1)S(1)} %get-tuple-element.533.refs_0_.refs_1_), channel_id=1, source_target_pairs={{0,1},{1,0},{2,3},{3,2},{4,5},{5,4},{6,7},{7,6},{8,9},{9,8},{10,11... | collective-permute-start | bytes 4718600 | tf_op jit(solution)/shard_map/ppermute | solution.py:55
  408.8 33.5 %collective-permute-start.67 = (bf16[256,3072]{1,0:T(8,128)(2,1)S(1)}, bf16[256,3072]{1,0:T(8,128)(2,1)S(1)}, u32[]{:S(2)}, u32[]{:S(2)}) collective-permute-start(bf16[256,3072]{1,0:T(8,128)(2,1)S(1)} %get-tuple-element.560.refs_0_.refs_1_), channel_id=1, source_target_pairs={{0,1},{1,0},{2,3},{3,2},{4,5},{5,4},{6,7},{7,6},{8,9},{9,8},{10,11... | collective-permute-start | bytes 4718600 | tf_op jit(solution)/shard_map/ppermute | solution.py:55
  442.3 48.7 %collective-permute-start.73 = (bf16[256,3072]{1,0:T(8,128)(2,1)S(1)}, bf16[256,3072]{1,0:T(8,128)(2,1)S(1)}, u32[]{:S(2)}, u32[]{:S(2)}) collective-permute-start(bf16[256,3072]{1,0:T(8,128)(2,1)S(1)} %get-tuple-element.587.refs_0_.refs_1_), channel_id=1, source_target_pairs={{0,1},{1,0},{2,3},{3,2},{4,5},{5,4},{6,7},{7,6},{8,9},{9,8},{10,11... | collective-permute-start | bytes 4718600 | tf_op jit(solution)/shard_map/ppermute | solution.py:55
  446.6 44.3 %collective-permute-start.69 = (bf16[384,1536]{1,0:T(8,128)(2,1)S(1)}, bf16[384,1536]{1,0:T(8,128)(2,1)S(1)}, u32[]{:S(2)}, u32[]{:S(2)}) collective-permute-start(bf16[384,1536]{1,0:T(8,128)(2,1)S(1)} %get-tuple-element.570), channel_id=1, source_target_pairs={{0,2},{1,3},{2,0},{3,1},{4,6},{5,7},{6,4},{7,5},{8,10},{9,11},{10,... | collective-permute-start | bytes 3538952 | tf_op jit(solution)/shard_map/ppermute | solution.py:55
  447.8 43.2 %collective-permute-start.70 = (bf16[384,1536]{1,0:T(8,128)(2,1)S(1)}, bf16[384,1536]{1,0:T(8,128)(2,1)S(1)}, u32[]{:S(2)}, u32[]{:S(2)}) collective-permute-start(bf16[384,1536]{1,0:T(8,128)(2,1)S(1)} %get-tuple-element.572), channel_id=1, source_target_pairs={{0,4},{1,5},{2,6},{3,7},{4,0},{5,1},{6,2},{7,3},{8,12},{9,13},{10,... | collective-permute-start | bytes 3538952 | tf_op jit(solution)/shard_map/ppermute | solution.py:55
  491.0 41.8 %collective-permute-start.80 = (bf16[256,3072]{1,0:T(8,128)(2,1)}, bf16[256,3072]{1,0:T(8,128)(2,1)}, u32[]{:S(2)}, u32[]{:S(2)}) collective-permute-start(bf16[256,3072]{1,0:T(8,128)(2,1)} %get-tuple-element.604.refs_0_.refs_1_), channel_id=1, source_target_pairs={{0,1},{1,0},{2,3},{3,2},{4,5},{5,4},{6,7},{7,6},{8,9},{9,8},{10,11... | collective-permute-start | bytes 4718600 | tf_op jit(solution)/shard_map/ppermute | solution.py:55
  532.8 36.6 %collective-permute-start.85 = (bf16[256,3072]{1,0:T(8,128)(2,1)S(1)}, bf16[256,3072]{1,0:T(8,128)(2,1)S(1)}, u32[]{:S(2)}, u32[]{:S(2)}) collective-permute-start(bf16[256,3072]{1,0:T(8,128)(2,1)S(1)} %get-tuple-element.622.refs_0_.refs_1_), channel_id=1, source_target_pairs={{0,1},{1,0},{2,3},{3,2},{4,5},{5,4},{6,7},{7,6},{8,9},{9,8},{10,11... | collective-permute-start | bytes 4718600 | tf_op jit(solution)/shard_map/ppermute | solution.py:55
  538.6 30.7 %collective-permute-start.81 = (bf16[384,1536]{1,0:T(8,128)(2,1)S(1)}, bf16[384,1536]{1,0:T(8,128)(2,1)S(1)}, u32[]{:S(2)}, u32[]{:S(2)}) collective-permute-start(bf16[384,1536]{1,0:T(8,128)(2,1)S(1)} %get-tuple-element.612), channel_id=1, source_target_pairs={{0,2},{1,3},{2,0},{3,1},{4,6},{5,7},{6,4},{7,5},{8,10},{9,11},{10,... | collective-permute-start | bytes 3538952 | tf_op jit(solution)/shard_map/ppermute | solution.py:55
  539.8 29.6 %collective-permute-start.82 = (bf16[384,1536]{1,0:T(8,128)(2,1)S(1)}, bf16[384,1536]{1,0:T(8,128)(2,1)S(1)}, u32[]{:S(2)}, u32[]{:S(2)}) collective-permute-start(bf16[384,1536]{1,0:T(8,128)(2,1)S(1)} %get-tuple-element.614), channel_id=1, source_target_pairs={{0,4},{1,5},{2,6},{3,7},{4,0},{5,1},{6,2},{7,3},{8,12},{9,13},{10,... | collective-permute-start | bytes 3538952 | tf_op jit(solution)/shard_map/ppermute | solution.py:55
  574.0 30.0 %collective-permute-start.87 = (bf16[384,1536]{1,0:T(8,128)(2,1)S(1)}, bf16[384,1536]{1,0:T(8,128)(2,1)S(1)}, u32[]{:S(2)}, u32[]{:S(2)}) collective-permute-start(bf16[384,1536]{1,0:T(8,128)(2,1)S(1)} %get-tuple-element.630), channel_id=1, source_target_pairs={{0,2},{1,3},{2,0},{3,1},{4,6},{5,7},{6,4},{7,5},{8,10},{9,11},{10,... | collective-permute-start | bytes 3538952 | tf_op jit(solution)/shard_map/ppermute | solution.py:55
  (268 other events, 3489.9 us)

commit v6 on v5

--- a/solution.py
+++ b/solution.py
@@ -773,7 +773,7 @@
     def busy(self):
         return any((self.kept, self.last, self.near_pair, self.far_pair))
 
-    def step(self, rights=None, segments=()):
+    def step(self, rights=None, segments=(), after=()):
         flow, rows, width = self.flow, self.rows, self.width
         tile = width // TILES
         args, specs, outs, out_specs = [], [], [], []
@@ -842,6 +842,8 @@
         result = results.pop(0) if self.far_pair else None
         self.kept, self.last = keep, stay
         self.come = send and [flow.swap(value, 1 + path) for path, value in enumerate(send)]
+        if near:
+            near[1] = lax.optimization_barrier((near[1],) + after)[0]
         self.near_pair = near and [near[0], flow.swap(near[1], self.near)]
         self.far_pair = far and [far[0], flow.swap(far[1], self.far)]
         return result
@@ -1122,13 +1124,14 @@
         nonlocal made, ready
         flow.next()
         moving = bool(made or ready or exchange.busy())
-        if ready or exchange.busy():
-            settle(exchange.step(*(group(*ready) if ready else ())))
-        ready = None
+        now, ready, after = ready, None, ()
         if made:
             right, parts = made
-            ready = ((right, flow.swap(right, 0)), parts)
+            after = (flow.swap(right, 0),)
+            ready = ((right,) + after, parts)
         made = None
+        if now or exchange.busy():
+            settle(exchange.step(*(group(*now) if now else (None, ())), after))
         step_endings()
         return moving
 
@@ -1151,8 +1154,11 @@
             elif not upstream_left:
                 far = flow.swap(theirs, 0)
                 upstream_left += [(mine, far, path) for path in range(2)]
-            if layer == LAYERS - 1 and chunk:
-                out_routes[CHUNKS - 1 - chunk].step()
+            if layer == LAYERS - 1 and chunk == CHUNKS - 1:
+                out_routes[0].step()
+            elif layer == LAYERS - 2 and chunk == CHUNKS - 1:
+                for route in out_routes:
+                    route.step()
             args = (offs, flow.tie(upstream_b), hidden[chunk], carried)
             columns = WIDTHS[chunk]
             parts = [
@@ -1181,8 +1187,7 @@
             gains_a[layer], middle_grad, items[base].pieces,
         )
         if layer:
-            for route in out_routes:
-                route.step()
+            out_routes[1].step()
         flow.keep(upstream_b, right)
         made = (right, [(2 * width, (normed_x, normed_y))])
         terms[layer] = (attn_term, mlp_term)

time: 666 us -> 665 us (level)
  waiting for transfers between devices: 272 us -> 259 us
  starting transfers between devices: 115 us -> 124 us
    ppermute x110, waiting for transfers between devices: 272 us -> 259 us  [route(): result = lax.ppermute(self.tie(value), axes, pairs)]
    ppermute x110, starting transfers between devices: 115 us -> 124 us  [route(): result = lax.ppermute(self.tie(value), axes, pairs)]
    unnamed x373 -> x363, local copies, waits for them, and re-layouts: 66.5 us -> 68.7 us
  transfers between devices with their start and end apart: 110 -> 110, of which waited for: 42 -> 46; matrix products, arithmetic and copies ran while one was open for 5% -> 6% of each run, Pallas kernels for 23% -> 23%
where the time goes in v6:
time: 665 us; the launch traced here: 657 us
  waiting for transfers between devices  259 us (39%)
  Pallas kernels  160 us (24%)
  starting transfers between devices  124 us (19%)
  local copies, waits for them, and re-layouts  77.4 us (12%)
  other arithmetic  20.2 us (3%)
  between operations  8.07 us (1%)
    ppermute x110, waiting for transfers between devices, route(): result = lax.ppermute(self.tie(value), axes, pairs)  259 us
    pallas_call x40, Pallas kernels, run(): pl.pallas_call(kernel, in_specs=specs, out_specs=results, **params)(*args)  160 us
    ppermute x110, starting transfers between devices, route(): result = lax.ppermute(self.tie(value), axes, pairs)  124 us
    unnamed x363, local copies, waits for them, and re-layouts  68.7 us
  transfers between devices with their start and end apart: 110, of which 46 were waited for; matrix products, arithmetic and copies ran while one was open for 6% of the time, Pallas kernels for 23%

profile of v6, /device:TPU:0, one launch (start us, length us, event | category | flops | bytes accessed | tf_op | source)
XLA Modules:
  0.0 656.6 jit_solution(4856237731183801556)
XLA Ops:
  47.1 10.1 %collective-permute-done.4 = bf16[256,1024]{1,0:T(8,128)(2,1)S(1)} collective-permute-done((bf16[256,1024]{1,0:T(8,128)(2,1)S(1)}, bf16[256,1024]{1,0:T(8,128)(2,1)S(1)}, u32[]{:S(2)}, u32[]{:S(2)}) %collective-permute-start.4) | collective-permute-done | bytes 524320 | tf_op jit(solution)/shard_map/ppermute | solution.py:55
  72.0 21.1 %collective-permute-done.9 = bf16[256,1024]{1,0:T(8,128)(2,1)S(1)} collective-permute-done((bf16[256,1024]{1,0:T(8,128)(2,1)S(1)}, bf16[256,1024]{1,0:T(8,128)(2,1)S(1)}, u32[]{:S(2)}, u32[]{:S(2)}) %collective-permute-start.9) | collective-permute-done | bytes 524320 | tf_op jit(solution)/shard_map/ppermute | solution.py:55
  98.7 6.2 shard_map.165
  110.7 14.4 %collective-permute-done.17.before = bf16[64,2048]{1,0:T(8,128)(2,1)S(1)} collective-permute-done((bf16[64,2048]{1,0:T(8,128)(2,1)S(1)}, bf16[64,2048]{1,0:T(8,128)(2,1)S(1)}, u32[]{:S(2)}, u32[]{:S(2)}) %collective-permute-start.17) | collective-permute-done | bytes 262176 | tf_op jit(solution)/shard_map/ppermute | solution.py:55
  139.1 10.2 %shard_map.166 = (bf16[256,1024]{1,0:T(8,128)(2,1)S(1)}, f32[256,1024]{1,0:T(8,128)S(1)}, bf16[256,1024]{1,0:T(8,128)(2,1)S(1)}) custom-call(s32[8]{0:T(128)S(1)} %stack.71.offs, bf16[256,3072]{1,0:T(8,128)(2,1)S(1)} %copy-done.28, bf16[64,2048]{1,0:T(8,128)(2,1)S(1)} %copy-done.64, bf16[64,2048]{1,0:T(8,128)(2,1)S(1)} %copy-done.67, ...), custom_call_target="tpu_custom_call" | custom-call | tf_op jit(solution)/shard_map/pallas_call | solution.py:148
  217.4 18.8 %collective-permute-done.37.before = bf16[64,2048]{1,0:T(8,128)(2,1)S(1)} collective-permute-done((bf16[64,2048]{1,0:T(8,128)(2,1)S(1)}, bf16[64,2048]{1,0:T(8,128)(2,1)S(1)}, u32[]{:S(2)}, u32[]{:S(2)}) %collective-permute-start.37) | collective-permute-done | bytes 262176 | tf_op jit(solution)/shard_map/ppermute | solution.py:55
  239.6 9.3 %shard_map.172 = (bf16[256,1024]{1,0:T(8,128)(2,1)S(1)}, f32[256,1024]{1,0:T(8,128)S(1)}, bf16[256,1024]{1,0:T(8,128)(2,1)S(1)}) custom-call(s32[8]{0:T(128)S(1)} %stack.71.offs, bf16[256,3072]{1,0:T(8,128)(2,1)S(1)} %get-tuple-element.446.qkv, bf16[64,2048]{1,0:T(8,128)(2,1)S(1)} %collective-permute-done.37.before, ...), custom_call_target="tpu_custom_call" | custom-call | tf_op jit(solution)/shard_map/pallas_call | solution.py:148
  251.2 6.5 collective-permute-done.39
  277.0 8.2 %collective-permute-done.45 = bf16[128,1024]{1,0:T(8,128)(2,1)S(1)} collective-permute-done((bf16[128,1024]{1,0:T(8,128)(2,1)S(1)}, bf16[128,1024]{1,0:T(8,128)(2,1)S(1)}, u32[]{:S(2)}, u32[]{:S(2)}) %collective-permute-start.45) | collective-permute-done | bytes 262176 | tf_op jit(solution)/shard_map/ppermute | solution.py:55
  296.9 10.1 %shard_map.182 = (bf16[256,1024]{1,0:T(8,128)(2,1)S(1)}, f32[256,2048]{1,0:T(8,128)S(1)}, bf16[64,2048]{1,0:T(8,128)(2,1)S(1)}, bf16[64,2048]{1,0:T(8,128)(2,1)S(1)}) custom-call(s32[8]{0:T(128)S(1)} %stack.71.offs, bf16[256,1024]{1,0:T(8,128)(2,1)S(1)} %get-tuple-element.496.middle_grad, bf16[256,3072]{1,0:T(8,128)(2,1)S(1)} %get-tuple-element.446.qkv, ...), custom_call_target="tpu_custom_call" | custom-call | tf_op jit(solution)/shard_map/pallas_call | solution.py:148
  311.9 10.3 %collective-permute-done.51.arrived_first = bf16[64,2048]{1,0:T(8,128)(2,1)S(1)} collective-permute-done((bf16[64,2048]{1,0:T(8,128)(2,1)S(1)}, bf16[64,2048]{1,0:T(8,128)(2,1)S(1)}, u32[]{:S(2)}, u32[]{:S(2)}) %collective-permute-start.51) | collective-permute-done | bytes 262176 | tf_op jit(solution)/shard_map/ppermute | solution.py:55
  329.8 5.9 shard_map.184
  336.7 7.2 %collective-permute-done.56 = bf16[128,1024]{1,0:T(8,128)(2,1)S(1)} collective-permute-done((bf16[128,1024]{1,0:T(8,128)(2,1)S(1)}, bf16[128,1024]{1,0:T(8,128)(2,1)S(1)}, u32[]{:S(2)}, u32[]{:S(2)}) %collective-permute-start.56) | collective-permute-done | bytes 262176 | tf_op jit(solution)/shard_map/ppermute | solution.py:55
  343.9 10.9 %collective-permute-done.54.refs_16_ = bf16[384,1536]{1,0:T(8,128)(2,1)S(1)} collective-permute-done((bf16[384,1536]{1,0:T(8,128)(2,1)S(1)}, bf16[384,1536]{1,0:T(8,128)(2,1)S(1)}, u32[]{:S(2)}, u32[]{:S(2)}) %collective-permute-start.54) | collective-permute-done | bytes 1179680 | tf_op jit(solution)/shard_map/ppermute | solution.py:55
  411.6 6.1 collective-permute-done.67.refs_19_
  417.7 12.1 %collective-permute-done.64.refs_14_ = bf16[384,1536]{1,0:T(8,128)(2,1)S(1)} collective-permute-done((bf16[384,1536]{1,0:T(8,128)(2,1)S(1)}, bf16[384,1536]{1,0:T(8,128)(2,1)S(1)}, u32[]{:S(2)}, u32[]{:S(2)}) %collective-permute-start.64) | collective-permute-done | bytes 1179680 | tf_op jit(solution)/shard_map/ppermute | solution.py:55
  444.2 11.1 %shard_map.191 = (bf16[256,1024]{1,0:T(8,128)(2,1)S(1)}, f32[256,2048]{1,0:T(8,128)S(1)}, bf16[64,2048]{1,0:T(8,128)(2,1)S(1)}, bf16[64,2048]{1,0:T(8,128)(2,1)S(1)}) custom-call(s32[8]{0:T(128)S(1)} %stack.71.offs, bf16[256,1024]{1,0:T(8,128)(2,1)S(1)} %get-tuple-element.565.middle_grad, bf16[256,3072]{1,0:T(8,128)(2,1)S(1)} %copy-done.29, ...), custom_call_target="tpu_custom_call" | custom-call | tf_op jit(solution)/shard_map/pallas_call | solution.py:148
  460.2 14.3 %collective-permute-done.74.arrived_first = bf16[64,2048]{1,0:T(8,128)(2,1)S(1)} collective-permute-done((bf16[64,2048]{1,0:T(8,128)(2,1)S(1)}, bf16[64,2048]{1,0:T(8,128)(2,1)S(1)}, u32[]{:S(2)}, u32[]{:S(2)}) %collective-permute-start.74) | collective-permute-done | bytes 262176 | tf_op jit(solution)/shard_map/ppermute | solution.py:55
  491.5 6.8 %shard_map.193 = (bf16[256,3072]{1,0:T(8,128)(2,1)}, f32[256,1024]{1,0:T(8,128)}, bf16[256,1024]{1,0:T(8,128)(2,1)S(1)}, f32[1,1024]{1,0:T(1,128)S(1)}) custom-call(s32[8]{0:T(128)S(1)} %stack.71.offs, bf16[256,1024]{1,0:T(8,128)(2,1)S(1)} %get-tuple-element.592.query_grad, f32[256,2048]{1,0:T(8,128)S(1)} %get-tuple-element.586.own_grad, ...), custom_call_target="tpu_custom_call" | custom-call | tf_op jit(solution)/shard_map/pallas_call | solution.py:148
  502.8 10.1 %collective-permute-done.77.refs_16_ = bf16[384,1536]{1,0:T(8,128)(2,1)S(1)} collective-permute-done((bf16[384,1536]{1,0:T(8,128)(2,1)S(1)}, bf16[384,1536]{1,0:T(8,128)(2,1)S(1)}, u32[]{:S(2)}, u32[]{:S(2)}) %collective-permute-start.77) | collective-permute-done | bytes 1179680 | tf_op jit(solution)/shard_map/ppermute | solution.py:55
  543.9 13.5 %collective-permute-done.85.refs_17_ = bf16[32,3072]{1,0:T(8,128)(2,1)S(1)} collective-permute-done((bf16[32,3072]{1,0:T(8,128)(2,1)S(1)}, bf16[32,3072]{1,0:T(8,128)(2,1)S(1)}, u32[]{:S(2)}, u32[]{:S(2)}) %collective-permute-start.85) | collective-permute-done | bytes 196640 | tf_op jit(solution)/shard_map/ppermute | solution.py:55
  580.7 9.9 %collective-permute-done.90.refs_9_ = bf16[32,3072]{1,0:T(8,128)(2,1)S(1)} collective-permute-done((bf16[32,3072]{1,0:T(8,128)(2,1)S(1)}, bf16[32,3072]{1,0:T(8,128)(2,1)S(1)}, u32[]{:S(2)}, u32[]{:S(2)}) %collective-permute-start.90) | collective-permute-done | bytes 196640 | tf_op jit(solution)/shard_map/ppermute | solution.py:55
  594.1 7.0 %collective-permute-done.91 = bf16[128,1024]{1,0:T(8,128)(2,1)S(1)} collective-permute-done((bf16[128,1024]{1,0:T(8,128)(2,1)S(1)}, bf16[128,1024]{1,0:T(8,128)(2,1)S(1)}, u32[]{:S(2)}, u32[]{:S(2)}) %collective-permute-start.91) | collective-permute-done | bytes 262176 | tf_op jit(solution)/shard_map/ppermute | solution.py:55
  619.9 9.6 %collective-permute-done.100 = bf16[128,1024]{1,0:T(8,128)(2,1)S(1)} collective-permute-done((bf16[128,1024]{1,0:T(8,128)(2,1)S(1)}, bf16[128,1024]{1,0:T(8,128)(2,1)S(1)}, u32[]{:S(2)}, u32[]{:S(2)}) %collective-permute-start.100) | collective-permute-done | bytes 262176 | tf_op jit(solution)/shard_map/ppermute | solution.py:55
  (702 shorter events, 398.9 us)
Async XLA Ops:
  3.8 31.5 %collective-permute-start.2 = (bf16[256,3072]{1,0:T(8,128)(2,1)}, bf16[256,3072]{1,0:T(8,128)(2,1)}, u32[]{:S(2)}, u32[]{:S(2)}) collective-permute-start(bf16[256,3072]{1,0:T(8,128)(2,1)} %get-tuple-element.361.p0), channel_id=1, source_target_pairs={{0,1},{1,0},{2,3},{3,2},{4,5},{5,4},{6,7},{7,6},{8,9},{9,8},{10,11... | collective-permute-start | bytes 4718600 | tf_op jit(solution)/shard_map/ppermute | solution.py:55
  4.3 31.1 %collective-permute-start.1 = (bf16[128,3072]{1,0:T(8,128)(2,1)S(1)}, bf16[128,3072]{1,0:T(8,128)(2,1)}, u32[]{:S(2)}, u32[]{:S(2)}) collective-permute-start(bf16[128,3072]{1,0:T(8,128)(2,1)S(1)} %get-tuple-element.360), channel_id=1, source_target_pairs={{0,2},{1,3},{2,0},{3,1},{4,6},{5,7},{6,4},{7,5},{8,10},{9,11},{10,... | collective-permute-start | bytes 2359304 | tf_op jit(solution)/shard_map/ppermute | solution.py:55
  61.2 31.9 %collective-permute-start.12 = (bf16[256,3072]{1,0:T(8,128)(2,1)}, bf16[256,3072]{1,0:T(8,128)(2,1)}, u32[]{:S(2)}, u32[]{:S(2)}) collective-permute-start(bf16[256,3072]{1,0:T(8,128)(2,1)} %constant_dynamic-update-slice_fusion.p1), channel_id=1, source_target_pairs={{0,1},{1,0},{2,3},{3,2},{4,5},{5,4},{6,7},{7,6},{8,9},{9,8},{10,11... | collective-permute-start | bytes 4718600 | tf_op jit(solution)/shard_map/ppermute | solution.py:55
  61.2 31.9 %collective-permute-start.13 = (bf16[256,3072]{1,0:T(8,128)(2,1)}, bf16[256,3072]{1,0:T(8,128)(2,1)}, u32[]{:S(2)}, u32[]{:S(2)}) collective-permute-start(bf16[256,3072]{1,0:T(8,128)(2,1)} %get-tuple-element.383.p0), channel_id=1, source_target_pairs={{0,1},{1,0},{2,3},{3,2},{4,5},{5,4},{6,7},{7,6},{8,9},{9,8},{10,11... | collective-permute-start | bytes 4718600 | tf_op jit(solution)/shard_map/ppermute | solution.py:55
  64.4 28.8 %collective-permute-start.10 = (bf16[128,3072]{1,0:T(8,128)(2,1)}, bf16[128,3072]{1,0:T(8,128)(2,1)S(1)}, u32[]{:S(2)}, u32[]{:S(2)}) collective-permute-start(bf16[128,3072]{1,0:T(8,128)(2,1)} %get-tuple-element.379), channel_id=1, source_target_pairs={{0,2},{1,3},{2,0},{3,1},{4,6},{5,7},{6,4},{7,5},{8,10},{9,11},{10,... | collective-permute-start | bytes 2359304 | tf_op jit(solution)/shard_map/ppermute | solution.py:55
  93.3 31.9 %collective-permute-start.16 = (bf16[256,2944]{1,0:T(8,128)(2,1)S(1)}, bf16[256,2944]{1,0:T(8,128)(2,1)}, u32[]{:S(2)}, u32[]{:S(2)}) collective-permute-start(bf16[256,2944]{1,0:T(8,128)(2,1)S(1)} %constant_dynamic-update-slice_fusion.2.p1), channel_id=1, source_target_pairs={{0,1},{1,0},{2,3},{3,2},{4,5},{5,4},{6,7},{7,6},{8,9},{9,8},{10,11... | collective-permute-start | bytes 4521992 | tf_op jit(solution)/shard_map/ppermute | solution.py:55
  96.0 29.2 %collective-permute-start.14 = (bf16[128,3072]{1,0:T(8,128)(2,1)}, bf16[128,3072]{1,0:T(8,128)(2,1)S(1)}, u32[]{:S(2)}, u32[]{:S(2)}) collective-permute-start(bf16[128,3072]{1,0:T(8,128)(2,1)} %copy-done.127), channel_id=1, source_target_pairs={{0,2},{1,3},{2,0},{3,1},{4,6},{5,7},{6,4},{7,5},{8,10},{9,11},{10,... | collective-permute-start | bytes 2359304 | tf_op jit(solution)/shard_map/ppermute | solution.py:55
  126.2 30.6 %collective-permute-start.21 = (bf16[256,3072]{1,0:T(8,128)(2,1)}, bf16[256,3072]{1,0:T(8,128)(2,1)}, u32[]{:S(2)}, u32[]{:S(2)}) collective-permute-start(bf16[256,3072]{1,0:T(8,128)(2,1)} %constant_dynamic-update-slice_fusion.4.p1), channel_id=1, source_target_pairs={{0,1},{1,0},{2,3},{3,2},{4,5},{5,4},{6,7},{7,6},{8,9},{9,8},{10,11... | collective-permute-start | bytes 4718600 | tf_op jit(solution)/shard_map/ppermute | solution.py:55
  126.2 30.6 %collective-permute-start.22 = (bf16[256,3072]{1,0:T(8,128)(2,1)}, bf16[256,3072]{1,0:T(8,128)(2,1)}, u32[]{:S(2)}, u32[]{:S(2)}) collective-permute-start(bf16[256,3072]{1,0:T(8,128)(2,1)} %get-tuple-element.407.p0), channel_id=1, source_target_pairs={{0,1},{1,0},{2,3},{3,2},{4,5},{5,4},{6,7},{7,6},{8,9},{9,8},{10,11... | collective-permute-start | bytes 4718600 | tf_op jit(solution)/shard_map/ppermute | solution.py:55
  205.3 31.0 %collective-permute-start.36 = (bf16[256,2944]{1,0:T(8,128)(2,1)S(1)}, bf16[256,2944]{1,0:T(8,128)(2,1)S(1)}, u32[]{:S(2)}, u32[]{:S(2)}) collective-permute-start(bf16[256,2944]{1,0:T(8,128)(2,1)S(1)} %constant_dynamic-update-slice_fusion.10.p1), channel_id=1, source_target_pairs={{0,1},{1,0},{2,3},{3,2},{4,5},{5,4},{6,7},{7,6},{8,9},{9,8},{10,11... | collective-permute-start | bytes 4521992 | tf_op jit(solution)/shard_map/ppermute | solution.py:55
  205.4 30.9 %collective-permute-start.34 = (bf16[128,3072]{1,0:T(8,128)(2,1)S(1)}, bf16[128,3072]{1,0:T(8,128)(2,1)S(1)}, u32[]{:S(2)}, u32[]{:S(2)}) collective-permute-start(bf16[128,3072]{1,0:T(8,128)(2,1)S(1)} %copy-done.123), channel_id=1, source_target_pairs={{0,2},{1,3},{2,0},{3,1},{4,6},{5,7},{6,4},{7,5},{8,10},{9,11},{10,... | collective-permute-start | bytes 2359304 | tf_op jit(solution)/shard_map/ppermute | solution.py:55
  206.4 29.9 %collective-permute-start.35 = (bf16[128,3072]{1,0:T(8,128)(2,1)S(1)}, bf16[128,3072]{1,0:T(8,128)(2,1)S(1)}, u32[]{:S(2)}, u32[]{:S(2)}) collective-permute-start(bf16[128,3072]{1,0:T(8,128)(2,1)S(1)} %collective-permute-done.29), channel_id=1, source_target_pairs={{0,4},{1,5},{2,6},{3,7},{4,0},{5,1},{6,2},{7,3},{8,12},{9,13},{10,... | collective-permute-start | bytes 2359304 | tf_op jit(solution)/shard_map/ppermute | solution.py:55
  289.4 32.8 %collective-permute-start.48 = (bf16[256,3072]{1,0:T(8,128)(2,1)S(1)}, bf16[256,3072]{1,0:T(8,128)(2,1)S(1)}, u32[]{:S(2)}, u32[]{:S(2)}) collective-permute-start(bf16[256,3072]{1,0:T(8,128)(2,1)S(1)} %get-tuple-element.504.refs_0_.refs_1_), channel_id=1, source_target_pairs={{0,1},{1,0},{2,3},{3,2},{4,5},{5,4},{6,7},{7,6},{8,9},{9,8},{10,11... | collective-permute-start | bytes 4718600 | tf_op jit(solution)/shard_map/ppermute | solution.py:55
  292.3 29.8 %collective-permute-start.49 = (bf16[256,1536]{1,0:T(8,128)(2,1)S(1)}, bf16[256,1536]{1,0:T(8,128)(2,1)S(1)}, u32[]{:S(2)}, u32[]{:S(2)}) collective-permute-start(bf16[256,1536]{1,0:T(8,128)(2,1)S(1)} %get-tuple-element.493), channel_id=1, source_target_pairs={{0,2},{1,3},{2,0},{3,1},{4,6},{5,7},{6,4},{7,5},{8,10},{9,11},{10,... | collective-permute-start | bytes 2359304 | tf_op jit(solution)/shard_map/ppermute | solution.py:55
  293.5 28.7 %collective-permute-start.50 = (bf16[256,1536]{1,0:T(8,128)(2,1)S(1)}, bf16[256,1536]{1,0:T(8,128)(2,1)S(1)}, u32[]{:S(2)}, u32[]{:S(2)}) collective-permute-start(bf16[256,1536]{1,0:T(8,128)(2,1)S(1)} %get-tuple-element.495), channel_id=1, source_target_pairs={{0,4},{1,5},{2,6},{3,7},{4,0},{5,1},{6,2},{7,3},{8,12},{9,13},{10,... | collective-permute-start | bytes 2359304 | tf_op jit(solution)/shard_map/ppermute | solution.py:55
  322.2 34.0 %collective-permute-start.53 = (bf16[256,3072]{1,0:T(8,128)(2,1)S(1)}, bf16[256,3072]{1,0:T(8,128)(2,1)S(1)}, u32[]{:S(2)}, u32[]{:S(2)}) collective-permute-start(bf16[256,3072]{1,0:T(8,128)(2,1)S(1)} %get-tuple-element.523.refs_0_.refs_1_), channel_id=1, source_target_pairs={{0,1},{1,0},{2,3},{3,2},{4,5},{5,4},{6,7},{7,6},{8,9},{9,8},{10,11... | collective-permute-start | bytes 4718600 | tf_op jit(solution)/shard_map/ppermute | solution.py:55
  327.4 28.8 %collective-permute-start.55 = (bf16[384,1536]{1,0:T(8,128)(2,1)S(1)}, bf16[384,1536]{1,0:T(8,128)(2,1)S(1)}, u32[]{:S(2)}, u32[]{:S(2)}) collective-permute-start(bf16[384,1536]{1,0:T(8,128)(2,1)S(1)} %get-tuple-element.510), channel_id=1, source_target_pairs={{0,4},{1,5},{2,6},{3,7},{4,0},{5,1},{6,2},{7,3},{8,12},{9,13},{10,... | collective-permute-start | bytes 3538952 | tf_op jit(solution)/shard_map/ppermute | solution.py:55
  366.1 28.6 %collective-permute-start.59 = (bf16[384,1536]{1,0:T(8,128)(2,1)}, bf16[384,1536]{1,0:T(8,128)(2,1)}, u32[]{:S(2)}, u32[]{:S(2)}) collective-permute-start(bf16[384,1536]{1,0:T(8,128)(2,1)} %get-tuple-element.529), channel_id=1, source_target_pairs={{0,2},{1,3},{2,0},{3,1},{4,6},{5,7},{6,4},{7,5},{8,10},{9,11},{10,... | collective-permute-start | bytes 3538952 | tf_op jit(solution)/shard_map/ppermute | solution.py:55
  434.8 39.7 %collective-permute-start.70 = (bf16[384,1536]{1,0:T(8,128)(2,1)S(1)}, bf16[384,1536]{1,0:T(8,128)(2,1)S(1)}, u32[]{:S(2)}, u32[]{:S(2)}) collective-permute-start(bf16[384,1536]{1,0:T(8,128)(2,1)S(1)} %get-tuple-element.578), channel_id=1, source_target_pairs={{0,2},{1,3},{2,0},{3,1},{4,6},{5,7},{6,4},{7,5},{8,10},{9,11},{10,... | collective-permute-start | bytes 3538952 | tf_op jit(solution)/shard_map/ppermute | solution.py:55
  435.9 38.6 %collective-permute-start.71 = (bf16[384,1536]{1,0:T(8,128)(2,1)S(1)}, bf16[384,1536]{1,0:T(8,128)(2,1)S(1)}, u32[]{:S(2)}, u32[]{:S(2)}) collective-permute-start(bf16[384,1536]{1,0:T(8,128)(2,1)S(1)} %get-tuple-element.580), channel_id=1, source_target_pairs={{0,4},{1,5},{2,6},{3,7},{4,0},{5,1},{6,2},{7,3},{8,12},{9,13},{10,... | collective-permute-start | bytes 3538952 | tf_op jit(solution)/shard_map/ppermute | solution.py:55
  437.7 36.8 %collective-permute-start.72 = (bf16[64,3072]{1,0:T(8,128)(2,1)S(1)}, bf16[64,3072]{1,0:T(8,128)(2,1)S(1)}, u32[]{:S(2)}, u32[]{:S(2)}) collective-permute-start(bf16[64,3072]{1,0:T(8,128)(2,1)S(1)} %get-tuple-element.583), channel_id=1, source_target_pairs={{0,8},{1,9},{2,10},{3,11},{4,12},{5,13},{6,14},{7,15},{8,0},{9,1},... | collective-permute-start | bytes 1179656 | tf_op jit(solution)/shard_map/ppermute | solution.py:55
  485.6 28.8 %collective-permute-start.78 = (bf16[384,1536]{1,0:T(8,128)(2,1)S(1)}, bf16[384,1536]{1,0:T(8,128)(2,1)S(1)}, u32[]{:S(2)}, u32[]{:S(2)}) collective-permute-start(bf16[384,1536]{1,0:T(8,128)(2,1)S(1)} %get-tuple-element.606), channel_id=1, source_target_pairs={{0,4},{1,5},{2,6},{3,7},{4,0},{5,1},{6,2},{7,3},{8,12},{9,13},{10,... | collective-permute-start | bytes 3538952 | tf_op jit(solution)/shard_map/ppermute | solution.py:55
  571.9 32.1 %collective-permute-start.87 = (bf16[384,1536]{1,0:T(8,128)(2,1)S(1)}, bf16[384,1536]{1,0:T(8,128)(2,1)S(1)}, u32[]{:S(2)}, u32[]{:S(2)}) collective-permute-start(bf16[384,1536]{1,0:T(8,128)(2,1)S(1)} %get-tuple-element.640), channel_id=1, source_target_pairs={{0,2},{1,3},{2,0},{3,1},{4,6},{5,7},{6,4},{7,5},{8,10},{9,11},{10,... | collective-permute-start | bytes 3538952 | tf_op jit(solution)/shard_map/ppermute | solution.py:55
  573.0 31.0 %collective-permute-start.88 = (bf16[384,1536]{1,0:T(8,128)(2,1)S(1)}, bf16[384,1536]{1,0:T(8,128)(2,1)S(1)}, u32[]{:S(2)}, u32[]{:S(2)}) collective-permute-start(bf16[384,1536]{1,0:T(8,128)(2,1)S(1)} %get-tuple-element.642), channel_id=1, source_target_pairs={{0,4},{1,5},{2,6},{3,7},{4,0},{5,1},{6,2},{7,3},{8,12},{9,13},{10,... | collective-permute-start | bytes 3538952 | tf_op jit(solution)/shard_map/ppermute | solution.py:55
  (263 other events, 3375.2 us)

commit v7 on v6

--- a/solution.py
+++ b/solution.py
@@ -1006,10 +1006,11 @@
         for place in owns.get(phase, ()):
             items[place].own()
 
-    flow.keep(gains)
     while phase < first_use or tok_route.levels:
         transfers()
         tok_route.step()
+        if phase == 2:
+            flow.keep(gains)
         if phase == 0:
             cot_route.step()
             flow.keep(*(item.shard for item in items[1:]))

time: 665 us -> 669 us (level)
    unnamed x363 -> x407, local copies, waits for them, and re-layouts: 68.7 us -> 71.8 us
  transfers between devices with their start and end apart: 110 -> 110, of which waited for: 46 -> 48; matrix products, arithmetic and copies ran while one was open for 6% -> 6% of each run, Pallas kernels for 23% -> 22%
where the time goes in v7:
time: 669 us; the launch traced here: 661 us
  waiting for transfers between devices  262 us (39%)
  Pallas kernels  157 us (23%)
  starting transfers between devices  123 us (18%)
  local copies, waits for them, and re-layouts  82.1 us (12%)
  other arithmetic  21 us (3%)
  between operations  8.22 us (1%)
    ppermute x110, waiting for transfers between devices, route(): result = lax.ppermute(self.tie(value), axes, pairs)  262 us
    pallas_call x40, Pallas kernels, run(): pl.pallas_call(kernel, in_specs=specs, out_specs=results, **params)(*args)  157 us
    ppermute x110, starting transfers between devices, route(): result = lax.ppermute(self.tie(value), axes, pairs)  123 us
    unnamed x407, local copies, waits for them, and re-layouts  71.8 us
  transfers between devices with their start and end apart: 110, of which 48 were waited for; matrix products, arithmetic and copies ran while one was open for 6% of the time, Pallas kernels for 22%

profile of v7, /device:TPU:0, one launch (start us, length us, event | category | flops | bytes accessed | tf_op | source)
XLA Modules:
  0.0 660.5 jit_solution(14192888066679453509)
XLA Ops:
  44.0 9.6 %collective-permute-done.4 = bf16[256,1024]{1,0:T(8,128)(2,1)S(1)} collective-permute-done((bf16[256,1024]{1,0:T(8,128)(2,1)S(1)}, bf16[256,1024]{1,0:T(8,128)(2,1)S(1)}, u32[]{:S(2)}, u32[]{:S(2)}) %collective-permute-start.4) | collective-permute-done | bytes 524320 | tf_op jit(solution)/shard_map/ppermute | solution.py:55
  74.0 22.5 %collective-permute-done.9 = bf16[256,1024]{1,0:T(8,128)(2,1)S(1)} collective-permute-done((bf16[256,1024]{1,0:T(8,128)(2,1)S(1)}, bf16[256,1024]{1,0:T(8,128)(2,1)S(1)}, u32[]{:S(2)}, u32[]{:S(2)}) %collective-permute-start.9) | collective-permute-done | bytes 524320 | tf_op jit(solution)/shard_map/ppermute | solution.py:55
  101.7 6.2 shard_map.165
  113.8 14.4 %collective-permute-done.17.before = bf16[64,2048]{1,0:T(8,128)(2,1)S(1)} collective-permute-done((bf16[64,2048]{1,0:T(8,128)(2,1)S(1)}, bf16[64,2048]{1,0:T(8,128)(2,1)S(1)}, u32[]{:S(2)}, u32[]{:S(2)}) %collective-permute-start.17) | collective-permute-done | bytes 262176 | tf_op jit(solution)/shard_map/ppermute | solution.py:55
  142.5 10.2 %shard_map.166 = (bf16[256,1024]{1,0:T(8,128)(2,1)S(1)}, f32[256,1024]{1,0:T(8,128)S(1)}, bf16[256,1024]{1,0:T(8,128)(2,1)S(1)}) custom-call(s32[8]{0:T(128)S(1)} %stack.71.offs, bf16[256,3072]{1,0:T(8,128)(2,1)S(1)} %copy-done.28, bf16[64,2048]{1,0:T(8,128)(2,1)S(1)} %copy-done.67, bf16[64,2048]{1,0:T(8,128)(2,1)S(1)} %copy-done.70, ...), custom_call_target="tpu_custom_call" | custom-call | tf_op jit(solution)/shard_map/pallas_call | solution.py:148
  199.9 6.2 collective-permute-done.33
  220.9 18.8 %collective-permute-done.37.before = bf16[64,2048]{1,0:T(8,128)(2,1)S(1)} collective-permute-done((bf16[64,2048]{1,0:T(8,128)(2,1)S(1)}, bf16[64,2048]{1,0:T(8,128)(2,1)S(1)}, u32[]{:S(2)}, u32[]{:S(2)}) %collective-permute-start.37) | collective-permute-done | bytes 262176 | tf_op jit(solution)/shard_map/ppermute | solution.py:55
  243.1 9.3 %shard_map.172 = (bf16[256,1024]{1,0:T(8,128)(2,1)S(1)}, f32[256,1024]{1,0:T(8,128)S(1)}, bf16[256,1024]{1,0:T(8,128)(2,1)S(1)}) custom-call(s32[8]{0:T(128)S(1)} %stack.71.offs, bf16[256,3072]{1,0:T(8,128)(2,1)S(1)} %get-tuple-element.446.qkv, bf16[64,2048]{1,0:T(8,128)(2,1)S(1)} %collective-permute-done.37.before, ...), custom_call_target="tpu_custom_call" | custom-call | tf_op jit(solution)/shard_map/pallas_call | solution.py:148
  254.6 6.5 collective-permute-done.39
  281.0 7.8 %collective-permute-done.45 = bf16[128,1024]{1,0:T(8,128)(2,1)S(1)} collective-permute-done((bf16[128,1024]{1,0:T(8,128)(2,1)}, bf16[128,1024]{1,0:T(8,128)(2,1)S(1)}, u32[]{:S(2)}, u32[]{:S(2)}) %collective-permute-start.45) | collective-permute-done | bytes 262176 | tf_op jit(solution)/shard_map/ppermute | solution.py:55
  301.9 10.1 %shard_map.182 = (bf16[256,1024]{1,0:T(8,128)(2,1)S(1)}, f32[256,2048]{1,0:T(8,128)S(1)}, bf16[64,2048]{1,0:T(8,128)(2,1)S(1)}, bf16[64,2048]{1,0:T(8,128)(2,1)S(1)}) custom-call(s32[8]{0:T(128)S(1)} %stack.71.offs, bf16[256,1024]{1,0:T(8,128)(2,1)S(1)} %get-tuple-element.496.middle_grad, bf16[256,3072]{1,0:T(8,128)(2,1)S(1)} %get-tuple-element.446.qkv, ...), custom_call_target="tpu_custom_call" | custom-call | tf_op jit(solution)/shard_map/pallas_call | solution.py:148
  316.7 9.8 %collective-permute-done.51.arrived_first = bf16[64,2048]{1,0:T(8,128)(2,1)S(1)} collective-permute-done((bf16[64,2048]{1,0:T(8,128)(2,1)S(1)}, bf16[64,2048]{1,0:T(8,128)(2,1)S(1)}, u32[]{:S(2)}, u32[]{:S(2)}) %collective-permute-start.51) | collective-permute-done | bytes 262176 | tf_op jit(solution)/shard_map/ppermute | solution.py:55
  340.1 8.2 %collective-permute-done.56 = bf16[128,1024]{1,0:T(8,128)(2,1)S(1)} collective-permute-done((bf16[128,1024]{1,0:T(8,128)(2,1)S(1)}, bf16[128,1024]{1,0:T(8,128)(2,1)S(1)}, u32[]{:S(2)}, u32[]{:S(2)}) %collective-permute-start.56) | collective-permute-done | bytes 262176 | tf_op jit(solution)/shard_map/ppermute | solution.py:55
  348.2 10.9 %collective-permute-done.54.refs_16_ = bf16[384,1536]{1,0:T(8,128)(2,1)S(1)} collective-permute-done((bf16[384,1536]{1,0:T(8,128)(2,1)S(1)}, bf16[384,1536]{1,0:T(8,128)(2,1)S(1)}, u32[]{:S(2)}, u32[]{:S(2)}) %collective-permute-start.54) | collective-permute-done | bytes 1179680 | tf_op jit(solution)/shard_map/ppermute | solution.py:55
  415.8 6.3 collective-permute-done.67.refs_19_
  422.1 12.1 %collective-permute-done.64.refs_14_ = bf16[384,1536]{1,0:T(8,128)(2,1)S(1)} collective-permute-done((bf16[384,1536]{1,0:T(8,128)(2,1)S(1)}, bf16[384,1536]{1,0:T(8,128)(2,1)S(1)}, u32[]{:S(2)}, u32[]{:S(2)}) %collective-permute-start.64) | collective-permute-done | bytes 1179680 | tf_op jit(solution)/shard_map/ppermute | solution.py:55
  448.4 11.1 %shard_map.191 = (bf16[256,1024]{1,0:T(8,128)(2,1)S(1)}, f32[256,2048]{1,0:T(8,128)S(1)}, bf16[64,2048]{1,0:T(8,128)(2,1)S(1)}, bf16[64,2048]{1,0:T(8,128)(2,1)S(1)}) custom-call(s32[8]{0:T(128)S(1)} %stack.71.offs, bf16[256,1024]{1,0:T(8,128)(2,1)S(1)} %get-tuple-element.565.middle_grad, bf16[256,3072]{1,0:T(8,128)(2,1)S(1)} %copy-done.29, ...), custom_call_target="tpu_custom_call" | custom-call | tf_op jit(solution)/shard_map/pallas_call | solution.py:148
  464.5 14.4 %collective-permute-done.74.arrived_first = bf16[64,2048]{1,0:T(8,128)(2,1)S(1)} collective-permute-done((bf16[64,2048]{1,0:T(8,128)(2,1)S(1)}, bf16[64,2048]{1,0:T(8,128)(2,1)S(1)}, u32[]{:S(2)}, u32[]{:S(2)}) %collective-permute-start.74) | collective-permute-done | bytes 262176 | tf_op jit(solution)/shard_map/ppermute | solution.py:55
  495.8 6.8 %shard_map.193 = (bf16[256,3072]{1,0:T(8,128)(2,1)}, f32[256,1024]{1,0:T(8,128)}, bf16[256,1024]{1,0:T(8,128)(2,1)S(1)}, f32[1,1024]{1,0:T(1,128)S(1)}) custom-call(s32[8]{0:T(128)S(1)} %stack.71.offs, bf16[256,1024]{1,0:T(8,128)(2,1)S(1)} %get-tuple-element.592.query_grad, f32[256,2048]{1,0:T(8,128)S(1)} %get-tuple-element.586.own_grad, ...), custom_call_target="tpu_custom_call" | custom-call | tf_op jit(solution)/shard_map/pallas_call | solution.py:148
  507.2 10.1 %collective-permute-done.77.refs_16_ = bf16[384,1536]{1,0:T(8,128)(2,1)S(1)} collective-permute-done((bf16[384,1536]{1,0:T(8,128)(2,1)S(1)}, bf16[384,1536]{1,0:T(8,128)(2,1)S(1)}, u32[]{:S(2)}, u32[]{:S(2)}) %collective-permute-start.77) | collective-permute-done | bytes 1179680 | tf_op jit(solution)/shard_map/ppermute | solution.py:55
  548.2 13.6 %collective-permute-done.85.refs_17_ = bf16[32,3072]{1,0:T(8,128)(2,1)S(1)} collective-permute-done((bf16[32,3072]{1,0:T(8,128)(2,1)S(1)}, bf16[32,3072]{1,0:T(8,128)(2,1)S(1)}, u32[]{:S(2)}, u32[]{:S(2)}) %collective-permute-start.85) | collective-permute-done | bytes 196640 | tf_op jit(solution)/shard_map/ppermute | solution.py:55
  584.9 10.1 %collective-permute-done.90.refs_9_ = bf16[32,3072]{1,0:T(8,128)(2,1)S(1)} collective-permute-done((bf16[32,3072]{1,0:T(8,128)(2,1)S(1)}, bf16[32,3072]{1,0:T(8,128)(2,1)S(1)}, u32[]{:S(2)}, u32[]{:S(2)}) %collective-permute-start.90) | collective-permute-done | bytes 196640 | tf_op jit(solution)/shard_map/ppermute | solution.py:55
  598.4 6.9 %collective-permute-done.91 = bf16[128,1024]{1,0:T(8,128)(2,1)S(1)} collective-permute-done((bf16[128,1024]{1,0:T(8,128)(2,1)S(1)}, bf16[128,1024]{1,0:T(8,128)(2,1)S(1)}, u32[]{:S(2)}, u32[]{:S(2)}) %collective-permute-start.91) | collective-permute-done | bytes 262176 | tf_op jit(solution)/shard_map/ppermute | solution.py:55
  624.4 9.4 %collective-permute-done.100 = bf16[128,1024]{1,0:T(8,128)(2,1)S(1)} collective-permute-done((bf16[128,1024]{1,0:T(8,128)(2,1)S(1)}, bf16[128,1024]{1,0:T(8,128)(2,1)S(1)}, u32[]{:S(2)}, u32[]{:S(2)}) %collective-permute-start.100) | collective-permute-done | bytes 262176 | tf_op jit(solution)/shard_map/ppermute | solution.py:55
  (746 shorter events, 401.2 us)
Async XLA Ops:
  3.8 28.6 %collective-permute-start.2 = (bf16[256,3072]{1,0:T(8,128)(2,1)}, bf16[256,3072]{1,0:T(8,128)(2,1)}, u32[]{:S(2)}, u32[]{:S(2)}) collective-permute-start(bf16[256,3072]{1,0:T(8,128)(2,1)} %get-tuple-element.361.p0), channel_id=1, source_target_pairs={{0,1},{1,0},{2,3},{3,2},{4,5},{5,4},{6,7},{7,6},{8,9},{9,8},{10,11... | collective-permute-start | bytes 4718600 | tf_op jit(solution)/shard_map/ppermute | solution.py:55
  57.9 38.6 %collective-permute-start.12 = (bf16[256,3072]{1,0:T(8,128)(2,1)}, bf16[256,3072]{1,0:T(8,128)(2,1)}, u32[]{:S(2)}, u32[]{:S(2)}) collective-permute-start(bf16[256,3072]{1,0:T(8,128)(2,1)} %constant_dynamic-update-slice_fusion.p1), channel_id=1, source_target_pairs={{0,1},{1,0},{2,3},{3,2},{4,5},{5,4},{6,7},{7,6},{8,9},{9,8},{10,11... | collective-permute-start | bytes 4718600 | tf_op jit(solution)/shard_map/ppermute | solution.py:55
  57.9 38.6 %collective-permute-start.13 = (bf16[256,3072]{1,0:T(8,128)(2,1)}, bf16[256,3072]{1,0:T(8,128)(2,1)}, u32[]{:S(2)}, u32[]{:S(2)}) collective-permute-start(bf16[256,3072]{1,0:T(8,128)(2,1)} %get-tuple-element.383.p0), channel_id=1, source_target_pairs={{0,1},{1,0},{2,3},{3,2},{4,5},{5,4},{6,7},{7,6},{8,9},{9,8},{10,11... | collective-permute-start | bytes 4718600 | tf_op jit(solution)/shard_map/ppermute | solution.py:55
  66.4 30.1 %collective-permute-start.10 = (bf16[128,3072]{1,0:T(8,128)(2,1)}, bf16[128,3072]{1,0:T(8,128)(2,1)S(1)}, u32[]{:S(2)}, u32[]{:S(2)}) collective-permute-start(bf16[128,3072]{1,0:T(8,128)(2,1)} %copy-done.139), channel_id=1, source_target_pairs={{0,2},{1,3},{2,0},{3,1},{4,6},{5,7},{6,4},{7,5},{8,10},{9,11},{10,... | collective-permute-start | bytes 2359304 | tf_op jit(solution)/shard_map/ppermute | solution.py:55
  96.6 31.6 %collective-permute-start.16 = (bf16[256,2944]{1,0:T(8,128)(2,1)S(1)}, bf16[256,2944]{1,0:T(8,128)(2,1)}, u32[]{:S(2)}, u32[]{:S(2)}) collective-permute-start(bf16[256,2944]{1,0:T(8,128)(2,1)S(1)} %constant_dynamic-update-slice_fusion.2.p1), channel_id=1, source_target_pairs={{0,1},{1,0},{2,3},{3,2},{4,5},{5,4},{6,7},{7,6},{8,9},{9,8},{10,11... | collective-permute-start | bytes 4521992 | tf_op jit(solution)/shard_map/ppermute | solution.py:55
  99.4 28.8 %collective-permute-start.14 = (bf16[128,3072]{1,0:T(8,128)(2,1)}, bf16[128,3072]{1,0:T(8,128)(2,1)S(1)}, u32[]{:S(2)}, u32[]{:S(2)}) collective-permute-start(bf16[128,3072]{1,0:T(8,128)(2,1)} %copy-done.138), channel_id=1, source_target_pairs={{0,2},{1,3},{2,0},{3,1},{4,6},{5,7},{6,4},{7,5},{8,10},{9,11},{10,... | collective-permute-start | bytes 2359304 | tf_op jit(solution)/shard_map/ppermute | solution.py:55
  129.3 31.0 %collective-permute-start.21 = (bf16[256,3072]{1,0:T(8,128)(2,1)}, bf16[256,3072]{1,0:T(8,128)(2,1)}, u32[]{:S(2)}, u32[]{:S(2)}) collective-permute-start(bf16[256,3072]{1,0:T(8,128)(2,1)} %constant_dynamic-update-slice_fusion.4.p1), channel_id=1, source_target_pairs={{0,1},{1,0},{2,3},{3,2},{4,5},{5,4},{6,7},{7,6},{8,9},{9,8},{10,11... | collective-permute-start | bytes 4718600 | tf_op jit(solution)/shard_map/ppermute | solution.py:55
  129.3 31.0 %collective-permute-start.22 = (bf16[256,3072]{1,0:T(8,128)(2,1)}, bf16[256,3072]{1,0:T(8,128)(2,1)}, u32[]{:S(2)}, u32[]{:S(2)}) collective-permute-start(bf16[256,3072]{1,0:T(8,128)(2,1)} %get-tuple-element.407.p0), channel_id=1, source_target_pairs={{0,1},{1,0},{2,3},{3,2},{4,5},{5,4},{6,7},{7,6},{8,9},{9,8},{10,11... | collective-permute-start | bytes 4718600 | tf_op jit(solution)/shard_map/ppermute | solution.py:55
  208.7 31.0 %collective-permute-start.36 = (bf16[256,2944]{1,0:T(8,128)(2,1)S(1)}, bf16[256,2944]{1,0:T(8,128)(2,1)S(1)}, u32[]{:S(2)}, u32[]{:S(2)}) collective-permute-start(bf16[256,2944]{1,0:T(8,128)(2,1)S(1)} %constant_dynamic-update-slice_fusion.10.p1), channel_id=1, source_target_pairs={{0,1},{1,0},{2,3},{3,2},{4,5},{5,4},{6,7},{7,6},{8,9},{9,8},{10,11... | collective-permute-start | bytes 4521992 | tf_op jit(solution)/shard_map/ppermute | solution.py:55
  208.8 30.9 %collective-permute-start.34 = (bf16[128,3072]{1,0:T(8,128)(2,1)S(1)}, bf16[128,3072]{1,0:T(8,128)(2,1)S(1)}, u32[]{:S(2)}, u32[]{:S(2)}) collective-permute-start(bf16[128,3072]{1,0:T(8,128)(2,1)S(1)} %copy-done.134), channel_id=1, source_target_pairs={{0,2},{1,3},{2,0},{3,1},{4,6},{5,7},{6,4},{7,5},{8,10},{9,11},{10,... | collective-permute-start | bytes 2359304 | tf_op jit(solution)/shard_map/ppermute | solution.py:55
  209.8 29.9 %collective-permute-start.35 = (bf16[128,3072]{1,0:T(8,128)(2,1)S(1)}, bf16[128,3072]{1,0:T(8,128)(2,1)S(1)}, u32[]{:S(2)}, u32[]{:S(2)}) collective-permute-start(bf16[128,3072]{1,0:T(8,128)(2,1)S(1)} %collective-permute-done.29), channel_id=1, source_target_pairs={{0,4},{1,5},{2,6},{3,7},{4,0},{5,1},{6,2},{7,3},{8,12},{9,13},{10,... | collective-permute-start | bytes 2359304 | tf_op jit(solution)/shard_map/ppermute | solution.py:55
  293.6 32.9 %collective-permute-start.48 = (bf16[256,3072]{1,0:T(8,128)(2,1)S(1)}, bf16[256,3072]{1,0:T(8,128)(2,1)S(1)}, u32[]{:S(2)}, u32[]{:S(2)}) collective-permute-start(bf16[256,3072]{1,0:T(8,128)(2,1)S(1)} %get-tuple-element.504.refs_0_.refs_1_), channel_id=1, source_target_pairs={{0,1},{1,0},{2,3},{3,2},{4,5},{5,4},{6,7},{7,6},{8,9},{9,8},{10,11... | collective-permute-start | bytes 4718600 | tf_op jit(solution)/shard_map/ppermute | solution.py:55
  296.5 30.0 %collective-permute-start.49 = (bf16[256,1536]{1,0:T(8,128)(2,1)S(1)}, bf16[256,1536]{1,0:T(8,128)(2,1)S(1)}, u32[]{:S(2)}, u32[]{:S(2)}) collective-permute-start(bf16[256,1536]{1,0:T(8,128)(2,1)S(1)} %get-tuple-element.493), channel_id=1, source_target_pairs={{0,2},{1,3},{2,0},{3,1},{4,6},{5,7},{6,4},{7,5},{8,10},{9,11},{10,... | collective-permute-start | bytes 2359304 | tf_op jit(solution)/shard_map/ppermute | solution.py:55
  297.7 28.8 %collective-permute-start.50 = (bf16[256,1536]{1,0:T(8,128)(2,1)S(1)}, bf16[256,1536]{1,0:T(8,128)(2,1)S(1)}, u32[]{:S(2)}, u32[]{:S(2)}) collective-permute-start(bf16[256,1536]{1,0:T(8,128)(2,1)S(1)} %get-tuple-element.495), channel_id=1, source_target_pairs={{0,4},{1,5},{2,6},{3,7},{4,0},{5,1},{6,2},{7,3},{8,12},{9,13},{10,... | collective-permute-start | bytes 2359304 | tf_op jit(solution)/shard_map/ppermute | solution.py:55
  326.5 34.0 %collective-permute-start.53 = (bf16[256,3072]{1,0:T(8,128)(2,1)S(1)}, bf16[256,3072]{1,0:T(8,128)(2,1)S(1)}, u32[]{:S(2)}, u32[]{:S(2)}) collective-permute-start(bf16[256,3072]{1,0:T(8,128)(2,1)S(1)} %get-tuple-element.523.refs_0_.refs_1_), channel_id=1, source_target_pairs={{0,1},{1,0},{2,3},{3,2},{4,5},{5,4},{6,7},{7,6},{8,9},{9,8},{10,11... | collective-permute-start | bytes 4718600 | tf_op jit(solution)/shard_map/ppermute | solution.py:55
  331.7 28.8 %collective-permute-start.55 = (bf16[384,1536]{1,0:T(8,128)(2,1)S(1)}, bf16[384,1536]{1,0:T(8,128)(2,1)S(1)}, u32[]{:S(2)}, u32[]{:S(2)}) collective-permute-start(bf16[384,1536]{1,0:T(8,128)(2,1)S(1)} %get-tuple-element.510), channel_id=1, source_target_pairs={{0,4},{1,5},{2,6},{3,7},{4,0},{5,1},{6,2},{7,3},{8,12},{9,13},{10,... | collective-permute-start | bytes 3538952 | tf_op jit(solution)/shard_map/ppermute | solution.py:55
  370.5 28.6 %collective-permute-start.59 = (bf16[384,1536]{1,0:T(8,128)(2,1)}, bf16[384,1536]{1,0:T(8,128)(2,1)}, u32[]{:S(2)}, u32[]{:S(2)}) collective-permute-start(bf16[384,1536]{1,0:T(8,128)(2,1)} %get-tuple-element.529), channel_id=1, source_target_pairs={{0,2},{1,3},{2,0},{3,1},{4,6},{5,7},{6,4},{7,5},{8,10},{9,11},{10,... | collective-permute-start | bytes 3538952 | tf_op jit(solution)/shard_map/ppermute | solution.py:55
  439.2 39.7 %collective-permute-start.70 = (bf16[384,1536]{1,0:T(8,128)(2,1)S(1)}, bf16[384,1536]{1,0:T(8,128)(2,1)S(1)}, u32[]{:S(2)}, u32[]{:S(2)}) collective-permute-start(bf16[384,1536]{1,0:T(8,128)(2,1)S(1)} %get-tuple-element.578), channel_id=1, source_target_pairs={{0,2},{1,3},{2,0},{3,1},{4,6},{5,7},{6,4},{7,5},{8,10},{9,11},{10,... | collective-permute-start | bytes 3538952 | tf_op jit(solution)/shard_map/ppermute | solution.py:55
  440.3 38.6 %collective-permute-start.71 = (bf16[384,1536]{1,0:T(8,128)(2,1)S(1)}, bf16[384,1536]{1,0:T(8,128)(2,1)S(1)}, u32[]{:S(2)}, u32[]{:S(2)}) collective-permute-start(bf16[384,1536]{1,0:T(8,128)(2,1)S(1)} %get-tuple-element.580), channel_id=1, source_target_pairs={{0,4},{1,5},{2,6},{3,7},{4,0},{5,1},{6,2},{7,3},{8,12},{9,13},{10,... | collective-permute-start | bytes 3538952 | tf_op jit(solution)/shard_map/ppermute | solution.py:55
  442.1 36.8 %collective-permute-start.72 = (bf16[64,3072]{1,0:T(8,128)(2,1)S(1)}, bf16[64,3072]{1,0:T(8,128)(2,1)S(1)}, u32[]{:S(2)}, u32[]{:S(2)}) collective-permute-start(bf16[64,3072]{1,0:T(8,128)(2,1)S(1)} %get-tuple-element.583), channel_id=1, source_target_pairs={{0,8},{1,9},{2,10},{3,11},{4,12},{5,13},{6,14},{7,15},{8,0},{9,1},... | collective-permute-start | bytes 1179656 | tf_op jit(solution)/shard_map/ppermute | solution.py:55
  490.0 28.8 %collective-permute-start.78 = (bf16[384,1536]{1,0:T(8,128)(2,1)S(1)}, bf16[384,1536]{1,0:T(8,128)(2,1)S(1)}, u32[]{:S(2)}, u32[]{:S(2)}) collective-permute-start(bf16[384,1536]{1,0:T(8,128)(2,1)S(1)} %get-tuple-element.606), channel_id=1, source_target_pairs={{0,4},{1,5},{2,6},{3,7},{4,0},{5,1},{6,2},{7,3},{8,12},{9,13},{10,... | collective-permute-start | bytes 3538952 | tf_op jit(solution)/shard_map/ppermute | solution.py:55
  541.6 28.4 %collective-permute-start.82 = (bf16[384,1536]{1,0:T(8,128)(2,1)S(1)}, bf16[384,1536]{1,0:T(8,128)(2,1)S(1)}, u32[]{:S(2)}, u32[]{:S(2)}) collective-permute-start(bf16[384,1536]{1,0:T(8,128)(2,1)S(1)} %get-tuple-element.622), channel_id=1, source_target_pairs={{0,2},{1,3},{2,0},{3,1},{4,6},{5,7},{6,4},{7,5},{8,10},{9,11},{10,... | collective-permute-start | bytes 3538952 | tf_op jit(solution)/shard_map/ppermute | solution.py:55
  576.2 32.1 %collective-permute-start.87 = (bf16[384,1536]{1,0:T(8,128)(2,1)S(1)}, bf16[384,1536]{1,0:T(8,128)(2,1)S(1)}, u32[]{:S(2)}, u32[]{:S(2)}) collective-permute-start(bf16[384,1536]{1,0:T(8,128)(2,1)S(1)} %get-tuple-element.640), channel_id=1, source_target_pairs={{0,2},{1,3},{2,0},{3,1},{4,6},{5,7},{6,4},{7,5},{8,10},{9,11},{10,... | collective-permute-start | bytes 3538952 | tf_op jit(solution)/shard_map/ppermute | solution.py:55
  577.4 30.9 %collective-permute-start.88 = (bf16[384,1536]{1,0:T(8,128)(2,1)S(1)}, bf16[384,1536]{1,0:T(8,128)(2,1)S(1)}, u32[]{:S(2)}, u32[]{:S(2)}) collective-permute-start(bf16[384,1536]{1,0:T(8,128)(2,1)S(1)} %get-tuple-element.642), channel_id=1, source_target_pairs={{0,4},{1,5},{2,6},{3,7},{4,0},{5,1},{6,2},{7,3},{8,12},{9,13},{10,... | collective-permute-start | bytes 3538952 | tf_op jit(solution)/shard_map/ppermute | solution.py:55
  (285 other events, 3581.2 us)
